TPU v7x, 32 devices: a whole 2x2x4 slice. The times are simulated.
32 devices in a mesh: expert: 4 (over y, core), fsdp: 8 (over z, x).
Axes of the slice: x: 2, y: 2, z: 4, core: 2. Of those that a mesh axis runs over, the one named last changes fastest.
Arguments:
- tokens: bfloat16 [8192, 1536], P(('expert', 'fsdp')), may hold values from -6 to 6
- routes: int32 [8192, 4], P(('expert', 'fsdp')), may hold values from 0 to 31, all different within a row; in each aligned block of 256 rows (0 to 255, 256 to 511, ...) at most 48 rows name the same one
- norm_attn: float32 [1536], replicated, may hold values from 0.1 to 1.9
- qkv_weight: bfloat16 [1536, 2048], P('fsdp'), may hold values from -0.15625 to 0.15625
- out_weight: bfloat16 [1536, 1536], P('fsdp'), may hold values from -0.625 to 0.625
- norm_moe: float32 [1536], replicated, may hold values from 0.1 to 1.9
- router_weight: bfloat16 [1536, 32], replicated, may hold values from -0.078125 to 0.078125
- gate_up: bfloat16 [32, 1536, 1536], P('expert', 'fsdp'), may hold values from -0.15625 to 0.15625
- down: bfloat16 [32, 768, 1536], P('expert', 'fsdp'), may hold values from -0.625 to 0.625
- grad_output: bfloat16 [8192, 1536], P(('expert', 'fsdp')), may hold values from -6 to 6
Outputs:
- mixed: bfloat16 [8192, 1536], P(('expert', 'fsdp'))
- grad_tokens: float32 [8192, 1536], P(('expert', 'fsdp'))
- grad_norm_attn: float32 [1536], replicated
- grad_qkv: float32 [1536, 2048], P('fsdp')
- grad_out_proj: float32 [1536, 1536], P('fsdp')
- grad_norm_moe: float32 [1536], replicated
- grad_router: float32 [1536, 32], replicated
- grad_gate_up: float32 [32, 1536, 1536], P('expert', 'fsdp')
- grad_down: float32 [32, 768, 1536], P('expert', 'fsdp')
Inputs may be any that keep to these rules, and one draw needn't show every extreme that they name: `routes`: each row names 4 different experts; in the 256 rows of one device no expert is named by more than 48 rows, and in every draw some device has an expert named by exactly 48 of its rows.
All inputs are finite; a program needn't handle non-finite values.
Results may differ from a plain program's by a relative error of at most 0.023.
Values may be sent and summed in bfloat16 or wider, within the bound.
No kernel may reach another device: no remote copies, remote signals or barrier semaphores. Data moves between devices by JAX's collectives and lax.ppermute only.
A program may use at most 320 MiB of HBM per device.

v0:
```python
import jax
import jax.numpy as jnp
from jax import lax
from jax.sharding import PartitionSpec as P

HEADS = 12
KV_HEADS = 2
HEAD_DIM = 128
FFE = 768
EXPERTS = 32
TOP = 4
CAP = 48


EPSILON = 1e-06


def rms_apply(values, gain):
    return values * lax.rsqrt(jnp.mean(values * values, axis=-1, keepdims=True) + EPSILON) * gain


def reglu_smooth(projected):
    return jax.nn.gelu(projected[..., :FFE]) * projected[..., FFE:]


def block_scores(query_block, keys, start, block_rows, seq_len):
    scores = jnp.einsum(
        "qhgd,khd->hgqk", query_block, keys, preferred_element_type=jnp.float32
    ) * HEAD_DIM ** (-0.5)
    causal = (start + jnp.arange(block_rows))[:, None] >= jnp.arange(seq_len)[None, :]
    return (scores, causal)


def attend_forward(queries, keys, values):
    seq_len = queries.shape[0]
    block_rows = min(512, seq_len)

    def one_block(block_index):
        start = block_index * block_rows
        scores, causal = block_scores(queries, keys, start, block_rows, seq_len)
        scores = jnp.where(causal, scores, -1e30)
        row_max = jnp.max(scores, axis=-1, keepdims=True)
        exponent = jnp.exp(scores - row_max)
        row_total = jnp.sum(exponent, axis=-1, keepdims=True)
        attn_probs = (exponent / row_total).astype(jnp.bfloat16)
        attended = jnp.einsum(
            "hgqk,khd->qhgd", attn_probs, values, preferred_element_type=jnp.float32
        )
        return (attended.astype(jnp.bfloat16), (row_max + jnp.log(row_total))[..., 0])

    attended, log_total = lax.map(one_block, jnp.arange(seq_len // block_rows))
    return (attended.reshape(seq_len, -1), log_total)


def attend_backward(queries, keys, values, grad_heads, log_total):
    seq_len = queries.shape[0]
    block_rows = min(512, seq_len)
    score_scale = HEAD_DIM ** (-0.5)

    def one_block(carry, block_index):
        grad_keys, grad_values = carry
        start = block_index * block_rows
        scores, causal = block_scores(queries, keys, start, block_rows, seq_len)
        attn_full = jnp.where(causal, jnp.exp(scores - log_total[block_index][..., None]), 0.0)
        attn_probs = attn_full.astype(jnp.bfloat16)
        grad_probs = jnp.einsum(
            "qhgd,khd->hgqk", grad_heads, values, preferred_element_type=jnp.float32
        )
        delta = jnp.sum(attn_full * grad_probs, axis=-1, keepdims=True)
        grad_scores = (attn_full * (grad_probs - delta)).astype(jnp.bfloat16)
        grad_query = (
            jnp.einsum("hgqk,khd->qhgd", grad_scores, keys, preferred_element_type=jnp.float32)
            * score_scale
        )
        grad_keys = (
            grad_keys
            + jnp.einsum("hgqk,qhgd->khd", grad_scores, queries, preferred_element_type=jnp.float32)
            * score_scale
        )
        grad_values = grad_values + jnp.einsum(
            "hgqk,qhgd->khd", attn_probs, grad_heads, preferred_element_type=jnp.float32
        )
        return ((grad_keys, grad_values), grad_query)

    empty = jnp.zeros(keys.shape, jnp.float32)
    (grad_keys, grad_values), grad_query = lax.scan(
        one_block, (empty, empty), jnp.arange(seq_len // block_rows)
    )
    return (
        grad_query.reshape(seq_len, -1),
        grad_keys.reshape(seq_len, -1),
        grad_values.reshape(seq_len, -1),
    )


def shards(
    tokens,
    routes,
    norm_attn,
    qkv_weight,
    out_weight,
    norm_moe,
    router_weight,
    gate_up,
    down,
    grad_output,
):
    seq_len = tokens.shape[0]
    model_width = tokens.shape[1]
    query_width = HEADS * HEAD_DIM
    kv_width = KV_HEADS * HEAD_DIM
    group_size = HEADS // KV_HEADS
    owner_count = lax.axis_size("expert")
    local_count = gate_up.shape[0]
    recv_rows = owner_count * CAP
    token_f = tokens.astype(jnp.float32)
    qkv_full, out_full = (
        lax.all_gather(qkv_weight, "fsdp", axis=0, tiled=True),
        lax.all_gather(out_weight, "fsdp", axis=0, tiled=True),
    )
    xn_first_f, norm_first_pull = jax.vjp(rms_apply, token_f, norm_attn)
    xn_first = xn_first_f.astype(jnp.bfloat16)
    joint = jnp.dot(xn_first, qkv_full, preferred_element_type=jnp.float32).astype(jnp.bfloat16)
    queries = joint[:, :query_width].reshape(seq_len, KV_HEADS, group_size, HEAD_DIM)
    keys = joint[:, query_width : query_width + kv_width].reshape(seq_len, KV_HEADS, HEAD_DIM)
    values = joint[:, query_width + kv_width :].reshape(seq_len, KV_HEADS, HEAD_DIM)
    attended, log_total = attend_forward(queries, keys, values)
    hidden = token_f + jnp.dot(attended, out_full, preferred_element_type=jnp.float32)
    xn_second_f, norm_second_pull = jax.vjp(rms_apply, hidden, norm_moe)
    xn_second = xn_second_f.astype(jnp.bfloat16)
    logits = jnp.dot(xn_second, router_weight, preferred_element_type=jnp.float32)
    chosen_mask = routes[:, :, None] == jnp.arange(EXPERTS, dtype=jnp.int32)[None, None, :]
    chosen = jnp.sum(jnp.where(chosen_mask, logits[:, None, :], 0.0), axis=-1)
    gate_probs = jax.nn.softmax(chosen, axis=-1)
    flat_mask = chosen_mask.reshape(seq_len * TOP, EXPERTS).astype(jnp.int32)
    before = jnp.cumsum(flat_mask, axis=0) - flat_mask
    slot_index = jnp.sum(before * flat_mask, axis=-1)
    buffer_rows = routes.reshape(-1) * CAP + slot_index
    token_rows = jnp.arange(seq_len * TOP, dtype=jnp.int32) // TOP
    send_rows = (
        jnp.zeros((EXPERTS * CAP, model_width), jnp.bfloat16)
        .at[buffer_rows]
        .set(xn_second[token_rows])
    )
    received = lax.all_to_all(
        send_rows.reshape(owner_count, local_count, CAP, model_width),
        "expert",
        split_axis=0,
        concat_axis=2,
        tiled=True,
    )
    received = received.reshape(local_count, recv_rows, model_width)
    kept_weights = []
    kept_projected = []
    kept_inner = []
    expert_outputs = []
    for member in range(local_count):
        gate_up_full, down_full = (
            lax.all_gather(gate_up[member], "fsdp", axis=0, tiled=True),
            lax.all_gather(down[member], "fsdp", axis=0, tiled=True),
        )
        projected = jnp.dot(received[member], gate_up_full, preferred_element_type=jnp.float32)
        inner_act = reglu_smooth(projected).astype(jnp.bfloat16)
        expert_outputs.append(
            jnp.dot(inner_act, down_full, preferred_element_type=jnp.float32).astype(jnp.bfloat16)
        )
        kept_weights.append((gate_up_full, down_full))
        kept_projected.append(projected)
        kept_inner.append(inner_act)
    stacked_out = jnp.stack(expert_outputs).reshape(1, local_count, recv_rows, model_width)
    returned = lax.all_to_all(
        stacked_out, "expert", split_axis=2, concat_axis=0, tiled=True
    ).reshape(EXPERTS * CAP, model_width)
    picked = returned[buffer_rows].reshape(seq_len, TOP, model_width)
    moe_sum = jnp.einsum("lk,lkd->ld", gate_probs, picked.astype(jnp.float32))
    mixed = (hidden + moe_sum).astype(jnp.bfloat16)
    grad_f = grad_output.astype(jnp.float32)
    grad_gates = jnp.einsum("lkd,ld->lk", picked.astype(jnp.float32), grad_f)
    grad_chosen = gate_probs * (
        grad_gates - jnp.sum(gate_probs * grad_gates, axis=-1, keepdims=True)
    )
    grad_logits = jnp.sum(jnp.where(chosen_mask, grad_chosen[:, :, None], 0.0), axis=1).astype(
        jnp.bfloat16
    )
    router_local = jnp.dot(xn_second.T, grad_logits, preferred_element_type=jnp.float32)
    grad_xn_second = jnp.dot(grad_logits, router_weight.T, preferred_element_type=jnp.float32)
    pair_grads = (
        (gate_probs[:, :, None] * grad_f[:, None, :])
        .astype(jnp.bfloat16)
        .reshape(seq_len * TOP, model_width)
    )
    grad_send = (
        jnp.zeros((EXPERTS * CAP, model_width), jnp.bfloat16).at[buffer_rows].set(pair_grads)
    )
    grad_received = lax.all_to_all(
        grad_send.reshape(owner_count, local_count, CAP, model_width),
        "expert",
        split_axis=0,
        concat_axis=2,
        tiled=True,
    )
    grad_received = grad_received.reshape(local_count, recv_rows, model_width)
    input_grads = []
    gate_up_shards = []
    down_shards = []
    for member in range(local_count):
        gate_up_full, down_full = kept_weights[member]
        grad_inner = jnp.einsum(
            "rd,fd->rf", grad_received[member], down_full, preferred_element_type=jnp.float32
        )
        unused, reglu_pull = jax.vjp(reglu_smooth, kept_projected[member])
        grad_projected = reglu_pull(grad_inner)[0].astype(jnp.bfloat16)
        gate_up_term = jnp.einsum(
            "rd,rf->df", received[member], grad_projected, preferred_element_type=jnp.float32
        )
        down_term = jnp.einsum(
            "rf,rd->fd",
            kept_inner[member],
            grad_received[member],
            preferred_element_type=jnp.float32,
        )
        input_grads.append(
            jnp.einsum(
                "rf,df->rd", grad_projected, gate_up_full, preferred_element_type=jnp.float32
            ).astype(jnp.bfloat16)
        )
        gate_up_part, down_part = (
            lax.psum_scatter(
                gate_up_term.astype(jnp.bfloat16), "fsdp", scatter_dimension=0, tiled=True
            ).astype(jnp.float32),
            lax.psum_scatter(
                down_term.astype(jnp.bfloat16), "fsdp", scatter_dimension=0, tiled=True
            ).astype(jnp.float32),
        )
        gate_up_shards.append(gate_up_part)
        down_shards.append(down_part)
    stacked_grads = jnp.stack(input_grads).reshape(1, local_count, recv_rows, model_width)
    grad_back = lax.all_to_all(
        stacked_grads, "expert", split_axis=2, concat_axis=0, tiled=True
    ).reshape(EXPERTS * CAP, model_width)
    grad_xn_second = grad_xn_second + jnp.sum(
        grad_back[buffer_rows].reshape(seq_len, TOP, model_width).astype(jnp.float32), axis=1
    )
    grad_hidden_norm, gain_moe_local = norm_second_pull(grad_xn_second)
    grad_hidden = grad_f + grad_hidden_norm
    grad_hidden_b = grad_hidden.astype(jnp.bfloat16)
    out_local = jnp.dot(attended.T, grad_hidden_b, preferred_element_type=jnp.float32)
    grad_attended = jnp.dot(grad_hidden_b, out_full.T, preferred_element_type=jnp.float32).astype(
        jnp.bfloat16
    )
    grad_heads = grad_attended.reshape(seq_len, KV_HEADS, group_size, HEAD_DIM)
    grad_query, grad_keys, grad_values = attend_backward(
        queries, keys, values, grad_heads, log_total
    )
    grad_joint = jnp.concatenate([grad_query, grad_keys, grad_values], axis=1).astype(jnp.bfloat16)
    qkv_local = jnp.dot(xn_first.T, grad_joint, preferred_element_type=jnp.float32)
    grad_xn_first = jnp.dot(grad_joint, qkv_full.T, preferred_element_type=jnp.float32)
    grad_token_norm, gain_attn_local = norm_first_pull(grad_xn_first)
    grad_tokens = grad_hidden + grad_token_norm
    sectioned_parts = (
        lax.psum_scatter(
            qkv_local.astype(jnp.bfloat16), "fsdp", scatter_dimension=0, tiled=True
        ).astype(jnp.float32),
        lax.psum_scatter(
            out_local.astype(jnp.bfloat16), "fsdp", scatter_dimension=0, tiled=True
        ).astype(jnp.float32),
    )
    grad_qkv, grad_out_proj = (
        lax.psum(sectioned_parts[0].astype(jnp.bfloat16), "expert").astype(jnp.float32),
        lax.psum(sectioned_parts[1].astype(jnp.bfloat16), "expert").astype(jnp.float32),
    )
    grad_norm_attn, grad_norm_moe, grad_router = lax.psum(
        (gain_attn_local, gain_moe_local, router_local), ("expert", "fsdp")
    )
    return (
        mixed,
        grad_tokens,
        grad_norm_attn,
        grad_qkv,
        grad_out_proj,
        grad_norm_moe,
        grad_router,
        jnp.stack(gate_up_shards),
        jnp.stack(down_shards),
    )


def solution(mesh):
    in_specs = (
        P(("expert", "fsdp"), None),
        P(("expert", "fsdp"), None),
        P(),
        P("fsdp", None),
        P("fsdp", None),
        P(),
        P(),
        P("expert", "fsdp", None),
        P("expert", "fsdp", None),
        P(("expert", "fsdp"), None),
    )
    out_specs = (
        P(("expert", "fsdp"), None),
        P(("expert", "fsdp"), None),
        P(),
        P("fsdp", None),
        P("fsdp", None),
        P(),
        P(),
        P("expert", "fsdp", None),
        P("expert", "fsdp", None),
    )
    return jax.shard_map(shards, mesh=mesh, in_specs=in_specs, out_specs=out_specs, check_vma=False)
```

profile of v0, /device:TPU:0, one launch (start us, length us, event | category | flops | bytes accessed | tf_op | source)
XLA Modules:
  0.0 3326.3 jit_solution(17248810672932164687)
XLA Ops:
  24.2 9.0 reduce-window.6
  33.8 78.2 %all-gather.35.cloned.1.call-done = bf16[1536,2048]{1,0:T(8,128)(2,1)} async-done(((bf16[192,2048]{1,0:T(8,128)(2,1)}), bf16[1536,2048]{1,0:T(8,128)(2,1)}) %all-gather.35.cloned.1.call-update) | async-done | bytes 6291472 | tf_op jit(solution)/shard_map/all_gather | solution.py:118
  123.5 68.8 %all-gather.37.cloned.1.call-done = bf16[1536,1536]{1,0:T(8,128)(2,1)} async-done(((bf16[192,1536]{1,0:T(8,128)(2,1)}), bf16[1536,1536]{1,0:T(8,128)(2,1)}) %all-gather.37.cloned.1.call-update) | async-done | bytes 4718608 | tf_op jit(solution)/shard_map/all_gather | solution.py:119
  198.8 19.3 scatter_custom_fusion
  223.6 53.3 %all-to-all-done = bf16[4,8,48,1536]{3,2,1,0:T(8,128)(2,1)} async-done(((bf16[4,8,48,1536]{3,2,1,0:T(8,128)(2,1)}), bf16[4,8,48,1536]{3,2,1,0:T(8,128)(2,1)}, u32[]{:S(2)}, u32[]{:S(2)}) %all-to-all-start) | async-done | bytes 4718624 | tf_op jit(solution)/shard_map/all_to_all | solution.py:145
  286.4 66.7 %all-gather.39.cloned.1.call-done = bf16[1,1536,1536]{2,1,0:T(8,128)(2,1)} async-done(((bf16[1,192,1536]{2,1,0:T(8,128)(2,1)}), bf16[1,1536,1536]{2,1,0:T(8,128)(2,1)}) %all-gather.39.cloned.1.call-update) | async-done | bytes 4718608 | tf_op jit(solution)/shard_map/all_gather | solution.py:159
  358.8 75.1 %all-gather.43.cloned.1.call-done = bf16[1,1536,1536]{2,1,0:T(8,128)(2,1)} async-done(((bf16[1,192,1536]{2,1,0:T(8,128)(2,1)}), bf16[1,1536,1536]{2,1,0:T(8,128)(2,1)}) %all-gather.43.cloned.1.call-update) | async-done | bytes 4718608 | tf_op jit(solution)/shard_map/all_gather | solution.py:159
  439.4 74.6 %all-gather.47.cloned.1.call-done = bf16[1,1536,1536]{2,1,0:T(8,128)(2,1)} async-done(((bf16[1,192,1536]{2,1,0:T(8,128)(2,1)}), bf16[1,1536,1536]{2,1,0:T(8,128)(2,1)}) %all-gather.47.cloned.1.call-update) | async-done | bytes 4718608 | tf_op jit(solution)/shard_map/all_gather | solution.py:159
  519.6 74.6 %all-gather.51.cloned.1.call-done = bf16[1,1536,1536]{2,1,0:T(8,128)(2,1)} async-done(((bf16[1,192,1536]{2,1,0:T(8,128)(2,1)}), bf16[1,1536,1536]{2,1,0:T(8,128)(2,1)}) %all-gather.51.cloned.1.call-update) | async-done | bytes 4718608 | tf_op jit(solution)/shard_map/all_gather | solution.py:159
  599.7 74.7 %all-gather.55.cloned.1.call-done = bf16[1,1536,1536]{2,1,0:T(8,128)(2,1)} async-done(((bf16[1,192,1536]{2,1,0:T(8,128)(2,1)}), bf16[1,1536,1536]{2,1,0:T(8,128)(2,1)}) %all-gather.55.cloned.1.call-update) | async-done | bytes 4718608 | tf_op jit(solution)/shard_map/all_gather | solution.py:159
  680.0 75.3 %all-gather.59.cloned.1.call-done = bf16[1,1536,1536]{2,1,0:T(8,128)(2,1)} async-done(((bf16[1,192,1536]{2,1,0:T(8,128)(2,1)}), bf16[1,1536,1536]{2,1,0:T(8,128)(2,1)}) %all-gather.59.cloned.1.call-update) | async-done | bytes 4718608 | tf_op jit(solution)/shard_map/all_gather | solution.py:159
  760.8 75.1 %all-gather.67.cloned.1.call-done = bf16[1,1536,1536]{2,1,0:T(8,128)(2,1)} async-done(((bf16[1,192,1536]{2,1,0:T(8,128)(2,1)}), bf16[1,1536,1536]{2,1,0:T(8,128)(2,1)}) %all-gather.67.cloned.1.call-update) | async-done | bytes 4718608 | tf_op jit(solution)/shard_map/all_gather | solution.py:159
  841.5 46.9 %all-gather.41.cloned.1.call-done = bf16[1,768,1536]{2,1,0:T(8,128)(2,1)} async-done(((bf16[1,96,1536]{2,1,0:T(8,128)(2,1)}), bf16[1,768,1536]{2,1,0:T(8,128)(2,1)}) %all-gather.41.cloned.1.call-update) | async-done | bytes 2359312 | tf_op jit(solution)/shard_map/all_gather | solution.py:160
  891.6 49.5 %all-gather.45.cloned.1.call-done = bf16[1,768,1536]{2,1,0:T(8,128)(2,1)} async-done(((bf16[1,96,1536]{2,1,0:T(8,128)(2,1)}), bf16[1,768,1536]{2,1,0:T(8,128)(2,1)}) %all-gather.45.cloned.1.call-update) | async-done | bytes 2359312 | tf_op jit(solution)/shard_map/all_gather | solution.py:160
  944.2 49.6 %all-gather.49.cloned.1.call-done = bf16[1,768,1536]{2,1,0:T(8,128)(2,1)} async-done(((bf16[1,96,1536]{2,1,0:T(8,128)(2,1)}), bf16[1,768,1536]{2,1,0:T(8,128)(2,1)}) %all-gather.49.cloned.1.call-update) | async-done | bytes 2359312 | tf_op jit(solution)/shard_map/all_gather | solution.py:160
  997.1 49.5 %all-gather.53.cloned.1.call-done = bf16[1,768,1536]{2,1,0:T(8,128)(2,1)} async-done(((bf16[1,96,1536]{2,1,0:T(8,128)(2,1)}), bf16[1,768,1536]{2,1,0:T(8,128)(2,1)}) %all-gather.53.cloned.1.call-update) | async-done | bytes 2359312 | tf_op jit(solution)/shard_map/all_gather | solution.py:160
  1049.8 49.5 %all-gather.57.cloned.1.call-done = bf16[1,768,1536]{2,1,0:T(8,128)(2,1)} async-done(((bf16[1,96,1536]{2,1,0:T(8,128)(2,1)}), bf16[1,768,1536]{2,1,0:T(8,128)(2,1)}) %all-gather.57.cloned.1.call-update) | async-done | bytes 2359312 | tf_op jit(solution)/shard_map/all_gather | solution.py:160
  1102.4 49.5 %all-gather.61.cloned.1.call-done = bf16[1,768,1536]{2,1,0:T(8,128)(2,1)} async-done(((bf16[1,96,1536]{2,1,0:T(8,128)(2,1)}), bf16[1,768,1536]{2,1,0:T(8,128)(2,1)}) %all-gather.61.cloned.1.call-update) | async-done | bytes 2359312 | tf_op jit(solution)/shard_map/all_gather | solution.py:160
  1155.1 49.5 %all-gather.65.cloned.1.call-done = bf16[1,768,1536]{2,1,0:T(8,128)(2,1)} async-done(((bf16[1,96,1536]{2,1,0:T(8,128)(2,1)}), bf16[1,768,1536]{2,1,0:T(8,128)(2,1)}) %all-gather.65.cloned.1.call-update) | async-done | bytes 2359312 | tf_op jit(solution)/shard_map/all_gather | solution.py:160
  1207.7 49.6 %all-gather.69.cloned.1.call-done = bf16[1,768,1536]{2,1,0:T(8,128)(2,1)} async-done(((bf16[1,96,1536]{2,1,0:T(8,128)(2,1)}), bf16[1,768,1536]{2,1,0:T(8,128)(2,1)}) %all-gather.69.cloned.1.call-update) | async-done | bytes 2359312 | tf_op jit(solution)/shard_map/all_gather | solution.py:160
  1277.4 7.7 mul.660
  1291.7 34.8 %all-to-all-done.1 = bf16[1,8,192,1536]{3,1,0,2:T(8,128)(2,1)} async-done(((bf16[1,8,192,1536]{3,1,0,2:T(8,128)(2,1)}), bf16[1,8,192,1536]{3,1,0,2:T(8,128)(2,1)}, u32[]{:S(2)}, u32[]{:S(2)}) %all-to-all-start.1) | async-done | bytes 4718624 | tf_op jit(solution)/shard_map/all_to_all | solution.py:171
  1332.6 10.3 gather_fusion
  1361.9 9.7 scatter_custom_fusion.1
  1371.6 57.6 %all_to_all.60 = bf16[4,8,48,1536]{3,2,1,0:T(8,128)(2,1)S(1)} all-to-all(bf16[4,8,48,1536]{3,2,1,0:T(8,128)(2,1)} %bitcast.453), channel_id=1, replica_groups=mesh['expert'=4,'fsdp'=8] {'expert'}, dimensions={0} | all-to-all | bytes 9437184 | tf_op jit(solution)/shard_map/all_to_all | solution.py:195
  1483.5 45.4 %all-to-all-done.3 = bf16[1,8,192,1536]{3,1,0,2:T(8,128)(2,1)} async-done(((bf16[1,8,192,1536]{3,1,0,2:T(8,128)(2,1)}), bf16[1,8,192,1536]{3,1,0,2:T(8,128)(2,1)}, u32[]{:S(2)}, u32[]{:S(2)}) %all-to-all-start.3) | async-done | bytes 4718624 | tf_op jit(solution)/shard_map/all_to_all | solution.py:238
  1535.0 10.5 gather_fusion.1
  1648.4 13.9 reduce-scatter.21.cloned.1.call-done
  1662.3 121.8 %reduce-scatter.19.cloned.1.call-done = bf16[192,2048]{1,0:T(8,128)(2,1)} async-done(((bf16[1536,2048]{1,0:T(8,128)(2,1)}), bf16[192,2048]{1,0:T(8,128)(2,1)}) %reduce-scatter.19.cloned.1.call-update) | async-done | bytes 786448 | tf_op jit(solution)/shard_map/reduce_scatter | solution.py:261
  1792.0 40.6 %all-reduce.16 = (f32[1536]{0:T(1024)}, f32[1536]{0:T(1024)}) all-reduce(f32[1536]{0:T(1024)S(1)} %get-tuple-element.47, f32[1536]{0:T(1024)S(1)} %copy-done.120), channel_id=1, replica_groups=mesh['expert'=4,'fsdp'=8] {'expert','fsdp'}, use_global_device_ids=true, to_apply=%region_19.20 | all-reduce | flops 3072 | bytes 24576 | tf_op jit(solution)/shard_map/psum | solution.py:272
  1832.6 23.9 reduce-scatter.39.cloned.1.call-done
  1857.5 70.6 %reduce-scatter.41.cloned.1.call-done = bf16[96,1536]{1,0:T(8,128)(2,1)} async-done(((bf16[768,1536]{1,0:T(8,128)(2,1)}), bf16[96,1536]{1,0:T(8,128)(2,1)}) %reduce-scatter.41.cloned.1.call-update) | async-done | bytes 294928 | tf_op jit(solution)/shard_map/reduce_scatter | solution.py:231
  1929.0 70.6 %reduce-scatter.43.cloned.1.call-done = bf16[96,1536]{1,0:T(8,128)(2,1)} async-done(((bf16[768,1536]{1,0:T(8,128)(2,1)}), bf16[96,1536]{1,0:T(8,128)(2,1)}) %reduce-scatter.43.cloned.1.call-update) | async-done | bytes 294928 | tf_op jit(solution)/shard_map/reduce_scatter | solution.py:231
  2000.6 70.4 %reduce-scatter.45.cloned.1.call-done = bf16[96,1536]{1,0:T(8,128)(2,1)} async-done(((bf16[768,1536]{1,0:T(8,128)(2,1)}), bf16[96,1536]{1,0:T(8,128)(2,1)}) %reduce-scatter.45.cloned.1.call-update) | async-done | bytes 294928 | tf_op jit(solution)/shard_map/reduce_scatter | solution.py:231
  2072.0 70.5 %reduce-scatter.47.cloned.1.call-done = bf16[96,1536]{1,0:T(8,128)(2,1)} async-done(((bf16[768,1536]{1,0:T(8,128)(2,1)}), bf16[96,1536]{1,0:T(8,128)(2,1)}) %reduce-scatter.47.cloned.1.call-update) | async-done | bytes 294928 | tf_op jit(solution)/shard_map/reduce_scatter | solution.py:231
  2143.5 70.4 %reduce-scatter.49.cloned.1.call-done = bf16[96,1536]{1,0:T(8,128)(2,1)} async-done(((bf16[768,1536]{1,0:T(8,128)(2,1)}), bf16[96,1536]{1,0:T(8,128)(2,1)}) %reduce-scatter.49.cloned.1.call-update) | async-done | bytes 294928 | tf_op jit(solution)/shard_map/reduce_scatter | solution.py:231
  2214.9 70.4 %reduce-scatter.51.cloned.1.call-done = bf16[96,1536]{1,0:T(8,128)(2,1)} async-done(((bf16[768,1536]{1,0:T(8,128)(2,1)}), bf16[96,1536]{1,0:T(8,128)(2,1)}) %reduce-scatter.51.cloned.1.call-update) | async-done | bytes 294928 | tf_op jit(solution)/shard_map/reduce_scatter | solution.py:231
  2286.3 70.6 %reduce-scatter.53.cloned.1.call-done = bf16[96,1536]{1,0:T(8,128)(2,1)} async-done(((bf16[768,1536]{1,0:T(8,128)(2,1)}), bf16[96,1536]{1,0:T(8,128)(2,1)}) %reduce-scatter.53.cloned.1.call-update) | async-done | bytes 294928 | tf_op jit(solution)/shard_map/reduce_scatter | solution.py:231
  2360.7 94.2 %reduce-scatter.23.cloned.1.call-done = bf16[192,1536]{1,0:T(8,128)(2,1)} async-done(((bf16[1536,1536]{1,0:T(8,128)(2,1)}), bf16[192,1536]{1,0:T(8,128)(2,1)}) %reduce-scatter.23.cloned.1.call-update) | async-done | bytes 589840 | tf_op jit(solution)/shard_map/reduce_scatter | solution.py:228
  2456.8 96.6 %reduce-scatter.25.cloned.1.call-done = bf16[192,1536]{1,0:T(8,128)(2,1)} async-done(((bf16[1536,1536]{1,0:T(8,128)(2,1)}), bf16[192,1536]{1,0:T(8,128)(2,1)}) %reduce-scatter.25.cloned.1.call-update) | async-done | bytes 589840 | tf_op jit(solution)/shard_map/reduce_scatter | solution.py:228
  2555.3 96.8 %reduce-scatter.27.cloned.1.call-done = bf16[192,1536]{1,0:T(8,128)(2,1)} async-done(((bf16[1536,1536]{1,0:T(8,128)(2,1)}), bf16[192,1536]{1,0:T(8,128)(2,1)}) %reduce-scatter.27.cloned.1.call-update) | async-done | bytes 589840 | tf_op jit(solution)/shard_map/reduce_scatter | solution.py:228
  2654.1 96.8 %reduce-scatter.29.cloned.1.call-done = bf16[192,1536]{1,0:T(8,128)(2,1)} async-done(((bf16[1536,1536]{1,0:T(8,128)(2,1)}), bf16[192,1536]{1,0:T(8,128)(2,1)}) %reduce-scatter.29.cloned.1.call-update) | async-done | bytes 589840 | tf_op jit(solution)/shard_map/reduce_scatter | solution.py:228
  2752.8 96.6 %reduce-scatter.31.cloned.1.call-done = bf16[192,1536]{1,0:T(8,128)(2,1)} async-done(((bf16[1536,1536]{1,0:T(8,128)(2,1)}), bf16[192,1536]{1,0:T(8,128)(2,1)}) %reduce-scatter.31.cloned.1.call-update) | async-done | bytes 589840 | tf_op jit(solution)/shard_map/reduce_scatter | solution.py:228
  2851.4 96.8 %reduce-scatter.33.cloned.1.call-done = bf16[192,1536]{1,0:T(8,128)(2,1)} async-done(((bf16[1536,1536]{1,0:T(8,128)(2,1)}), bf16[192,1536]{1,0:T(8,128)(2,1)}) %reduce-scatter.33.cloned.1.call-update) | async-done | bytes 589840 | tf_op jit(solution)/shard_map/reduce_scatter | solution.py:228
  2950.1 96.9 %reduce-scatter.35.cloned.1.call-done = bf16[192,1536]{1,0:T(8,128)(2,1)} async-done(((bf16[1536,1536]{1,0:T(8,128)(2,1)}), bf16[192,1536]{1,0:T(8,128)(2,1)}) %reduce-scatter.35.cloned.1.call-update) | async-done | bytes 589840 | tf_op jit(solution)/shard_map/reduce_scatter | solution.py:228
  3048.9 96.8 %reduce-scatter.37.cloned.1.call-done = bf16[192,1536]{1,0:T(8,128)(2,1)} async-done(((bf16[1536,1536]{1,0:T(8,128)(2,1)}), bf16[192,1536]{1,0:T(8,128)(2,1)}) %reduce-scatter.37.cloned.1.call-update) | async-done | bytes 589840 | tf_op jit(solution)/shard_map/reduce_scatter | solution.py:228
  3155.0 32.9 all-reduce.23.cloned.1.call-done
  3191.6 126.4 %all-reduce.21.cloned.1.call-done = f32[1536,32]{0,1:T(8,128)} async-done(((f32[1536,32]{0,1:T(8,128)}), f32[1536,32]{0,1:T(8,128)}) %all-reduce.21.cloned.1.call-update) | async-done | bytes 196624 | tf_op jit(solution)/shard_map/psum | solution.py:272
  (537 shorter events, 371.5 us)
Async XLA Ops:
  7.2 1279.2 %copy-start = (bf16[1536,32]{0,1:T(8,128)(2,1)S(1)}, bf16[1536,32]{0,1:T(8,128)(2,1)}, u32[]{:S(2)}) copy-start(bf16[1536,32]{0,1:T(8,128)(2,1)} %param.16) | copy-start | bytes 294916
  7.2 104.8 %all-gather.35.cloned.1.call-start = ((), (), s32[]{:S(2)}) async-start(), calls=%async_computation.22 | async-start | bytes 7077888 | tf_op jit(solution)/shard_map/all_gather | solution.py:118
  7.9 184.3 %all-gather.37.cloned.1.call-start = ((), (), s32[]{:S(2)}) async-start(), calls=%async_computation.23 | async-start | bytes 5308416 | tf_op jit(solution)/shard_map/all_gather | solution.py:119
  8.7 272.8 %all-gather.63.cloned.1.call-start = ((), (), s32[]{:S(2)}) async-start(), calls=%async_computation.55 | async-start | bytes 5308416 | tf_op jit(solution)/shard_map/all_gather | solution.py:159
  13.3 339.9 %all-gather.39.cloned.1.call-start = ((), (), s32[]{:S(2)}) async-start(), calls=%async_computation.43 | async-start | bytes 5308416 | tf_op jit(solution)/shard_map/all_gather | solution.py:159
  13.9 420.0 %all-gather.43.cloned.1.call-start = ((), (), s32[]{:S(2)}) async-start(), calls=%async_computation.45 | async-start | bytes 5308416 | tf_op jit(solution)/shard_map/all_gather | solution.py:159
  14.5 499.5 %all-gather.47.cloned.1.call-start = ((), (), s32[]{:S(2)}) async-start(), calls=%async_computation.47 | async-start | bytes 5308416 | tf_op jit(solution)/shard_map/all_gather | solution.py:159
  15.0 579.1 %all-gather.51.cloned.1.call-start = ((), (), s32[]{:S(2)}) async-start(), calls=%async_computation.49 | async-start | bytes 5308416 | tf_op jit(solution)/shard_map/all_gather | solution.py:159
  15.8 658.6 %all-gather.55.cloned.1.call-start = ((), (), s32[]{:S(2)}) async-start(), calls=%async_computation.51 | async-start | bytes 5308416 | tf_op jit(solution)/shard_map/all_gather | solution.py:159
  16.5 738.7 %all-gather.59.cloned.1.call-start = ((), (), s32[]{:S(2)}) async-start(), calls=%async_computation.53 | async-start | bytes 5308416 | tf_op jit(solution)/shard_map/all_gather | solution.py:159
  17.3 818.6 %all-gather.67.cloned.1.call-start = ((), (), s32[]{:S(2)}) async-start(), calls=%async_computation.57 | async-start | bytes 5308416 | tf_op jit(solution)/shard_map/all_gather | solution.py:159
  17.9 870.5 %all-gather.41.cloned.1.call-start = ((), (), s32[]{:S(2)}) async-start(), calls=%async_computation.44 | async-start | bytes 2654208 | tf_op jit(solution)/shard_map/all_gather | solution.py:160
  19.6 921.5 %all-gather.45.cloned.1.call-start = ((), (), s32[]{:S(2)}) async-start(), calls=%async_computation.46 | async-start | bytes 2654208 | tf_op jit(solution)/shard_map/all_gather | solution.py:160
  20.1 973.7 %all-gather.49.cloned.1.call-start = ((), (), s32[]{:S(2)}) async-start(), calls=%async_computation.48 | async-start | bytes 2654208 | tf_op jit(solution)/shard_map/all_gather | solution.py:160
  20.9 1025.7 %all-gather.53.cloned.1.call-start = ((), (), s32[]{:S(2)}) async-start(), calls=%async_computation.50 | async-start | bytes 2654208 | tf_op jit(solution)/shard_map/all_gather | solution.py:160
  21.5 1077.8 %all-gather.57.cloned.1.call-start = ((), (), s32[]{:S(2)}) async-start(), calls=%async_computation.52 | async-start | bytes 2654208 | tf_op jit(solution)/shard_map/all_gather | solution.py:160
  22.0 1129.8 %all-gather.61.cloned.1.call-start = ((), (), s32[]{:S(2)}) async-start(), calls=%async_computation.54 | async-start | bytes 2654208 | tf_op jit(solution)/shard_map/all_gather | solution.py:160
  22.6 1182.0 %all-gather.65.cloned.1.call-start = ((), (), s32[]{:S(2)}) async-start(), calls=%async_computation.56 | async-start | bytes 2654208 | tf_op jit(solution)/shard_map/all_gather | solution.py:160
  33.8 165.0 %copy-start.126 = (s32[1024,1]{0,1:T(1,128)}, s32[1024,1]{0,1:T(1,128)S(1)}, u32[]{:S(2)}) copy-start(s32[1024,1]{0,1:T(1,128)S(1)} %compare_select_fusion.1) | copy-start | bytes 12292
  218.1 58.8 %all-to-all-start = ((bf16[4,8,48,1536]{3,2,1,0:T(8,128)(2,1)}), bf16[4,8,48,1536]{3,2,1,0:T(8,128)(2,1)}, u32[]{:S(2)}, u32[]{:S(2)}) async-start(bf16[4,8,48,1536]{3,2,1,0:T(8,128)(2,1)} %bitcast.451), calls=%async_computation | async-start | bytes 9437184 | tf_op jit(solution)/shard_map/all_to_all | solution.py:145
  223.0 1034.2 %all-gather.69.cloned.1.call-start = ((), (), s32[]{:S(2)}) async-start(), calls=%async_computation.58 | async-start | bytes 2654208 | tf_op jit(solution)/shard_map/all_gather | solution.py:160
  1267.5 59.0 %all-to-all-start.1 = ((bf16[1,8,192,1536]{3,1,0,2:T(8,128)(2,1)}), bf16[1,8,192,1536]{3,1,0,2:T(8,128)(2,1)}, u32[]{:S(2)}, u32[]{:S(2)}) async-start(bf16[1,8,192,1536]{3,1,0,2:T(8,128)(2,1)} %copy.89), calls=%async_computation.1 | async-start | bytes 9437184 | tf_op jit(solution)/shard_map/all_to_all | solution.py:171
  1470.1 58.8 %all-to-all-start.3 = ((bf16[1,8,192,1536]{3,1,0,2:T(8,128)(2,1)}), bf16[1,8,192,1536]{3,1,0,2:T(8,128)(2,1)}, u32[]{:S(2)}, u32[]{:S(2)}) async-start(bf16[1,8,192,1536]{3,1,0,2:T(8,128)(2,1)} %copy.92), calls=%async_computation.3 | async-start | bytes 9437184 | tf_op jit(solution)/shard_map/all_to_all | solution.py:238
  1475.0 187.2 %reduce-scatter.21.cloned.1.call-start = ((), (), s32[]{:S(2)}) async-start(), calls=%async_computation.25 | async-start | bytes 5308416 | tf_op jit(solution)/shard_map/reduce_scatter | solution.py:264
  1569.3 214.8 %reduce-scatter.19.cloned.1.call-start = ((), (), s32[]{:S(2)}) async-start(), calls=%async_computation.24 | async-start | bytes 7077888 | tf_op jit(solution)/shard_map/reduce_scatter | solution.py:261
  1589.1 267.4 %reduce-scatter.39.cloned.1.call-start = ((), (), s32[]{:S(2)}) async-start(), calls=%async_computation.35 | async-start | bytes 2654208 | tf_op jit(solution)/shard_map/reduce_scatter | solution.py:231
  1592.5 335.6 %reduce-scatter.41.cloned.1.call-start = ((), (), s32[]{:S(2)}) async-start(), calls=%async_computation.36 | async-start | bytes 2654208 | tf_op jit(solution)/shard_map/reduce_scatter | solution.py:231
  1594.8 404.8 %reduce-scatter.43.cloned.1.call-start = ((), (), s32[]{:S(2)}) async-start(), calls=%async_computation.37 | async-start | bytes 2654208 | tf_op jit(solution)/shard_map/reduce_scatter | solution.py:231
  1597.1 473.9 %reduce-scatter.45.cloned.1.call-start = ((), (), s32[]{:S(2)}) async-start(), calls=%async_computation.38 | async-start | bytes 2654208 | tf_op jit(solution)/shard_map/reduce_scatter | solution.py:231
  1599.4 543.1 %reduce-scatter.47.cloned.1.call-start = ((), (), s32[]{:S(2)}) async-start(), calls=%async_computation.39 | async-start | bytes 2654208 | tf_op jit(solution)/shard_map/reduce_scatter | solution.py:231
  1601.7 612.2 %reduce-scatter.49.cloned.1.call-start = ((), (), s32[]{:S(2)}) async-start(), calls=%async_computation.40 | async-start | bytes 2654208 | tf_op jit(solution)/shard_map/reduce_scatter | solution.py:231
  1604.1 681.2 %reduce-scatter.51.cloned.1.call-start = ((), (), s32[]{:S(2)}) async-start(), calls=%async_computation.41 | async-start | bytes 2654208 | tf_op jit(solution)/shard_map/reduce_scatter | solution.py:231
  1606.5 750.4 %reduce-scatter.53.cloned.1.call-start = ((), (), s32[]{:S(2)}) async-start(), calls=%async_computation.42 | async-start | bytes 2654208 | tf_op jit(solution)/shard_map/reduce_scatter | solution.py:231
  1609.2 845.7 %reduce-scatter.23.cloned.1.call-start = ((), (), s32[]{:S(2)}) async-start(), calls=%async_computation.27 | async-start | bytes 5308416 | tf_op jit(solution)/shard_map/reduce_scatter | solution.py:228
  1613.0 940.4 %reduce-scatter.25.cloned.1.call-start = ((), (), s32[]{:S(2)}) async-start(), calls=%async_computation.28 | async-start | bytes 5308416 | tf_op jit(solution)/shard_map/reduce_scatter | solution.py:228
  1618.0 1034.2 %reduce-scatter.27.cloned.1.call-start = ((), (), s32[]{:S(2)}) async-start(), calls=%async_computation.29 | async-start | bytes 5308416 | tf_op jit(solution)/shard_map/reduce_scatter | solution.py:228
  1623.0 1127.8 %reduce-scatter.29.cloned.1.call-start = ((), (), s32[]{:S(2)}) async-start(), calls=%async_computation.30 | async-start | bytes 5308416 | tf_op jit(solution)/shard_map/reduce_scatter | solution.py:228
  1628.2 1221.2 %reduce-scatter.31.cloned.1.call-start = ((), (), s32[]{:S(2)}) async-start(), calls=%async_computation.31 | async-start | bytes 5308416 | tf_op jit(solution)/shard_map/reduce_scatter | solution.py:228
  1633.2 1314.9 %reduce-scatter.33.cloned.1.call-start = ((), (), s32[]{:S(2)}) async-start(), calls=%async_computation.32 | async-start | bytes 5308416 | tf_op jit(solution)/shard_map/reduce_scatter | solution.py:228
  1638.3 1408.7 %reduce-scatter.35.cloned.1.call-start = ((), (), s32[]{:S(2)}) async-start(), calls=%async_computation.33 | async-start | bytes 5308416 | tf_op jit(solution)/shard_map/reduce_scatter | solution.py:228
  1643.3 1502.5 %reduce-scatter.37.cloned.1.call-start = ((), (), s32[]{:S(2)}) async-start(), calls=%async_computation.34 | async-start | bytes 5308416 | tf_op jit(solution)/shard_map/reduce_scatter | solution.py:228
  1648.3 137.0 %copy-start.5 = (bf16[256,1536]{1,0:T(8,128)(2,1)S(1)}, bf16[256,1536]{1,0:T(8,128)(2,1)}, u32[]{:S(2)}) copy-start(bf16[256,1536]{1,0:T(8,128)(2,1)} %param.10) | copy-start | bytes 2359300
  1648.3 137.0 %copy-start.37 = (bf16[2,128,6,256]{3,1,2,0:T(8,128)(2,1)S(1)}, bf16[2,128,6,256]{3,1,2,0:T(8,128)(2,1)}, u32[]{:S(2)}) copy-start(bf16[2,128,6,256]{3,1,2,0:T(8,128)(2,1)} %copy-done.36) | copy-start | bytes 2359300
  1648.3 137.0 %copy-start.107 = (bf16[2,128,256]{2,1,0:T(8,128)(2,1)S(1)}, bf16[2,128,256]{2,1,0:T(8,128)(2,1)}, u32[]{:S(2)}) copy-start(bf16[2,128,256]{2,1,0:T(8,128)(2,1)} %copy-done.106) | copy-start | bytes 393220
  1648.3 137.0 %copy-start.112 = (bf16[2,128,256]{2,1,0:T(8,128)(2,1)S(1)}, bf16[2,128,256]{2,1,0:T(8,128)(2,1)}, u32[]{:S(2)}) copy-start(bf16[2,128,256]{2,1,0:T(8,128)(2,1)} %copy-done.111) | copy-start | bytes 393220
  1648.4 136.9 %copy-start.119 = (f32[1536]{0:T(1024)S(1)}, f32[1536]{0:T(1024)}, u32[]{:S(2)}) copy-start(f32[1536]{0:T(1024)} %param.12) | copy-start | bytes 18436
  1648.4 1539.6 %all-reduce.23.cloned.1.call-start = ((), (), s32[]{:S(2)}) async-start(), calls=%async_computation.59 | async-start | bytes 2752512 | tf_op jit(solution)/shard_map/psum | solution.py:269
  1784.1 1533.9 %all-reduce.21.cloned.1.call-start = ((), (), s32[]{:S(2)}) async-start(), calls=%async_computation.26 | async-start | bytes 393216 | tf_op jit(solution)/shard_map/psum | solution.py:272
  (141 other events, 1283.3 us)
Sparse Core Ops, SparseCore 0:
  10.2 101.7 all-gather.34
  114.1 78.0 all-gather.36
  194.4 78.0 all-gather.62
  275.1 78.0 all-gather.38
  355.8 78.0 all-gather.42
  435.9 78.0 all-gather.46
  516.1 78.0 all-gather.50
  596.4 78.0 all-gather.54
  677.2 78.0 all-gather.58
  757.8 78.0 all-gather.66
  838.1 50.2 all-gather.40
  890.4 50.5 all-gather.44
  943.2 50.5 all-gather.48
  995.9 50.5 all-gather.52
  1048.6 50.5 all-gather.56
  1101.2 50.5 all-gather.60
  1153.9 50.5 all-gather.64
  1206.6 50.5 all-gather.68
  1569.4 92.8 reduce-scatter.20
  1666.3 117.7 reduce-scatter.18
  1787.6 68.8 reduce-scatter.38
  1860.0 68.0 reduce-scatter.40
  1931.6 67.9 reduce-scatter.42
  2003.0 67.9 reduce-scatter.44
  2074.5 67.9 reduce-scatter.46
  2145.9 67.9 reduce-scatter.48
  2217.3 67.9 reduce-scatter.50
  2288.8 68.0 reduce-scatter.52
  2360.5 94.2 reduce-scatter.22
  2458.4 94.9 reduce-scatter.24
  2557.1 95.0 reduce-scatter.26
  2655.8 94.9 reduce-scatter.28
  2754.3 95.0 reduce-scatter.30
  2853.1 95.0 reduce-scatter.32
  2951.8 95.1 reduce-scatter.34
  3050.5 95.1 reduce-scatter.36
  3148.1 39.8 all-reduce.22
  3195.0 122.9 all-reduce.20
where the time goes:
time: 3340 us; the launch traced here: 3330 us
  waiting for transfers between devices  2780 us (83%)
  matrix products  180 us (5%)
  local copies, waits for them, and re-layouts  167 us (5%)
  blocking collectives  98.2 us (3%)
  other arithmetic  63.4 us (2%)
    reduce_scatter x8, waiting for transfers between devices, shards(): lax.psum_scatter(gate_up_term.astype(jnp.bfloat16), 'fsdp', scatter_dimen...  772 us
    reduce_scatter x8, waiting for transfers between devices, shards(): lax.psum_scatter(down_term.astype(jnp.bfloat16), 'fsdp', scatter_dimensio...  517 us
    all_gather x8, waiting for transfers between devices, shards(): lax.all_gather(gate_up[member], 'fsdp', axis=0, tiled=True)  516 us
    all_gather x8, waiting for transfers between devices, shards(): lax.all_gather(down[member], 'fsdp', axis=0, tiled=True)  393 us
    psum x1, waiting for transfers between devices, shards(): lax.psum((gain_attn_local, gain_moe_local, router_local), ('expert', 'fsd...  126 us
    reduce_scatter x1, waiting for transfers between devices, shards(): lax.psum_scatter(qkv_local.astype(jnp.bfloat16), 'fsdp', scatter_dimensio...  122 us
    all_gather x1, waiting for transfers between devices, shards(): lax.all_gather(qkv_weight, 'fsdp', axis=0, tiled=True)  78.2 us
    all_gather x1, waiting for transfers between devices, shards(): lax.all_gather(out_weight, 'fsdp', axis=0, tiled=True)  68.8 us
  transfers between devices with their start and end apart: 41, of which 40 were waited for; matrix products, arithmetic and copies ran while one was open for 8% of the time, Pallas kernels for 0%

commit v1 on v0

v1 whole, which is shorter than its diff:
```python
import jax
import jax.numpy as jnp
from jax import lax
from jax.sharding import PartitionSpec as P

HEADS = 12
KV_HEADS = 2
HEAD_DIM = 128
FFE = 768
EXPERTS = 32
TOP = 4
CAP = 48
EPSILON = 1e-06
BOTH = ("expert", "fsdp")
f32 = jnp.float32
bf16 = jnp.bfloat16


def dot(a, b):
    return jnp.dot(a, b, preferred_element_type=f32)


def dot_t(a, b):
    return lax.dot_general(a, b, (((1,), (1,)), ((), ())), preferred_element_type=f32)


def t_dot(a, b):
    return lax.dot_general(a, b, (((0,), (0,)), ((), ())), preferred_element_type=f32)


def rms_apply(values, gain):
    return values * lax.rsqrt(jnp.mean(values * values, axis=-1, keepdims=True) + EPSILON) * gain


def reglu_smooth(projected):
    return jax.nn.gelu(projected[..., :FFE]) * projected[..., FFE:]


def attention_probs(queries, keys):
    seq_len = queries.shape[0]
    scores = jnp.einsum("qhgd,khd->hgqk", queries, keys, preferred_element_type=f32) * HEAD_DIM ** (-0.5)
    causal = jnp.arange(seq_len)[:, None] >= jnp.arange(seq_len)[None, :]
    scores = jnp.where(causal, scores, -1e30)
    row_max = jnp.max(scores, axis=-1, keepdims=True)
    exponent = jnp.exp(scores - row_max)
    return exponent / jnp.sum(exponent, axis=-1, keepdims=True)


def attend_backward(queries, keys, values, grad_heads):
    seq_len = queries.shape[0]
    score_scale = HEAD_DIM ** (-0.5)
    attn_full = attention_probs(queries, keys)
    attn_probs = attn_full.astype(bf16)
    grad_probs = jnp.einsum("qhgd,khd->hgqk", grad_heads, values, preferred_element_type=f32)
    delta = jnp.sum(attn_full * grad_probs, axis=-1, keepdims=True)
    grad_scores = (attn_full * (grad_probs - delta)).astype(bf16)
    grad_query = jnp.einsum("hgqk,khd->qhgd", grad_scores, keys, preferred_element_type=f32) * score_scale
    grad_keys = jnp.einsum("hgqk,qhgd->khd", grad_scores, queries, preferred_element_type=f32) * score_scale
    grad_values = jnp.einsum("hgqk,qhgd->khd", attn_probs, grad_heads, preferred_element_type=f32)
    return (
        grad_query.reshape(seq_len, -1),
        grad_keys.reshape(seq_len, -1),
        grad_values.reshape(seq_len, -1),
    )


def shards(
    tokens,
    routes,
    norm_attn,
    qkv_weight,
    out_weight,
    norm_moe,
    router_weight,
    gate_up,
    down,
    grad_output,
):
    seq_len, model_width = tokens.shape
    query_width = HEADS * HEAD_DIM
    kv_width = KV_HEADS * HEAD_DIM
    group_size = HEADS // KV_HEADS
    fsdp = lax.axis_size("fsdp")
    devices = lax.axis_size("expert") * fsdp
    local_count = gate_up.shape[0]
    parts = fsdp // local_count
    rows = EXPERTS * CAP

    def to_owner(weight):
        whole = weight
        if parts > 1:
            whole = jnp.repeat(weight, parts, axis=0)
        return lax.all_to_all(whole, "fsdp", split_axis=0, concat_axis=0, tiled=True).reshape(
            -1, weight.shape[-1]
        )

    def to_shards(grad, like):
        back = lax.all_to_all(
            grad.reshape(fsdp, like.shape[1], like.shape[2]), "fsdp", split_axis=0, concat_axis=0, tiled=True
        ).astype(f32)
        if parts > 1:
            back = jnp.sum(back.reshape((local_count, parts) + like.shape[1:]), axis=1)
        return back

    def exchange(buffer):
        width = buffer.shape[-1]
        return lax.all_to_all(
            buffer.reshape(devices, rows // devices, width), BOTH, split_axis=0, concat_axis=0, tiled=True
        ).reshape(rows, width)

    token_f = tokens.astype(f32)
    grad_f = grad_output.astype(f32)
    qkv_full, out_full = (
        lax.all_gather(qkv_weight, "fsdp", axis=0, tiled=True),
        lax.all_gather(out_weight, "fsdp", axis=0, tiled=True),
    )

    expert_ids = jnp.arange(EXPERTS, dtype=jnp.int32)
    chosen_mask = routes[:, :, None] == expert_ids[None, None, :]
    mask = jnp.any(chosen_mask, axis=1)
    mask_b = mask.astype(bf16)
    order = jnp.arange(seq_len)
    earlier = (order[None, :] < order[:, None]).astype(bf16)
    position = dot(earlier, mask_b).astype(jnp.int32)
    slot = jnp.where(mask, position, -1).T
    place = (slot[:, None, :] == jnp.arange(CAP, dtype=jnp.int32)[None, :, None]).astype(bf16)
    place = place.reshape(rows, seq_len)

    grad_rows = exchange(dot(place, grad_output).astype(bf16))
    gate_up_full = to_owner(gate_up)
    down_full = to_owner(down)

    xn_first_f, norm_first_pull = jax.vjp(rms_apply, token_f, norm_attn)
    xn_first = xn_first_f.astype(bf16)
    joint = dot(xn_first, qkv_full).astype(bf16)
    queries = joint[:, :query_width].reshape(seq_len, KV_HEADS, group_size, HEAD_DIM)
    keys = joint[:, query_width : query_width + kv_width].reshape(seq_len, KV_HEADS, HEAD_DIM)
    values = joint[:, query_width + kv_width :].reshape(seq_len, KV_HEADS, HEAD_DIM)
    probs = attention_probs(queries, keys).astype(bf16)
    attended = (
        jnp.einsum("hgqk,khd->qhgd", probs, values, preferred_element_type=f32)
        .astype(bf16)
        .reshape(seq_len, query_width)
    )
    hidden = token_f + dot(attended, out_full)
    xn_second_f, norm_second_pull = jax.vjp(rms_apply, hidden, norm_moe)
    xn_second = xn_second_f.astype(bf16)

    logits = dot(xn_second, router_weight)
    masked = jnp.where(mask, logits, -1e30)
    exponent = jnp.where(mask, jnp.exp(masked - jnp.max(masked, axis=-1, keepdims=True)), 0.0)
    gates = exponent / jnp.sum(exponent, axis=-1, keepdims=True)

    received = exchange(dot(place, xn_second).astype(bf16))
    place_cube = place.reshape(EXPERTS, CAP, seq_len).astype(f32)
    gate_send = jnp.sum(place_cube * gates.T[:, None, :], axis=-1)
    gate_rows = exchange(gate_send.reshape(rows, 1))

    projected = dot(received, gate_up_full)
    inner, reglu_pull = jax.vjp(reglu_smooth, projected)
    inner = inner.astype(bf16)
    expert_out = dot(inner, down_full).astype(bf16)
    d_gate_rows = jnp.sum(expert_out.astype(f32) * grad_rows.astype(f32), axis=-1, keepdims=True)
    d_out = (gate_rows * grad_rows.astype(f32)).astype(bf16)
    d_inner = dot_t(d_out, down_full)
    d_projected = reglu_pull(d_inner)[0].astype(bf16)
    d_pair_in = dot_t(d_projected, gate_up_full).astype(bf16)
    grad_down = to_shards(t_dot(inner, d_out).astype(bf16), down)
    grad_gate_up = to_shards(t_dot(received, d_projected).astype(bf16), gate_up)

    back_in = exchange(d_pair_in)
    back_gate = exchange(d_gate_rows)
    back_out = exchange(expert_out)

    gate_place = jnp.where(place_cube > 0, gates.T[:, None, :], 0.0).reshape(rows, seq_len)
    gate_hi = gate_place.astype(bf16)
    gate_lo = (gate_place - gate_hi.astype(f32)).astype(bf16)
    moe_sum = t_dot(gate_hi, back_out) + t_dot(gate_lo, back_out)
    mixed = (hidden + moe_sum).astype(bf16)
    d_gates = jnp.sum(place_cube * back_gate.reshape(EXPERTS, CAP, 1), axis=1).T
    d_chosen = gates * (d_gates - jnp.sum(gates * d_gates, axis=-1, keepdims=True))
    d_logits = d_chosen.astype(bf16)
    router_local = t_dot(xn_second, d_logits)
    d_xn_second = dot_t(d_logits, router_weight) + t_dot(place, back_in)

    d_hidden_norm, gain_moe_local = norm_second_pull(d_xn_second)
    d_hidden = grad_f + d_hidden_norm
    d_hidden_b = d_hidden.astype(bf16)
    out_local = t_dot(attended, d_hidden_b)
    d_attended = dot_t(d_hidden_b, out_full).astype(bf16)
    grad_heads = d_attended.reshape(seq_len, KV_HEADS, group_size, HEAD_DIM)
    grad_query, grad_keys, grad_values = attend_backward(queries, keys, values, grad_heads)
    grad_joint = jnp.concatenate([grad_query, grad_keys, grad_values], axis=1).astype(bf16)
    qkv_local = t_dot(xn_first, grad_joint)
    d_xn_first = dot_t(grad_joint, qkv_full)
    d_token_norm, gain_attn_local = norm_first_pull(d_xn_first)
    grad_tokens = d_hidden + d_token_norm

    sectioned = (
        lax.psum_scatter(qkv_local.astype(bf16), "fsdp", scatter_dimension=0, tiled=True),
        lax.psum_scatter(out_local.astype(bf16), "fsdp", scatter_dimension=0, tiled=True),
    )
    grad_qkv, grad_out_proj = (
        lax.psum(sectioned[0], "expert").astype(f32),
        lax.psum(sectioned[1], "expert").astype(f32),
    )
    grad_norm_attn, grad_norm_moe, grad_router = lax.psum(
        (gain_attn_local, gain_moe_local, router_local), BOTH
    )
    return (
        mixed,
        grad_tokens,
        grad_norm_attn,
        grad_qkv,
        grad_out_proj,
        grad_norm_moe,
        grad_router,
        grad_gate_up,
        grad_down,
    )


def solution(mesh):
    in_specs = (
        P(BOTH, None),
        P(BOTH, None),
        P(),
        P("fsdp", None),
        P("fsdp", None),
        P(),
        P(),
        P("expert", "fsdp", None),
        P("expert", "fsdp", None),
        P(BOTH, None),
    )
    out_specs = (
        P(BOTH, None),
        P(BOTH, None),
        P(),
        P("fsdp", None),
        P("fsdp", None),
        P(),
        P(),
        P("expert", "fsdp", None),
        P("expert", "fsdp", None),
    )
    return jax.shard_map(shards, mesh=mesh, in_specs=in_specs, out_specs=out_specs, check_vma=False)
```

time: 3340 us -> 1300 us (0.39)
  waiting for transfers between devices: 2780 us -> 1020 us
  local copies, waits for them, and re-layouts: 167 us -> 14.2 us
  matrix products: 180 us -> 121 us
  blocking collectives: 98.2 us -> 47 us
    reduce_scatter x18 -> x2, waiting for transfers between devices: 1420 us -> 138 us  [the longest x1 138 us: shards(): lax.psum_scatter(qkv_local.astype(bf16), 'fsdp', scatter_dimension=0, til...]
    all_gather x16 -> x0, waiting for transfers between devices: 909 us -> none  [the longest x8 516 us: shards(): lax.all_gather(gate_up[member], 'fsdp', axis=0, tiled=True)]
    all_to_all x3 -> x9, waiting for transfers between devices: 133 us -> 581 us  [the longest x5 302 us: exchange(): lax.all_to_all(buffer.reshape(devices, rows // devices, width), BOTH, spl...]
    dot_general x65 -> x26, matrix products: 180 us -> 118 us  [the longest x8 40.7 us: t_dot(): lax.dot_general(a, b, (((0,), (0,)), ((), ())), preferred_element_type=f32)]
    psum x2, waiting for transfers between devices: 159 us -> 103 us  [the longest x1 103 us: shards(): lax.psum((gain_attn_local, gain_moe_local, router_local), BOTH)]
    all_to_all x1, blocking collectives: 57.6 us -> 9.07 us  [exchange(): lax.all_to_all(buffer.reshape(devices, rows // devices, width), BOTH, spl...]
    all_gather x1, waiting for transfers between devices: 68.8 us -> 112 us  [shards(): lax.all_gather(out_weight, 'fsdp', axis=0, tiled=True)]
    unnamed x312 -> x85, local copies, waits for them, and re-layouts: 52.7 us -> 10 us
  transfers between devices with their start and end apart: 41 -> 15, of which waited for: 40 -> 11; matrix products, arithmetic and copies ran while one was open for 8% -> 9% of each run, Pallas kernels for 0% -> 0%
where the time goes in v1:
time: 1300 us; the launch traced here: 1290 us
  waiting for transfers between devices  1020 us (78%)
  matrix products  121 us (9%)
  blocking collectives  47 us (4%)
  starting transfers between devices  40 us (3%)
  other arithmetic  32.7 us (3%)
  between operations  15 us (1%)
  local copies, waits for them, and re-layouts  14.2 us (1%)
    all_to_all x5, waiting for transfers between devices, exchange(): lax.all_to_all(buffer.reshape(devices, rows // devices, width), BOTH, spl...  302 us
    all_to_all x2, waiting for transfers between devices, to_shards(): lax.all_to_all(grad.reshape(fsdp, like.shape[1], like.shape[2]), 'fsdp',...  201 us
    reduce_scatter x1, waiting for transfers between devices, shards(): lax.psum_scatter(qkv_local.astype(bf16), 'fsdp', scatter_dimension=0, til...  138 us
    all_gather x1, waiting for transfers between devices, shards(): lax.all_gather(out_weight, 'fsdp', axis=0, tiled=True)  112 us
    psum x1, waiting for transfers between devices, shards(): lax.psum((gain_attn_local, gain_moe_local, router_local), BOTH)  103 us
    all_gather x1, waiting for transfers between devices, shards(): lax.all_gather(qkv_weight, 'fsdp', axis=0, tiled=True)  85.9 us
    all_to_all x2, waiting for transfers between devices, to_owner(): lax.all_to_all(whole, 'fsdp', split_axis=0, concat_axis=0, tiled=True)  78.6 us
    dot_general x8, matrix products, t_dot(): lax.dot_general(a, b, (((0,), (0,)), ((), ())), preferred_element_type=f32)  40.7 us
  transfers between devices with their start and end apart: 15, of which 11 were waited for; matrix products, arithmetic and copies ran while one was open for 9% of the time, Pallas kernels for 0%

profile of v1, /device:TPU:0, one launch (start us, length us, event | category | flops | bytes accessed | tf_op | source)
XLA Modules:
  0.0 1291.8 jit_solution(10008504819524817200)
XLA Ops:
  7.9 7.3 all-to-all-start.2
  16.0 78.6 %all-to-all-done.2 = bf16[8,96,1536]{2,1,0:T(8,128)(2,1)} async-done(((bf16[8,96,1536]{2,1,0:T(8,128)(2,1)}), bf16[8,96,1536]{2,1,0:T(8,128)(2,1)}, u32[]{:S(2)}, u32[]{:S(2)}) %all-to-all-start.2) | async-done | bytes 2359328 | tf_op jit(solution)/shard_map/all_to_all | solution.py:93
  94.6 5.6 all-to-all-start.1
  102.4 85.9 %all-gather.3.cloned.1.call-done = bf16[1536,2048]{1,0:T(8,128)(2,1)} async-done(((bf16[192,2048]{1,0:T(8,128)(2,1)}), bf16[1536,2048]{1,0:T(8,128)(2,1)}) %all-gather.3.cloned.1.call-update) | async-done | bytes 6291472 | tf_op jit(solution)/shard_map/all_gather | solution.py:114
  188.4 4.6 convolution_convert_fusion.8
  193.6 3.8 fusion.79
  197.4 2.3 convolution_convert_fusion.10
  199.8 112.2 %all-gather.5.cloned.1.call-done = bf16[1536,1536]{1,0:T(8,128)(2,1)} async-done(((bf16[192,1536]{1,0:T(8,128)(2,1)}), bf16[1536,1536]{1,0:T(8,128)(2,1)}) %all-gather.5.cloned.1.call-update) | async-done | bytes 4718608 | tf_op jit(solution)/shard_map/all_gather | solution.py:115
  312.0 3.9 multiply_reduce_fusion.2
  316.1 3.6 convolution_convert_fusion.4
  319.7 3.6 all-to-all-start
  323.3 4.8 convolution_convert_fusion.2
  328.1 101.6 %all-to-all-done = bf16[32,48,1536]{2,1,0:T(8,128)(2,1)} async-done(((bf16[32,48,1536]{2,1,0:T(8,128)(2,1)}), bf16[32,48,1536]{2,1,0:T(8,128)(2,1)}, u32[]{:S(2)}, u32[]{:S(2)}) %all-to-all-start) | async-done | bytes 4718624 | tf_op jit(solution)/shard_map/all_to_all | solution.py:107
  429.7 3.8 all-to-all-start.4
  433.9 11.1 fusion.80
  445.0 3.7 copy-done.7
  448.7 2.7 multiply_convert_fusion
  451.4 88.5 %all-to-all-done.4 = bf16[32,48,1536]{2,1,0:T(8,128)(2,1)} async-done(((bf16[32,48,1536]{2,1,0:T(8,128)(2,1)}), bf16[32,48,1536]{2,1,0:T(8,128)(2,1)}, u32[]{:S(2)}, u32[]{:S(2)}) %all-to-all-start.4) | async-done | bytes 4718624 | tf_op jit(solution)/shard_map/all_to_all | solution.py:107
  539.9 10.0 fusion.2
  550.6 2.6 all-to-all-start.5
  553.2 7.0 all-to-all-done.5
  561.1 9.1 all_to_all.50
  570.2 3.3 fusion.1
  575.3 9.6 fusion.19
  584.9 13.9 %convolution_convert_fusion.6 = bf16[1536,1536]{1,0:T(8,128)(2,1)} fusion(bf16[1536,1536]{1,0:T(8,128)(2,1)} %bitcast.11, f32[1536,768]{1,0:T(8,128)} %get-tuple-element.20, f32[1536,768]{1,0:T(8,128)S(1)} %get-tuple-element.19), kind=kOutput, calls=%fused_computation.14 | convolution fusion | flops 7254835200 | bytes 18874368 | tf_op jit(solution)/shard_map/dot_general | solution.py:24
  598.9 3.7 all-to-all-start.7
  604.4 104.5 %all-to-all-done.7 = bf16[32,48,1536]{2,1,0:T(8,128)(2,1)} async-done(((bf16[32,48,1536]{2,1,0:T(8,128)(2,1)}), bf16[32,48,1536]{2,1,0:T(8,128)(2,1)}, u32[]{:S(2)}, u32[]{:S(2)}) %all-to-all-start.7) | async-done | bytes 4718624 | tf_op jit(solution)/shard_map/all_to_all | solution.py:107
  709.0 3.8 convolution_bitcast_fusion
  715.5 3.6 convolution_convert_fusion.1
  719.1 3.3 fusion.3
  722.5 5.2 convolution_convert_fusion.7
  727.6 4.4 all-to-all-start.9
  732.0 13.7 %convolution_convert_fusion.5 = bf16[1536,1536]{1,0:T(8,128)(2,1)} fusion(bf16[1536,1536]{1,0:T(8,128)(2,1)} %bitcast.10, f32[1536,768]{1,0:T(8,128)} %get-tuple-element.20, f32[1536,768]{1,0:T(8,128)} %copy-done.39), kind=kOutput, calls=%fused_computation.13 | convolution fusion | flops 7254835200 | bytes 18874368 | tf_op jit(solution)/shard_map/dot_general | solution.py:28
  745.8 70.1 %all-to-all-done.9 = bf16[8,96,1536]{2,1,0:T(8,128)(2,1)} async-done(((bf16[8,96,1536]{2,1,0:T(8,128)(2,1)}), bf16[8,96,1536]{2,1,0:T(8,128)(2,1)}, u32[]{:S(2)}, u32[]{:S(2)}) %all-to-all-start.9) | async-done | bytes 2359328 | tf_op jit(solution)/shard_map/all_to_all | solution.py:98
  815.9 4.6 all-to-all-start.8
  820.7 5.1 convolution_convert_fusion.9
  828.2 2.8 fusion.10
  834.6 4.7 convolution_convert_fusion
  839.2 130.5 %all-to-all-done.8 = bf16[8,192,1536]{2,1,0:T(8,128)(2,1)} async-done(((bf16[8,192,1536]{2,1,0:T(8,128)(2,1)}), bf16[8,192,1536]{2,1,0:T(8,128)(2,1)}, u32[]{:S(2)}, u32[]{:S(2)}) %all-to-all-start.8) | async-done | bytes 4718624 | tf_op jit(solution)/shard_map/all_to_all | solution.py:98
  969.8 3.6 all-to-all-start.3
  973.5 137.7 %reduce-scatter.3.cloned.1.call-done = bf16[192,2048]{1,0:T(8,128)(2,1)} async-done(((bf16[1536,2048]{1,0:T(8,128)(2,1)}), bf16[192,2048]{1,0:T(8,128)(2,1)}) %reduce-scatter.3.cloned.1.call-update) | async-done | bytes 786448 | tf_op jit(solution)/shard_map/reduce_scatter | solution.py:200
  1112.2 4.5 convert_element_type.174
  1116.7 7.7 convert_element_type.171
  1124.3 4.0 convolution_bitcast_fusion.1
  1128.3 4.9 fusion.15
  1137.1 37.9 %all-reduce.2 = (f32[1536]{0:T(1024)}, f32[1536]{0:T(1024)}) all-reduce(f32[1536]{0:T(1024)S(1)} %get-tuple-element.11, f32[1536]{0:T(1024)S(1)} %get-tuple-element.9), channel_id=1, replica_groups=mesh['expert'=4,'fsdp'=8] {'expert','fsdp'}, use_global_device_ids=true, to_apply=%region_15.16 | all-reduce | flops 3072 | bytes 24576 | tf_op jit(solution)/shard_map/psum | solution.py:207
  1175.0 2.5 convert_element_type.167
  1179.6 103.5 %all-reduce.7.cloned.1.call-done = f32[1536,32]{0,1:T(8,128)} async-done(((f32[1536,32]{0,1:T(8,128)}), f32[1536,32]{0,1:T(8,128)}) %all-reduce.7.cloned.1.call-update) | async-done | bytes 196624 | tf_op jit(solution)/shard_map/psum | solution.py:207
  (140 shorter events, 27.6 us)
Async XLA Ops:
  7.2 426.3 %copy-start = (bf16[1536,32]{0,1:T(8,128)(2,1)S(1)}, bf16[1536,32]{0,1:T(8,128)(2,1)}, u32[]{:S(2)}) copy-start(bf16[1536,32]{0,1:T(8,128)(2,1)} %param.16) | copy-start | bytes 294916
  7.2 181.2 %all-gather.3.cloned.1.call-start = ((), (), s32[]{:S(2)}) async-start(), calls=%async_computation.12 | async-start | bytes 7077888 | tf_op jit(solution)/shard_map/all_gather | solution.py:114
  7.9 86.7 %all-to-all-start.2 = ((bf16[8,96,1536]{2,1,0:T(8,128)(2,1)}), bf16[8,96,1536]{2,1,0:T(8,128)(2,1)}, u32[]{:S(2)}, u32[]{:S(2)}) async-start(bf16[8,96,1536]{2,1,0:T(8,128)(2,1)} %param.18), calls=%async_computation.2 | async-start | bytes 4718592 | tf_op jit(solution)/shard_map/all_to_all | solution.py:93
  15.2 296.8 %all-gather.5.cloned.1.call-start = ((), (), s32[]{:S(2)}) async-start(), calls=%async_computation.13 | async-start | bytes 5308416 | tf_op jit(solution)/shard_map/all_gather | solution.py:115
  15.9 84.3 %copy-start.38 = (s32[256,4]{0,1:T(4,128)S(1)}, s32[256,4]{0,1:T(4,128)}, u32[]{:S(2)}) copy-start(s32[256,4]{0,1:T(4,128)} %param.11) | copy-start | bytes 12292
  16.0 86.2 %copy-start.2 = (bf16[256,1536]{1,0:T(8,128)(2,1)S(1)}, bf16[256,1536]{1,0:T(8,128)(2,1)}, u32[]{:S(2)}) copy-start(bf16[256,1536]{1,0:T(8,128)(2,1)} %param.10) | copy-start | bytes 2359300
  16.0 172.4 %copy-start.26 = (f32[1536]{0:T(1024)S(1)}, f32[1536]{0:T(1024)}, u32[]{:S(2)}) copy-start(f32[1536]{0:T(1024)} %param.12) | copy-start | bytes 18436
  94.6 225.1 %all-to-all-start.1 = ((bf16[8,192,1536]{2,1,0:T(8,128)(2,1)}), bf16[8,192,1536]{2,1,0:T(8,128)(2,1)}, u32[]{:S(2)}, u32[]{:S(2)}) async-start(bf16[8,192,1536]{2,1,0:T(8,128)(2,1)} %param.17), calls=%async_computation.1 | async-start | bytes 9437184 | tf_op jit(solution)/shard_map/all_to_all | solution.py:93
  100.5 459.7 %copy-start.22 = (s32[32,256]{1,0:T(8,128)}, s32[32,256]{1,0:T(8,128)S(1)}, u32[]{:S(2)}) copy-start(s32[32,256]{1,0:T(8,128)S(1)} %fusion.36) | copy-start | bytes 98308
  102.4 90.6 %copy-start.34 = (f32[256]{0:T(256)}, f32[256]{0:T(256)S(1)}, u32[]{:S(2)}) copy-start(f32[256]{0:T(256)S(1)} %fusion.27) | copy-start | bytes 3076
  102.4 90.6 %copy-start.29 = (f32[256]{0:T(256)}, f32[256]{0:T(256)S(1)}, u32[]{:S(2)}) copy-start(f32[256]{0:T(256)S(1)} %fusion.68) | copy-start | bytes 3076
  193.3 4.1 copy-start.12
  193.6 6.2 copy-start.18
  197.4 2.4 copy-start.27
  199.8 116.1 %copy-start.5 = (bf16[2,128,6,256]{3,1,2,0:T(8,128)(2,1)}, bf16[2,128,6,256]{3,1,2,0:T(8,128)(2,1)S(1)}, u32[]{:S(2)}) copy-start(bf16[2,128,6,256]{3,1,2,0:T(8,128)(2,1)S(1)} %convolution_convert_fusion.10) | copy-start | bytes 2359300
  312.0 3.9 copy-start.25
  312.0 4.1 copy-start.9
  315.8 3.8 copy-start.36
  315.9 3.8 copy-start.32
  319.7 110.0 %all-to-all-start = ((bf16[32,48,1536]{2,1,0:T(8,128)(2,1)}), bf16[32,48,1536]{2,1,0:T(8,128)(2,1)}, u32[]{:S(2)}, u32[]{:S(2)}) async-start(bf16[32,48,1536]{2,1,0:T(8,128)(2,1)} %bitcast.150), calls=%async_computation | async-start | bytes 9437184 | tf_op jit(solution)/shard_map/all_to_all | solution.py:107
  429.7 110.2 %all-to-all-start.4 = ((bf16[32,48,1536]{2,1,0:T(8,128)(2,1)}), bf16[32,48,1536]{2,1,0:T(8,128)(2,1)}, u32[]{:S(2)}, u32[]{:S(2)}) async-start(bf16[32,48,1536]{2,1,0:T(8,128)(2,1)} %bitcast.149), calls=%async_computation.4 | async-start | bytes 9437184 | tf_op jit(solution)/shard_map/all_to_all | solution.py:107
  445.0 3.7 copy-start.7
  550.6 9.6 all-to-all-start.5
  553.2 8.0 copy-start.20
  570.2 5.1 copy-start.8
  584.9 14.0 %copy-start.39 = (f32[1536,768]{1,0:T(8,128)}, f32[1536,768]{1,0:T(8,128)S(1)}, u32[]{:S(2)}) copy-start(f32[1536,768]{1,0:T(8,128)S(1)} %get-tuple-element.19) | copy-start | bytes 14155780
  598.9 110.1 %copy-start.23 = (s32[32,256]{1,0:T(8,128)S(1)}, s32[32,256]{1,0:T(8,128)}, u32[]{:S(2)}) copy-start(s32[32,256]{1,0:T(8,128)} %copy-done.22) | copy-start | bytes 98308
  598.9 110.1 %all-to-all-start.7 = ((bf16[32,48,1536]{2,1,0:T(8,128)(2,1)}), bf16[32,48,1536]{2,1,0:T(8,128)(2,1)}, u32[]{:S(2)}, u32[]{:S(2)}) async-start(bf16[32,48,1536]{2,1,0:T(8,128)(2,1)} %bitcast.155), calls=%async_computation.7 | async-start | bytes 9437184 | tf_op jit(solution)/shard_map/all_to_all | solution.py:107
  602.6 370.9 %reduce-scatter.5.cloned.1.call-start = ((), (), s32[]{:S(2)}) async-start(), calls=%async_computation.15 | async-start | bytes 5308416 | tf_op jit(solution)/shard_map/reduce_scatter | solution.py:201
  604.4 108.3 %copy-start.33 = (f32[256]{0:T(256)S(1)}, f32[256]{0:T(256)}, u32[]{:S(2)}) copy-start(f32[256]{0:T(256)} %copy-done.32) | copy-start | bytes 3076
  719.1 3.3 copy-start.16
  727.6 88.2 %all-to-all-start.9 = ((bf16[8,96,1536]{2,1,0:T(8,128)(2,1)}), bf16[8,96,1536]{2,1,0:T(8,128)(2,1)}, u32[]{:S(2)}, u32[]{:S(2)}) async-start(bf16[8,96,1536]{2,1,0:T(8,128)(2,1)} %bitcast.161), calls=%async_computation.11 | async-start | bytes 4718592 | tf_op jit(solution)/shard_map/all_to_all | solution.py:98
  815.9 153.9 %all-to-all-start.8 = ((bf16[8,192,1536]{2,1,0:T(8,128)(2,1)}), bf16[8,192,1536]{2,1,0:T(8,128)(2,1)}, u32[]{:S(2)}, u32[]{:S(2)}) async-start(bf16[8,192,1536]{2,1,0:T(8,128)(2,1)} %bitcast.154), calls=%async_computation.10 | async-start | bytes 9437184 | tf_op jit(solution)/shard_map/all_to_all | solution.py:98
  820.5 7.7 copy-start.19
  820.5 7.6 copy-start.28
  820.5 290.6 %reduce-scatter.3.cloned.1.call-start = ((), (), s32[]{:S(2)}) async-start(), calls=%async_computation.14 | async-start | bytes 7077888 | tf_op jit(solution)/shard_map/reduce_scatter | solution.py:200
  828.2 3.1 copy-start.14
  969.8 154.5 %all-to-all-start.3 = ((bf16[32,48,1536]{2,1,0:T(8,128)(2,1)}), bf16[32,48,1536]{2,1,0:T(8,128)(2,1)}, u32[]{:S(2)}, u32[]{:S(2)}) async-start(bf16[32,48,1536]{2,1,0:T(8,128)(2,1)} %bitcast.153), calls=%async_computation.3 | async-start | bytes 9437184 | tf_op jit(solution)/shard_map/all_to_all | solution.py:107
  973.4 201.6 %all-reduce.9.cloned.1.call-start = ((), (), s32[]{:S(2)}) async-start(), calls=%async_computation.17 | async-start | bytes 2752512 | tf_op jit(solution)/shard_map/psum | solution.py:204
  1111.2 171.9 %all-reduce.7.cloned.1.call-start = ((), (), s32[]{:S(2)}) async-start(), calls=%async_computation.16 | async-start | bytes 393216 | tf_op jit(solution)/shard_map/psum | solution.py:207
  1116.7 7.7 copy-start.21
  1116.7 7.7 copy-start.24
  1124.3 8.9 slice-start
  1128.3 4.9 copy-start.11
  1128.3 4.9 slice-start.1
  1133.2 2.2 copy-start.4
  1133.3 2.2 copy-start.31
  1135.5 149.2 %copy-start.1 = (bf16[1536,32]{0,1:T(8,128)(2,1)S(1)}, bf16[1536,32]{0,1:T(8,128)(2,1)}, u32[]{:S(2)}) copy-start(bf16[1536,32]{0,1:T(8,128)(2,1)} %param.16) | copy-start | bytes 294916
  (9 other events, 11.5 us)
Sparse Core Ops, SparseCore 0:
  10.2 178.1 all-gather.2
  190.5 121.3 all-gather.4
  719.3 158.8 reduce-scatter.4
  882.2 228.8 reduce-scatter.2
  1113.5 39.9 all-reduce.8
  1160.3 122.7 all-reduce.6

commit v2 on v1

v2 whole, which is shorter than its diff:
```python
import jax
import jax.numpy as jnp
from jax import lax
from jax.experimental import pallas as pl
from jax.experimental.pallas import tpu as pltpu
from jax.sharding import Mesh
from jax.sharding import PartitionSpec as P

HEADS = 12
KV_HEADS = 2
HEAD_DIM = 128
FFE = 768
EXPERTS = 32
TOP = 4
CAP = 48
EPSILON = 1e-06
VMEM_LIMIT = 56 * 1024 * 1024
EXTRA = 128
EXPERT = ("y", "c")
FSDP = ("h", "r")
BOTH = EXPERT + FSDP
HALF = ("y", "c", "r")
f32 = jnp.float32
bf16 = jnp.bfloat16


def dot(a, b):
    return jnp.dot(a, b, preferred_element_type=f32)


def dot_t(a, b):
    return lax.dot_general(a, b, (((1,), (1,)), ((), ())), preferred_element_type=f32)


def t_dot(a, b):
    return lax.dot_general(a, b, (((0,), (0,)), ((), ())), preferred_element_type=f32)


def rms_apply(values, gain):
    return values * lax.rsqrt(jnp.mean(values * values, axis=-1, keepdims=True) + EPSILON) * gain


def reglu_smooth(projected):
    return jax.nn.gelu(projected[..., :FFE]) * projected[..., FFE:]


def swap(value, axis, bit=1):
    size = lax.axis_size(axis)
    return lax.ppermute(value, axis, [(i, i ^ bit) for i in range(size)])


def sum_over(value, axes):
    for axis in axes:
        bit = 1
        while bit < lax.axis_size(axis):
            value = value + swap(value, axis, bit)
            bit *= 2
    return value


def together(*values):
    return lax.optimization_barrier(values)


def marker_kernel(*refs):
    pass


def mark(values):
    flat, tree = jax.tree.flatten(values)
    anywhere = [pl.BlockSpec(memory_space=pl.ANY)] * len(flat)
    same = pl.pallas_call(
        marker_kernel,
        in_specs=anywhere,
        out_specs=anywhere,
        out_shape=[jax.ShapeDtypeStruct(value.shape, value.dtype) for value in flat],
        input_output_aliases={number: number for number in range(len(flat))},
        cost_estimate=pl.CostEstimate(flops=10**12, bytes_accessed=0, transcendentals=0),
    )(*flat)
    return jax.tree.unflatten(tree, same)


def order_by(index, mine, other, axis):
    size = mine.shape[axis]
    shape = mine.shape[:axis] + (2 * size,) + mine.shape[axis + 1 :]
    start = [0] * mine.ndim
    start[axis] = index * size
    both = lax.dynamic_update_slice(jnp.zeros(shape, mine.dtype), mine, start)
    start[axis] = (1 - index) * size
    return lax.dynamic_update_slice(both, other, start)


def part_of(value, index, axis):
    size = value.shape[axis] // 2
    return lax.dynamic_slice_in_dim(value, index * size, size, axis=axis)


def split_width(width):
    first = (width // 2 + 127) // 128 * 128
    return first, width - first


def fsdp_bits():
    size = lax.axis_size("r")
    bits = [("h", 1, 0)]
    bit = size // 2
    while bit:
        bits.append(("r", bit, len(bits)))
        bit //= 2
    return bits


def bit_index(axis, bit):
    return (lax.axis_index(axis) // bit) % 2


def gather_step(block, step):
    axis, bit, dim = step
    return order_by(bit_index(axis, bit), block, swap(block, axis, bit), dim)


def scatter_step(block, step):
    axis, bit, dim = step
    index = bit_index(axis, bit)
    other = swap(part_of(block, 1 - index, dim).astype(bf16), axis, bit)
    return part_of(block, index, dim).astype(f32) + other.astype(f32)


def gather_shards(shard, first_done):
    steps = fsdp_bits()
    rows, columns = shard.shape
    whole_rows = rows * lax.axis_size(FSDP)
    shape = (1,) * len(steps) + (rows, columns)
    if lax.axis_size("y") != 2:
        block = shard.reshape(shape)
        for step in steps:
            block = gather_step(block, step)
        return first_done(block).reshape(whole_rows, columns)
    lane = len(steps) + 1
    y_step, x_step = ("y", 1, lane), steps[-1]
    block = part_of(shard.reshape(shape), lax.axis_index("y"), lane)
    for step in steps[:-1]:
        block = gather_step(block, step)
    block = first_done(block)
    first, last = jnp.split(block, [split_width(columns // 2)[0]], axis=lane)
    first, last = gather_step(first, x_step), gather_step(last, y_step)
    first, last = gather_step(first, y_step), gather_step(last, x_step)
    parts = [
        piece for pair in zip(jnp.split(first, 2, axis=lane), jnp.split(last, 2, axis=lane)) for piece in pair
    ]
    return jnp.concatenate(parts, axis=lane).reshape(whole_rows, columns)


def scatter_sends(left, right):
    if lax.axis_size("y") != 2:
        return None
    x_step = fsdp_bits()[-1]
    left_of, right_of, right_last = product_parts(left, right)
    y_index, x_index = lax.axis_index("y"), bit_index(*x_step[:2])
    return (
        swap(t_dot(left, right_of(1 - y_index)).astype(bf16), "y"),
        swap(t_dot(left_of(1 - x_index), right_last).astype(bf16), *x_step[:2]),
    )


def product_parts(left, right):
    tokens, whole_rows = left.shape
    columns = right.shape[1]
    rows = whole_rows // lax.axis_size(FSDP)
    width = split_width(columns // 2)[0]
    left_blocks = left.reshape(tokens, -1, 2, rows)
    cube = right.reshape(tokens, 2, columns // 2)
    right_first, right_last = cube[:, :, :width], cube[:, :, width:].reshape(tokens, -1)

    def left_of(index):
        return lax.dynamic_index_in_dim(left_blocks, index, 2, keepdims=False).reshape(tokens, -1)

    def right_of(index):
        return lax.dynamic_index_in_dim(right_first, index, 1, keepdims=False)

    return left_of, right_of, right_last


def scatter_products(pairs, sends, rounds):
    steps = fsdp_bits()
    size = lax.axis_size(FSDP)
    if lax.axis_size("y") != 2:
        blocks = [t_dot(left, right) for left, right in pairs]
        blocks = [block.reshape((2,) * len(steps) + (block.shape[0] // size, -1)) for block in blocks]
        for number, step in enumerate(reversed(steps)):
            blocks = [scatter_step(block, step) for block in blocks]
            if number < 2:
                blocks = rounds[number](blocks)
        blocks = rounds[2](blocks)
        blocks = [block.astype(bf16).reshape(block.shape[-2:]) for block in blocks]
        return [sum_over(block, ("y",)).astype(bf16) for block in blocks]
    lane = len(steps) + 1
    y_step, x_step = ("y", 1, lane), steps[-1]
    y_index, x_index = lax.axis_index("y"), bit_index(*x_step[:2])
    firsts, lasts = [], []
    for (left, right), (first_sent, last_sent) in zip(pairs, sends):
        left_of, right_of, right_last = product_parts(left, right)
        rows = left.shape[1] // size
        first = t_dot(left, right_of(y_index)) + first_sent.astype(f32)
        last = t_dot(left_of(x_index), right_last) + last_sent.astype(f32)
        firsts.append(first.reshape((2,) * len(steps) + (rows, -1)))
        lasts.append(last.reshape((2,) * (len(steps) - 1) + (1, rows, 2, last.shape[1] // 2)))
    widths = [block.shape[-1] for block in firsts + lasts]
    first = jnp.concatenate(firsts, axis=lane)
    last = jnp.concatenate(lasts, axis=lane + 1)
    last = last.reshape(last.shape[:lane] + (-1,))
    first, last = rounds[0]((first, last))
    first, last = scatter_step(first, x_step), scatter_step(last, y_step)
    block = rounds[1](jnp.concatenate([first, last], axis=lane))
    for step in reversed(steps[:-1]):
        block = scatter_step(block, step)
    block = rounds[2](block).astype(bf16).reshape(block.shape[-2:])
    cuts = [sum(widths[: number + 1]) for number in range(len(widths) - 1)]
    halves = [jnp.split(half, cuts, axis=1) for half in jnp.split(order_by(y_index, block, swap(block, "y"), 1), 2, axis=1)]
    count = len(pairs)
    return [
        jnp.concatenate([half[number + part] for half in halves for part in (0, count)], axis=1)
        for number in range(count)
    ]


def head_probs(query, key):
    seq_len = query.shape[0]
    scores = dot_t(query, key) * HEAD_DIM ** (-0.5)
    rows = lax.broadcasted_iota(jnp.int32, (seq_len, seq_len), 0)
    columns = lax.broadcasted_iota(jnp.int32, (seq_len, seq_len), 1)
    scores = jnp.where(rows >= columns, scores, -1e30)
    exponent = jnp.exp(scores - jnp.max(scores, axis=-1, keepdims=True))
    return exponent / jnp.sum(exponent, axis=-1, keepdims=True)


def attend_kernel(xn_ref, weight_ref, joint_ref, attended_ref):
    joint = dot(xn_ref[...], weight_ref[...]).astype(bf16)
    joint_ref[...] = joint
    width = HEADS // 2 * HEAD_DIM
    key, value = joint[:, width : width + HEAD_DIM], joint[:, width + HEAD_DIM :]
    for head in range(HEADS // 2):
        columns = slice(head * HEAD_DIM, (head + 1) * HEAD_DIM)
        probs = head_probs(joint[:, columns], key).astype(bf16)
        attended_ref[:, columns] = dot(probs, value).astype(bf16)


def attend(xn_pair, weight, seq_len):
    rows, model_width = xn_pair.shape
    width = weight.shape[1]
    query_width = HEADS // 2 * HEAD_DIM
    return pl.pallas_call(
        attend_kernel,
        grid=(rows // seq_len,),
        in_specs=[
            pl.BlockSpec((seq_len, model_width), lambda i: (i, 0)),
            pl.BlockSpec((model_width, width), lambda i: (0, 0)),
        ],
        out_specs=[
            pl.BlockSpec((seq_len, width), lambda i: (i, 0)),
            pl.BlockSpec((seq_len, query_width), lambda i: (i, 0)),
        ],
        out_shape=[
            jax.ShapeDtypeStruct((rows, width), bf16),
            jax.ShapeDtypeStruct((rows, query_width), bf16),
        ],
        compiler_params=pltpu.CompilerParams(vmem_limit_bytes=VMEM_LIMIT),
        cost_estimate=pl.CostEstimate(flops=0, bytes_accessed=0, transcendentals=0),
    )(xn_pair, weight)


def attend_backward_kernel(joint_ref, grad_ref, weight_ref, grad_joint_ref, grad_xn_ref):
    scale = HEAD_DIM ** (-0.5)
    width = HEADS // 2 * HEAD_DIM
    joint = joint_ref[...]
    grad = grad_ref[...]
    key, value = joint[:, width : width + HEAD_DIM], joint[:, width + HEAD_DIM :]
    grad_key = jnp.zeros(key.shape, f32)
    grad_value = jnp.zeros(value.shape, f32)
    for head in range(HEADS // 2):
        columns = slice(head * HEAD_DIM, (head + 1) * HEAD_DIM)
        query, grad_head = joint[:, columns], grad[:, columns]
        probs = head_probs(query, key)
        grad_probs = dot_t(grad_head, value)
        delta = jnp.sum(probs * grad_probs, axis=-1, keepdims=True)
        grad_scores = (probs * (grad_probs - delta)).astype(bf16)
        grad_joint_ref[:, columns] = (dot(grad_scores, key) * scale).astype(bf16)
        grad_key = grad_key + t_dot(grad_scores, query)
        grad_value = grad_value + t_dot(probs.astype(bf16), grad_head)
    grad_joint_ref[:, width : width + HEAD_DIM] = (grad_key * scale).astype(bf16)
    grad_joint_ref[:, width + HEAD_DIM :] = grad_value.astype(bf16)
    grad_xn_ref[...] = dot_t(grad_joint_ref[...], weight_ref[...])


def attend_backward(joint, grad_attended, weight, seq_len):
    rows, width = joint.shape
    model_width = weight.shape[0]
    query_width = HEADS // 2 * HEAD_DIM
    return pl.pallas_call(
        attend_backward_kernel,
        grid=(rows // seq_len,),
        in_specs=[
            pl.BlockSpec((seq_len, width), lambda i: (i, 0)),
            pl.BlockSpec((seq_len, query_width), lambda i: (i, 0)),
            pl.BlockSpec((model_width, width), lambda i: (0, 0)),
        ],
        out_specs=[
            pl.BlockSpec((seq_len, width), lambda i: (i, 0)),
            pl.BlockSpec((seq_len, model_width), lambda i: (i, 0)),
        ],
        out_shape=[
            jax.ShapeDtypeStruct((rows, width), bf16),
            jax.ShapeDtypeStruct((rows, model_width), f32),
        ],
        compiler_params=pltpu.CompilerParams(vmem_limit_bytes=VMEM_LIMIT),
        cost_estimate=pl.CostEstimate(flops=0, bytes_accessed=0, transcendentals=0),
    )(joint, grad_attended, weight)


def expert_kernel(
    expert_ref,
    rows_ref,
    grad_ref,
    router_ref,
    up_ref,
    down_ref,
    inner_ref,
    out_ref,
    d_out_ref,
    d_projected_ref,
    d_in_ref,
):
    rows = rows_ref[...]
    width = rows.shape[1]
    mask = grad_ref[:, width : width + EXPERTS] > 0
    logits = jnp.where(mask, dot(rows, router_ref[...]), -1e30)
    exponent = jnp.where(mask, jnp.exp(logits - jnp.max(logits, axis=-1, keepdims=True)), 0.0)
    total = jnp.sum(exponent, axis=-1, keepdims=True)
    mine = lax.broadcasted_iota(jnp.int32, exponent.shape, 1) == expert_ref[0]
    gate = jnp.sum(jnp.where(mine, exponent, 0.0), axis=-1, keepdims=True)
    gate = gate / jnp.where(total > 0, total, 1.0)

    projected = dot(rows, up_ref[...])
    lower, upper = projected[:, :FFE], projected[:, FFE:]
    slope = (2.0 / 3.141592653589793) ** 0.5
    bend = jnp.tanh(slope * (lower + 0.044715 * lower * lower * lower))
    gelu = 0.5 * lower * (1.0 + bend)
    gelu_grad = 0.5 * (1.0 + bend) + 0.5 * lower * (1.0 - bend * bend) * slope * (
        1.0 + 3 * 0.044715 * lower * lower
    )
    inner = (gelu * upper).astype(bf16)
    inner_ref[...] = inner
    out = dot(inner, down_ref[...]).astype(bf16)
    out_ref[...] = out
    grad = grad_ref[:, :width].astype(f32)
    d_gate = jnp.sum(out.astype(f32) * grad, axis=-1, keepdims=True)
    d_gate_high = d_gate.astype(bf16).astype(f32)
    column = lax.broadcasted_iota(jnp.int32, (rows.shape[0], EXTRA), 1)
    d_in_ref[:, width:] = jnp.where(
        column == expert_ref[1],
        d_gate_high,
        jnp.where(column == expert_ref[1] + EXPERTS // 2, d_gate - d_gate_high, 0.0),
    ).astype(bf16)
    d_out = (gate * grad).astype(bf16)
    d_out_ref[...] = d_out
    d_inner = dot_t(d_out, down_ref[...])
    d_projected_ref[:, :FFE] = (d_inner * upper * gelu_grad).astype(bf16)
    d_projected_ref[:, FFE:] = (d_inner * gelu).astype(bf16)
    d_in_ref[:, :width] = dot_t(d_projected_ref[...], up_ref[...]).astype(bf16)


def expert_part(expert, received, grad_rows, router, up, down):
    rows, model_width = received.shape
    block = 256

    def row_block(width):
        return pl.BlockSpec((block, width), lambda i, *_: (i, 0))

    def whole(array):
        return pl.BlockSpec(array.shape, lambda i, *_: (0, 0))

    widths = (FFE, model_width, model_width, 2 * FFE, model_width + EXTRA)
    return pl.pallas_call(
        expert_kernel,
        grid_spec=pltpu.PrefetchScalarGridSpec(
            num_scalar_prefetch=1,
            grid=(rows // block,),
            in_specs=[
                row_block(model_width),
                row_block(model_width + EXTRA),
                whole(router),
                whole(up),
                whole(down),
            ],
            out_specs=[row_block(width) for width in widths],
        ),
        out_shape=[jax.ShapeDtypeStruct((rows, width), bf16) for width in widths],
        compiler_params=pltpu.CompilerParams(vmem_limit_bytes=VMEM_LIMIT),
        cost_estimate=pl.CostEstimate(flops=0, bytes_accessed=0, transcendentals=0),
    )(expert, received, grad_rows, router, up, down)


def expert_weights_kernel(x_own, x_far, p_own, p_far, i_own, i_far, d_own, d_far, up_ref, down_ref):
    up_ref[...] = (t_dot(x_own[...], p_own[...]) + t_dot(x_far[...], p_far[...])).astype(bf16)
    down_ref[...] = (t_dot(i_own[...], d_own[...]) + t_dot(i_far[...], d_far[...])).astype(bf16)


def expert_weights(received, d_projected, inner, d_out):
    rows, model_width = received[0].shape
    steps = 3

    def columns(array):
        return pl.BlockSpec((rows, array.shape[1] // steps), lambda i: (0, i))

    def whole(array):
        return pl.BlockSpec(array.shape, lambda i: (0, 0))

    return pl.pallas_call(
        expert_weights_kernel,
        grid=(steps,),
        in_specs=[columns(a) for a in received]
        + [whole(a) for a in d_projected]
        + [columns(a) for a in inner]
        + [whole(a) for a in d_out],
        out_specs=[
            pl.BlockSpec((model_width // steps, 2 * FFE), lambda i: (i, 0)),
            pl.BlockSpec((FFE // steps, model_width), lambda i: (i, 0)),
        ],
        out_shape=[
            jax.ShapeDtypeStruct((model_width, 2 * FFE), bf16),
            jax.ShapeDtypeStruct((FFE, model_width), bf16),
        ],
        compiler_params=pltpu.CompilerParams(vmem_limit_bytes=VMEM_LIMIT),
        cost_estimate=pl.CostEstimate(flops=0, bytes_accessed=0, transcendentals=0),
    )(*received, *d_projected, *inner, *d_out)


def shards(
    tokens,
    routes,
    norm_attn,
    qkv_weight,
    out_weight,
    norm_moe,
    router_weight,
    gate_up,
    down,
    grad_output,
):
    seq_len, model_width = tokens.shape
    query_half = HEADS * HEAD_DIM // 2
    kv_half = KV_HEADS * HEAD_DIM // 2
    out_half = out_weight.shape[1] // 2
    groups = lax.axis_size(EXPERT)
    fsdp = lax.axis_size(FSDP)
    half_devices = groups * fsdp // 2
    local_count = gate_up.shape[0]
    parts = fsdp // local_count
    half_experts = EXPERTS // 2
    rows = half_experts * CAP
    core = lax.axis_index("c")
    half = lax.axis_index("h")
    me = lax.axis_index(FSDP)
    group = lax.axis_index(EXPERT)
    my_expert = jnp.stack(
        [
            group * local_count + me // parts,
            group * (local_count // 2) + me // parts - half * (local_count // 2),
        ]
    ).astype(jnp.int32)

    def fsdp_partner(value, bit):
        return lax.ppermute(value, FSDP, [(i, i ^ bit) for i in range(fsdp)])

    box = {}

    def tie(value, *names):
        value, held = together(value, [box[name] for name in names])
        box.update(zip(names, held))
        return value

    up_width, down_width = gate_up.shape[1], down.shape[1]
    even, odd = [list(range(fsdp // 2 + first, fsdp, 2)) for first in range(2)]
    middle = len(even) // 2
    turns = [even[:middle], even[middle:], odd[:middle], odd[middle:]]
    near = [list(range(1, fsdp // 2))[turn::3] for turn in range(3)]

    def fetch(bits, *names):
        for bit in bits:
            expert = (me ^ bit) // parts
            piece = jnp.concatenate(
                [
                    lax.dynamic_index_in_dim(gate_up, expert, 0, keepdims=False),
                    lax.dynamic_index_in_dim(down, expert, 0, keepdims=False),
                ],
                axis=0,
            )
            box["in", bit] = fsdp_partner(tie(piece, *names), bit) if bit else piece

    def coming(bits):
        return [("in", bit) for bit in bits]

    def assemble():
        up_full = jnp.zeros((fsdp * up_width, gate_up.shape[2]), gate_up.dtype)
        down_full = jnp.zeros((fsdp * down_width, down.shape[2]), down.dtype)
        for bit in [0] + near[1] + turns[0] + near[0] + turns[1] + turns[2] + turns[3] + near[2]:
            other, piece = me ^ bit, box["in", bit]
            up_full = lax.dynamic_update_slice(up_full, piece[:up_width], (other * up_width, 0))
            down_full = lax.dynamic_update_slice(down_full, piece[up_width:], (other * down_width, 0))
        return up_full, down_full

    columns = fsdp // 4
    stay = [(0, 0)]
    same = [(1, 0), (3, 0), (2, 0)]
    across = [(step, cross) for cross in range(1, columns) for step in (1, 3)]
    opposite = [(2, cross) for cross in range(1, columns)]
    level = [(0, cross) for cross in range(1, columns)]

    def target(index, move, sign=1):
        step, cross = move
        return (index // columns + sign * step + 4) % 4 * columns + (index % columns ^ cross)

    def give(moves, up_grad, down_grad, *names):
        for move in moves:
            to = target(me, move)
            piece = jnp.concatenate(
                [
                    lax.dynamic_slice_in_dim(up_grad, to * up_width, up_width, axis=0),
                    lax.dynamic_slice_in_dim(down_grad, to * down_width, down_width, axis=0),
                ],
                axis=0,
            )
            if move != (0, 0):
                piece = lax.ppermute(tie(piece, *names), FSDP, [(i, target(i, move)) for i in range(fsdp)])
            box["out", move] = piece

    def going(moves):
        return [("out", move) for move in moves]

    def collect():
        up_sum = jnp.zeros(gate_up.shape, f32)
        down_sum = jnp.zeros(down.shape, f32)
        for move in stay + same + opposite + across + level:
            expert = target(me, move, -1) // parts
            piece = box["out", move].astype(f32)[None]
            up_part, down_part = piece[:, :up_width], piece[:, up_width:]
            if parts > 1:
                up_part = up_part + lax.dynamic_slice_in_dim(up_sum, expert, 1, axis=0)
                down_part = down_part + lax.dynamic_slice_in_dim(down_sum, expert, 1, axis=0)
            up_sum = lax.dynamic_update_slice(up_sum, up_part, (expert, 0, 0))
            down_sum = lax.dynamic_update_slice(down_sum, down_part, (expert, 0, 0))
        return up_sum, down_sum

    def exchange(buffer):
        shape = buffer.shape
        return lax.all_to_all(
            buffer.reshape((half_devices, rows // half_devices) + shape[1:]),
            HALF,
            split_axis=0,
            concat_axis=0,
            tiled=True,
        ).reshape(shape)

    def half_columns(table, index):
        cube = table.reshape(table.shape[0], groups, 2, local_count // 2)
        return lax.dynamic_index_in_dim(cube, index, 2, keepdims=False).reshape(table.shape[0], half_experts)

    def both_columns(mine, other):
        shape = (mine.shape[0], groups, 1, local_count // 2)
        return order_by(half, mine.reshape(shape), other.reshape(shape), 2).reshape(-1, EXPERTS)

    token_f = tokens.astype(f32)
    grad_f = grad_output.astype(f32)

    qkv_mine = jnp.concatenate(
        [
            lax.dynamic_slice_in_dim(qkv_weight, core * query_half, query_half, axis=1),
            lax.dynamic_slice_in_dim(qkv_weight, 2 * query_half + core * kv_half, kv_half, axis=1),
            lax.dynamic_slice_in_dim(qkv_weight, 2 * query_half + (2 + core) * kv_half, kv_half, axis=1),
        ],
        axis=1,
    )
    out_mine = lax.dynamic_slice_in_dim(out_weight, core * out_half, out_half, axis=1)
    expert_ids = jnp.arange(EXPERTS, dtype=jnp.int32)
    order = jnp.arange(seq_len)
    earlier = (order[None, :] < order[:, None]).astype(bf16)

    def placing(routing):
        mask = jnp.any(routing[:, :, None] == expert_ids[None, None, :], axis=1)
        position = dot(earlier, mask.astype(bf16)).astype(jnp.int32)
        slot = half_columns(jnp.where(mask, position, -1), half).T
        place = slot[:, None, :] == jnp.arange(CAP, dtype=jnp.int32)[None, :, None]
        return mask, place

    mask_own, cube_own = placing(routes)
    mask_far, cube_far = placing(swap(routes, "h"))
    place_own = cube_own.astype(bf16).reshape(rows, seq_len)
    place_far = cube_far.astype(bf16).reshape(rows, seq_len)

    def first_done(block):
        nonlocal gate_up, down
        sent, block, gate_up, down = together(grad_output, block, gate_up, down)
        box["grad_far"] = swap(sent, "h")
        fetch(near[1] + turns[0])
        return mark(block)

    def send_rows(place, grad, mask):
        extra = jnp.pad(mask.astype(bf16), ((0, 0), (0, EXTRA - EXPERTS)))
        return dot(place, jnp.concatenate([grad, extra], axis=1)).astype(bf16)

    xn_first_f, norm_first_pull = jax.vjp(rms_apply, token_f, norm_attn)
    xn_first = xn_first_f.astype(bf16)
    xn_pair = jnp.concatenate([xn_first, swap(xn_first, "c")], axis=0)
    shard = jnp.concatenate([qkv_mine, out_mine], axis=1)
    core_weights, xn_pair, own_sent = tie(
        (gather_shards(shard, first_done), xn_pair, send_rows(place_own, grad_output, mask_own)),
        "grad_far",
        *coming(turns[0] + near[1]),
    )
    box["grad_rows_own"] = exchange(own_sent)
    fetch(turns[1] + near[0], *coming(turns[0]))
    xn_pair = mark(xn_pair)
    qkv_width = query_half + 2 * kv_half
    qkv_core, out_core = core_weights[:, :qkv_width], core_weights[:, qkv_width:]

    joint, attended_mine = attend(xn_pair, qkv_core, seq_len)
    out_full = order_by(core, out_core, swap(out_core, "c"), 1)
    attended_mine = attended_mine.reshape(2, seq_len, query_half)
    far_sent = send_rows(place_far, box["grad_far"], mask_far)
    attended_mine, far_sent = tie((attended_mine, far_sent), "grad_rows_own", *coming(turns[1] + near[0]))
    box["grad_rows_far"] = exchange(far_sent)
    fetch(turns[2], *coming(turns[1]))
    attended_mine = mark(attended_mine)
    attended_other = swap(attended_mine, "c")
    attended = order_by(core, attended_mine[0], attended_other[1], 1)
    attended_next = order_by(core, attended_mine[1], attended_other[0], 1)
    hidden = token_f + dot(attended, out_full)
    xn_second_f, norm_second_pull = jax.vjp(rms_apply, hidden, norm_moe)
    xn_second = xn_second_f.astype(bf16)

    def gating(values_b, mask):
        logits = dot(values_b, router_weight)
        top = jnp.max(jnp.where(mask, logits, -1e30), axis=-1, keepdims=True)
        exponent = jnp.where(mask, jnp.exp(jnp.where(mask, logits - top, 0.0)), 0.0)
        total = jnp.sum(exponent, axis=-1, keepdims=True)
        return exponent / jnp.where(total > 0, total, 1.0)

    own_sent, xn_sent = tie(
        (dot(place_own, xn_second).astype(bf16), xn_second), "grad_rows_far", *coming(turns[2])
    )
    fetch(turns[3], *coming(turns[2]))
    box["received_own"] = exchange(mark(own_sent))
    fetch([0])
    box["in", 0] = mark(tie(box["in", 0], *coming(turns[2])))
    xn_sent = tie(xn_sent, "received_own", *coming(turns[3]))
    box["xn_far"] = swap(xn_sent, "h")
    fetch(near[2], *coming(turns[3]))
    far_sent = tie(dot(place_far, box["xn_far"]).astype(bf16), *coming(near[2]))
    box["received_far"] = exchange(far_sent)
    gate_up_full, down_full = assemble()
    box["own"] = expert_part(
        my_expert, box["received_own"], box["grad_rows_own"], router_weight, gate_up_full, down_full
    )
    xn_far = box["xn_far"]
    gates = gating(xn_second, mask_own)
    gates_far = gating(xn_far, mask_far)

    box["back_in_own"] = exchange(tie(box["own"][4], "received_far"))
    box["far"] = expert_part(
        my_expert, box["received_far"], box["grad_rows_far"], router_weight, gate_up_full, down_full
    )
    box["back_in_far"] = exchange(tie(box["far"][4], "back_in_own"))
    box["d_in_sum_far"] = swap(t_dot(place_far, box["back_in_far"]).astype(bf16), "h")
    received, d_projected, inner, d_out = [
        list(pair)
        for pair in zip(
            (box["received_own"], box["own"][3], box["own"][0], box["own"][2]),
            (box["received_far"], box["far"][3], box["far"][0], box["far"][2]),
        )
    ]
    up_grad, down_grad = expert_weights(received, d_projected, inner, d_out)
    give(stay, up_grad, down_grad)

    d_in_sum = t_dot(place_own, box["back_in_own"])

    def gate_columns(wide):
        high = wide[:, model_width : model_width + half_experts]
        low = wide[:, model_width + half_experts : model_width + 2 * half_experts]
        return high.astype(f32) + low.astype(f32)

    d_in_sum_far = box["d_in_sum_far"]
    d_gates = both_columns(gate_columns(d_in_sum), gate_columns(d_in_sum_far))
    d_in_sum = d_in_sum[:, :model_width] + d_in_sum_far[:, :model_width].astype(f32)
    d_chosen = gates * (d_gates - jnp.sum(gates * d_gates, axis=-1, keepdims=True))
    d_logits = d_chosen.astype(bf16)
    router_local = t_dot(d_logits, xn_second)
    d_xn_second = dot_t(d_logits, router_weight) + d_in_sum

    def mix(cube, gate, back):
        spread = jnp.where(cube, half_columns(gate, half).T[:, None, :], 0.0).reshape(rows, seq_len)
        high = spread.astype(bf16)
        low = (spread - high.astype(f32)).astype(bf16)
        return t_dot(high, back) + t_dot(low, back)

    d_hidden_norm, gain_moe_local = norm_second_pull(d_xn_second)
    d_hidden = grad_f + d_hidden_norm
    d_hidden_b = d_hidden.astype(bf16)
    d_hidden_b, out_far = together(d_hidden_b, box["far"][1])
    box["back_out_far"] = exchange(out_far)
    d_hidden_b, up_grad, down_grad = together(d_hidden_b, up_grad, down_grad)
    give(same, up_grad, down_grad)
    d_attended = dot_t(d_hidden_b, out_full).astype(bf16)

    def halves(value):
        first, last = jnp.split(value, 2, axis=1)
        return jnp.where(core == 0, first, last), jnp.where(core == 0, last, first)

    d_att_mine, d_att_send = halves(d_attended)
    grad_heads = jnp.stack([d_att_mine, swap(d_att_send, "c")]).reshape(2 * seq_len, query_half)
    d_hid_mine, d_hid_send = halves(d_hidden_b)
    d_hid_next = swap(d_hid_send, "c")
    out_pair = (
        jnp.concatenate([attended, attended_next], axis=0),
        jnp.concatenate([d_hid_mine, d_hid_next], axis=0),
    )
    out_sends = scatter_sends(*out_pair)
    grad_heads = mark(grad_heads)
    grad_joint, d_xn_pair = attend_backward(joint, grad_heads, qkv_core, seq_len)
    grad_joint, out_sends, out_own = tie((grad_joint, out_sends, box["own"][1]), "back_out_far")
    box["back_out_own"] = exchange(out_own)
    moe_sent = mix(cube_far, gates_far, box["back_out_far"]).astype(bf16)

    def first_round(blocks):
        blocks, sent = tie((blocks, moe_sent), "small", "back_out_own", *going(same))
        box["moe_far"] = swap(sent, "h")
        give(opposite, up_grad, down_grad, *going(same))
        box["small"] = sum_over(box["small"], ("c", "y", "r"))
        return mark(blocks)

    def second_round(blocks):
        blocks = tie(blocks, "small", "moe_far", *going(opposite))
        give(across + level, up_grad, down_grad, *going(opposite))
        box["small"] = sum_over(box["small"], ("h",))
        return mark(blocks)

    def third_round(blocks):
        return tie(blocks, "small", *going(across + level))

    d_xn_first = d_xn_pair[:seq_len] + swap(d_xn_pair[seq_len:], "c")
    d_token_norm, gain_attn_local = norm_first_pull(d_xn_first)
    grad_tokens = d_hidden + d_token_norm

    box["small"] = jnp.concatenate([router_local, gain_moe_local[None], gain_attn_local[None]], axis=0)
    qkv_grad, out_grad = scatter_products(
        ((xn_pair, grad_joint), out_pair),
        (scatter_sends(xn_pair, grad_joint), out_sends),
        (first_round, second_round, third_round),
    )
    moe_own = mix(cube_own, gates, box["back_out_own"])
    small = box["small"]
    mixed = (hidden + (moe_own + box["moe_far"].astype(f32))).astype(bf16)
    grad_gate_up, grad_down = collect()
    grad_out_proj = order_by(core, out_grad.astype(f32), swap(out_grad, "c").astype(f32), 1)
    qkv_grad_other = swap(qkv_grad, "c")
    first = jnp.where(core == 0, qkv_grad, qkv_grad_other).astype(f32)
    last = jnp.where(core == 0, qkv_grad_other, qkv_grad).astype(f32)
    cut = (query_half, query_half + kv_half)
    grad_qkv = jnp.concatenate(
        [piece for pair in zip(jnp.split(first, cut, axis=1), jnp.split(last, cut, axis=1)) for piece in pair],
        axis=1,
    )

    return (
        mixed,
        grad_tokens,
        small[EXPERTS + 1],
        grad_qkv,
        grad_out_proj,
        small[EXPERTS],
        small[:EXPERTS].T,
        grad_gate_up,
        grad_down,
    )


def solution(mesh):
    expert, fsdp = mesh.devices.shape
    fine = Mesh(mesh.devices.reshape(expert // 2, 2, 2, fsdp // 2), BOTH)
    in_specs = (
        P(BOTH, None),
        P(BOTH, None),
        P(),
        P(FSDP, None),
        P(FSDP, None),
        P(),
        P(),
        P(EXPERT, FSDP, None),
        P(EXPERT, FSDP, None),
        P(BOTH, None),
    )
    out_specs = (
        P(BOTH, None),
        P(BOTH, None),
        P(),
        P(FSDP, None),
        P(FSDP, None),
        P(),
        P(),
        P(EXPERT, FSDP, None),
        P(EXPERT, FSDP, None),
    )
    return jax.shard_map(shards, mesh=fine, in_specs=in_specs, out_specs=out_specs, check_vma=False)
```

time: 1300 us -> 835 us (0.64)
  waiting for transfers between devices: 1020 us -> 393 us
  local copies, waits for them, and re-layouts: 14.2 us -> 135 us
  Pallas kernels: 0 us -> 73.8 us
  starting transfers between devices: 40 us -> 113 us
  matrix products: 121 us -> 55.1 us
  blocking collectives: 47 us -> 0 us
  other arithmetic: 32.7 us -> 51 us
    all_to_all x9 -> x8, waiting for transfers between devices: 581 us -> 16.9 us  [exchange(): lax.all_to_all(buffer.reshape((half_devices, rows // half_devices) + shap...]
    ppermute x0 -> x47, waiting for transfers between devices: none -> 376 us  [the longest x33 246 us: swap(): return lax.ppermute(value, axis, [(i, i ^ bit) for i in range(size)])]
    all_gather x2 -> x0, waiting for transfers between devices: 198 us -> none  [the longest x1 112 us: shards(): lax.all_gather(out_weight, 'fsdp', axis=0, tiled=True)]
    reduce_scatter x2 -> x0, waiting for transfers between devices: 138 us -> none  [the longest x1 138 us: shards(): lax.psum_scatter(qkv_local.astype(bf16), 'fsdp', scatter_dimension=0, til...]
    psum x2 -> x0, waiting for transfers between devices: 103 us -> none  [the longest x1 103 us: shards(): lax.psum((gain_attn_local, gain_moe_local, router_local), BOTH)]
    ppermute x0 -> x47, starting transfers between devices: none -> 76.2 us  [the longest x33 48 us: swap(): return lax.ppermute(value, axis, [(i, i ^ bit) for i in range(size)])]
    pallas_call x0 -> x13, Pallas kernels: none -> 73.8 us  [the longest x2 37.6 us: expert_part(): pl.pallas_call(expert_kernel, grid_spec=pltpu.PrefetchScalarGridSpec(num_...]
    dynamic_update_slice x0 -> x49, local copies, waits for them, and re-layouts: none -> 43.5 us  [the longest x8 13.2 us: assemble(): lax.dynamic_update_slice(up_full, piece[:up_width], (other * up_width, 0))]
  transfers between devices with their start and end apart: 15 -> 55, of which waited for: 11 -> 28; matrix products, arithmetic and copies ran while one was open for 9% -> 25% of each run, Pallas kernels for 0% -> 9%
where the time goes in v2:
time: 835 us; the launch traced here: 824 us
  waiting for transfers between devices  393 us (47%)
  local copies, waits for them, and re-layouts  135 us (16%)
  starting transfers between devices  113 us (14%)
  Pallas kernels  73.8 us (9%)
  matrix products  55.1 us (7%)
  other arithmetic  51 us (6%)
    ppermute x33, waiting for transfers between devices, swap(): return lax.ppermute(value, axis, [(i, i ^ bit) for i in range(size)])  246 us
    ppermute x7, waiting for transfers between devices, fsdp_partner(): return lax.ppermute(value, FSDP, [(i, i ^ bit) for i in range(fsdp)])  127 us
    ppermute x33, starting transfers between devices, swap(): return lax.ppermute(value, axis, [(i, i ^ bit) for i in range(size)])  48 us
    pallas_call x2, Pallas kernels, expert_part(): pl.pallas_call(expert_kernel, grid_spec=pltpu.PrefetchScalarGridSpec(num_...  37.6 us
    all_to_all x8, starting transfers between devices, exchange(): lax.all_to_all(buffer.reshape((half_devices, rows // half_devices) + shap...  37.1 us
    dot_general x15, matrix products, t_dot(): lax.dot_general(a, b, (((0,), (0,)), ((), ())), preferred_element_type=f32)  34.5 us
    pallas_call x1, Pallas kernels, expert_weights(): pl.pallas_call(expert_weights_kernel, grid=(steps,), in_specs=[columns(a)...  17.3 us
    all_to_all x8, waiting for transfers between devices, exchange(): lax.all_to_all(buffer.reshape((half_devices, rows // half_devices) + shap...  16.9 us
  transfers between devices with their start and end apart: 55, of which 28 were waited for; matrix products, arithmetic and copies ran while one was open for 25% of the time, Pallas kernels for 9%

profile of v2, /device:TPU:0, one launch (start us, length us, event | category | flops | bytes accessed | tf_op | source)
XLA Modules:
  0.0 824.3 jit_solution(16817530506136660764)
XLA Ops:
  3.1 4.1 collective-permute-start
  10.0 12.8 %collective-permute-done.10 = s32[256,4]{0,1:T(4,128)S(1)} collective-permute-done((s32[256,4]{0,1:T(4,128)S(1)}, s32[256,4]{0,1:T(4,128)S(1)}, u32[]{:S(2)}, u32[]{:S(2)}) %collective-permute-start.10) | collective-permute-done | bytes 4128 | tf_op jit(solution)/shard_map/ppermute | solution.py:49
  30.7 9.2 %collective-permute-done.1 = bf16[2,1,1,192,896]{4,3,2,1,0:T(8,128)(2,1)S(1)} collective-permute-done((bf16[2,1,1,192,896]{4,3,2,1,0:T(8,128)(2,1)S(1)}, bf16[2,1,1,192,896]{4,3,2,1,0:T(8,128)(2,1)S(1)}, u32[]{:S(2)}, u32[]{:S(2)}) %collective-permute-start.1) | collective-permute-done | bytes 688160 | tf_op jit(solution)/shard_map/ppermute | solution.py:49
  57.5 7.1 collective-permute-done.2
  70.4 16.5 %collective-permute-done.5 = bf16[2,2,1,192,768]{4,3,2,1,0:T(8,128)(2,1)S(1)} collective-permute-done((bf16[2,2,1,192,768]{4,3,2,1,0:T(8,128)(2,1)S(1)}, bf16[2,2,1,192,768]{4,3,2,1,0:T(8,128)(2,1)S(1)}, u32[]{:S(2)}, u32[]{:S(2)}) %collective-permute-start.5) | collective-permute-done | bytes 1179680 | tf_op jit(solution)/shard_map/ppermute | solution.py:49
  87.5 7.8 collective-permute-done.3
  98.6 3.8 collective-permute-done.7
  102.5 17.9 %collective-permute-done.8 = bf16[288,1536]{1,0:T(8,128)(2,1)S(1)} collective-permute-done((bf16[288,1536]{1,0:T(8,128)(2,1)S(1)}, bf16[288,1536]{1,0:T(8,128)(2,1)S(1)}, u32[]{:S(2)}, u32[]{:S(2)}) %collective-permute-start.8) | collective-permute-done | bytes 884768 | tf_op jit(solution)/shard_map/ppermute | solution.py:473
  122.2 4.5 all-to-all-start
  130.7 3.9 slice.171.weight_ref
  137.1 4.2 fusion.55
  141.3 7.1 shard_map.171
  150.8 27.9 %collective-permute-done.11 = bf16[288,1536]{1,0:T(8,128)(2,1)} collective-permute-done((bf16[288,1536]{1,0:T(8,128)(2,1)}, bf16[288,1536]{1,0:T(8,128)(2,1)}, u32[]{:S(2)}, u32[]{:S(2)}) %collective-permute-start.11) | collective-permute-done | bytes 884768 | tf_op jit(solution)/shard_map/ppermute | solution.py:473
  178.6 4.9 all-to-all-start.1
  195.4 4.1 multiply_reduce_fusion.2
  202.9 29.7 %collective-permute-done.15 = bf16[288,1536]{1,0:T(8,128)(2,1)} collective-permute-done((bf16[288,1536]{1,0:T(8,128)(2,1)S(1)}, bf16[288,1536]{1,0:T(8,128)(2,1)}, u32[]{:S(2)}, u32[]{:S(2)}) %collective-permute-start.15) | collective-permute-done | bytes 884768 | tf_op jit(solution)/shard_map/ppermute | solution.py:473
  235.4 4.4 all-to-all-start.2
  247.3 51.2 %collective-permute-done.16 = bf16[288,1536]{1,0:T(8,128)(2,1)} collective-permute-done((bf16[288,1536]{1,0:T(8,128)(2,1)}, bf16[288,1536]{1,0:T(8,128)(2,1)}, u32[]{:S(2)}, u32[]{:S(2)}) %collective-permute-start.16) | collective-permute-done | bytes 884768 | tf_op jit(solution)/shard_map/ppermute | solution.py:473
  298.5 3.6 collective-permute-start.18
  306.5 28.9 %collective-permute-done.17 = bf16[256,1536]{1,0:T(8,128)(2,1)S(1)} collective-permute-done((bf16[256,1536]{1,0:T(8,128)(2,1)S(1)}, bf16[256,1536]{1,0:T(8,128)(2,1)S(1)}, u32[]{:S(2)}, u32[]{:S(2)}) %collective-permute-start.17) | collective-permute-done | bytes 786464 | tf_op jit(solution)/shard_map/ppermute | solution.py:49
  338.7 3.7 all-to-all-start.3
  359.9 18.8 %shard_map.175 = (bf16[768,768]{1,0:T(8,128)(2,1)}, bf16[768,1536]{1,0:T(8,128)(2,1)}, bf16[768,1536]{1,0:T(8,128)(2,1)}, bf16[768,1536]{1,0:T(8,128)(2,1)}, bf16[768,1664]{1,0:T(8,128)(2,1)}) custom-call(s32[2]{0:T(128)} %pad_add_fusion.expert_ref, bf16[768,1536]{1,0:T(8,128)(2,1)} %bitcast.28.rows_ref.x_own, bf16[768,1664]{1,0:T(8,128)(2,1)} %bitcast.12.grad_ref, ...), custom_call_target="tpu_custom_call" | custom-call | tf_op jit(solution)/shard_map/pallas_call | solution.py:383
  380.1 5.1 all-to-all-start.4
  385.3 18.8 %shard_map.176 = (bf16[768,768]{1,0:T(8,128)(2,1)}, bf16[768,1536]{1,0:T(8,128)(2,1)}, bf16[768,1536]{1,0:T(8,128)(2,1)}, bf16[768,1536]{1,0:T(8,128)(2,1)}, bf16[768,1664]{1,0:T(8,128)(2,1)}) custom-call(s32[2]{0:T(128)} %pad_add_fusion.expert_ref, bf16[768,1536]{1,0:T(8,128)(2,1)} %bitcast.242, bf16[768,1664]{1,0:T(8,128)(2,1)} %bitcast.24.grad_ref, ...), custom_call_target="tpu_custom_call" | custom-call | tf_op jit(solution)/shard_map/pallas_call | solution.py:383
  404.1 14.1 %all-to-all-done.4 = bf16[16,48,1664]{2,1,0:T(8,128)(2,1)} async-done(((bf16[16,48,1664]{2,1,0:T(8,128)(2,1)}), bf16[16,48,1664]{2,1,0:T(8,128)(2,1)}, u32[]{:S(2)}, u32[]{:S(2)}) %all-to-all-start.4) | async-done | bytes 2555936 | tf_op jit(solution)/shard_map/all_to_all | solution.py:556
  418.2 4.8 all-to-all-start.5
  432.7 17.3 %shard_map.177 = (bf16[1536,1536]{1,0:T(8,128)(2,1)}, bf16[768,1536]{1,0:T(8,128)(2,1)}) custom-call(bf16[768,1536]{1,0:T(8,128)(2,1)} %bitcast.28.rows_ref.x_own, bf16[768,1536]{1,0:T(8,128)(2,1)} %bitcast.243, bf16[768,1536]{1,0:T(8,128)(2,1)} %get-tuple-element.150.p_own, bf16[768,1536]{1,0:T(8,128)(2,1)} %get-tuple-element.151.p_far, ...), custom_call_target="tpu_custom_call" | custom-call | tf_op jit(solution)/shard_map/pallas_call | solution.py:418
  452.2 4.9 broadcast_in_dim.172
  458.3 3.6 fusion.2
  471.1 31.5 %collective-permute-done.19 = bf16[256,1664]{1,0:T(8,128)(2,1)} collective-permute-done((bf16[256,1664]{1,0:T(8,128)(2,1)}, bf16[256,1664]{1,0:T(8,128)(2,1)}, u32[]{:S(2)}, u32[]{:S(2)}) %collective-permute-start.19) | collective-permute-done | bytes 852000 | tf_op jit(solution)/shard_map/ppermute | solution.py:49
  511.5 3.7 convolution_convert_fusion.6
  516.8 4.6 all-to-all-start.6
  522.5 3.6 constant_dynamic-slice_fusion.1
  533.9 11.8 %shard_map.179 = (bf16[512,1024]{1,0:T(8,128)(2,1)}, f32[512,1536]{1,0:T(8,128)}) custom-call(bf16[512,1024]{1,0:T(8,128)(2,1)} %get-tuple-element.118.joint_ref, bf16[512,768]{1,0:T(8,128)(2,1)} %shard_map.178.grad_ref, bf16[1536,1024]{1,0:T(8,128)(2,1)} %slice.171.weight_ref), custom_call_target="tpu_custom_call" | custom-call | tf_op jit(solution)/shard_map/pallas_call | solution.py:299
  568.2 7.4 collective-permute-done.23
  575.5 6.5 collective-permute-done.22
  582.1 5.0 all-to-all-start.7
  587.9 4.5 fusion.10
  616.5 17.9 %collective-permute-done.25 = bf16[768,512]{1,0:T(8,128)(2,1)} collective-permute-done((bf16[768,512]{1,0:T(8,128)(2,1)}, bf16[768,512]{1,0:T(8,128)(2,1)}, u32[]{:S(2)}, u32[]{:S(2)}) %collective-permute-start.25) | collective-permute-done | bytes 786464 | tf_op jit(solution)/shard_map/ppermute | solution.py:49
  640.4 3.9 pad_maximum_fusion.3
  644.4 4.4 reshape.317.refs_1_
  672.6 3.8 fusion.66
  680.1 6.7 collective-permute-done.34
  686.8 17.7 %collective-permute-start.35 = (f32[34,1536]{1,0:T(8,128)S(1)}, f32[34,1536]{1,0:T(8,128)S(1)}, u32[]{:S(2)}, u32[]{:S(2)}) collective-permute-start(f32[34,1536]{1,0:T(8,128)S(1)} %add.661), channel_id=1, source_target_pairs={{0,2},{1,3},{2,0},{3,1},{4,6},{5,7},{6,4},{7,5},{8,10},{9,11},{10,... | collective-permute-start | bytes 626696 | tf_op jit(solution)/shard_map/ppermute | solution.py:49
  706.5 32.0 %collective-permute-done.35 = f32[34,1536]{1,0:T(8,128)S(1)} collective-permute-done((f32[34,1536]{1,0:T(8,128)S(1)}, f32[34,1536]{1,0:T(8,128)S(1)}, u32[]{:S(2)}, u32[]{:S(2)}) %collective-permute-start.35) | collective-permute-done | bytes 208928 | tf_op jit(solution)/shard_map/ppermute | solution.py:49
  744.9 4.0 collective-permute-start.42
  753.0 31.3 %collective-permute-done.38 = bf16[2,1,1,192,896]{4,3,2,1,0:T(8,128)(2,1)S(1)} collective-permute-done((bf16[2,1,1,192,896]{4,3,2,1,0:T(8,128)(2,1)S(1)}, bf16[2,1,1,192,896]{4,3,2,1,0:T(8,128)(2,1)S(1)}, u32[]{:S(2)}, u32[]{:S(2)}) %collective-permute-start.38) | collective-permute-done | bytes 688160 | tf_op jit(solution)/shard_map/ppermute | solution.py:49
  788.1 19.7 %collective-permute-done.39 = bf16[1,1,1,192,896]{4,3,2,1,0:T(8,128)(2,1)S(1)} collective-permute-done((bf16[1,1,1,192,896]{4,3,2,1,0:T(8,128)(2,1)S(1)}, bf16[1,1,1,192,896]{4,3,2,1,0:T(8,128)(2,1)S(1)}, u32[]{:S(2)}, u32[]{:S(2)}) %collective-permute-start.39) | collective-permute-done | bytes 344096 | tf_op jit(solution)/shard_map/ppermute | solution.py:49
  (561 shorter events, 255.9 us)
Async XLA Ops:
  3.1 20.0 %collective-permute-start = (bf16[1,1,1,192,896]{4,3,2,1,0:T(8,128)(2,1)S(1)}, bf16[1,1,1,192,896]{4,3,2,1,0:T(8,128)(2,1)S(1)}, u32[]{:S(2)}, u32[]{:S(2)}) collective-permute-start(bf16[1,1,1,192,896]{4,3,2,1,0:T(8,128)(2,1)S(1)} %get-tuple-element.209), channel_id=1, source_target_pairs={{0,4},{4,0},{1,5},{5,1},{2,6},{6,2},{3,7},{7,3},{8,12},{12,8},{9,1... | collective-permute-start | bytes 1032200 | tf_op jit(solution)/shard_map/ppermute | solution.py:49
  7.7 20.6 %collective-permute-start.6 = (bf16[256,1536]{1,0:T(8,128)(2,1)S(1)}, bf16[256,1536]{1,0:T(8,128)(2,1)}, u32[]{:S(2)}, u32[]{:S(2)}) collective-permute-start(bf16[256,1536]{1,0:T(8,128)(2,1)S(1)} %fusion.7), channel_id=1, source_target_pairs={{0,8},{8,0},{1,9},{9,1},{2,10},{10,2},{3,11},{11,3},{4,12},{12,4},... | collective-permute-start | bytes 2359304 | tf_op jit(solution)/shard_map/ppermute | solution.py:49
  7.8 15.0 %collective-permute-start.10 = (s32[256,4]{0,1:T(4,128)S(1)}, s32[256,4]{0,1:T(4,128)S(1)}, u32[]{:S(2)}, u32[]{:S(2)}) collective-permute-start(s32[256,4]{0,1:T(4,128)S(1)} %copy-done.122), channel_id=1, source_target_pairs={{0,4},{4,0},{1,5},{5,1},{2,6},{6,2},{3,7},{7,3},{8,12},{12,8},{9,1... | collective-permute-start | bytes 12296 | tf_op jit(solution)/shard_map/ppermute | solution.py:49
  23.1 16.7 %collective-permute-start.1 = (bf16[2,1,1,192,896]{4,3,2,1,0:T(8,128)(2,1)S(1)}, bf16[2,1,1,192,896]{4,3,2,1,0:T(8,128)(2,1)S(1)}, u32[]{:S(2)}, u32[]{:S(2)}) collective-permute-start(bf16[2,1,1,192,896]{4,3,2,1,0:T(8,128)(2,1)S(1)} %constant_dynamic-update-slice_fusion.20), channel_id=1, source_target_pairs={{0,2},{1,3},{2,0},{3,1},{4,6},{5,7},{6,4},{7,5},{8,10},{9,11},{10,... | collective-permute-start | bytes 2064392 | tf_op jit(solution)/shard_map/ppermute | solution.py:49
  42.5 13.7 %collective-permute-start.4 = (bf16[2,2,1,192,384]{4,3,2,1,0:T(8,128)(2,1)S(1)}, bf16[2,2,1,192,384]{4,3,2,1,0:T(8,128)(2,1)S(1)}, u32[]{:S(2)}, u32[]{:S(2)}) collective-permute-start(bf16[2,2,1,192,384]{4,3,2,1,0:T(8,128)(2,1)S(1)} %get-tuple-element.252), channel_id=1, source_target_pairs={{0,16},{16,0},{1,17},{17,1},{2,18},{18,2},{3,19},{19,3},{4,20},{20... | collective-permute-start | bytes 1769480 | tf_op jit(solution)/shard_map/ppermute | solution.py:49
  44.1 20.5 %collective-permute-start.2 = (bf16[2,2,1,192,512]{4,3,2,1,0:T(8,128)(2,1)S(1)}, bf16[2,2,1,192,512]{4,3,2,1,0:T(8,128)(2,1)S(1)}, u32[]{:S(2)}, u32[]{:S(2)}) collective-permute-start(bf16[2,2,1,192,512]{4,3,2,1,0:T(8,128)(2,1)S(1)} %get-tuple-element.250), channel_id=1, source_target_pairs={{0,1},{1,0},{2,3},{3,2},{4,5},{5,4},{6,7},{7,6},{8,9},{9,8},{10,11... | collective-permute-start | bytes 2359304 | tf_op jit(solution)/shard_map/ppermute | solution.py:49
  45.7 56.8 %collective-permute-start.7 = (bf16[256,1536]{1,0:T(8,128)(2,1)S(1)}, bf16[256,1536]{1,0:T(8,128)(2,1)S(1)}, u32[]{:S(2)}, u32[]{:S(2)}) collective-permute-start(bf16[256,1536]{1,0:T(8,128)(2,1)S(1)} %copy-done.23), channel_id=1, source_target_pairs={{0,4},{4,0},{1,5},{5,1},{2,6},{6,2},{3,7},{7,3},{8,12},{12,8},{9,1... | collective-permute-start | bytes 2359304 | tf_op jit(solution)/shard_map/ppermute | solution.py:49
  51.1 69.3 %collective-permute-start.8 = (bf16[288,1536]{1,0:T(8,128)(2,1)S(1)}, bf16[288,1536]{1,0:T(8,128)(2,1)S(1)}, u32[]{:S(2)}, u32[]{:S(2)}) collective-permute-start(bf16[288,1536]{1,0:T(8,128)(2,1)S(1)} %pad_maximum_fusion.6), channel_id=1, source_target_pairs={{0,4},{1,5},{2,6},{3,7},{4,0},{5,1},{6,2},{7,3},{8,12},{9,13},{10,... | collective-permute-start | bytes 2654216 | tf_op jit(solution)/shard_map/ppermute | solution.py:473
  51.3 69.1 %collective-permute-start.9 = (bf16[288,1536]{1,0:T(8,128)(2,1)S(1)}, bf16[288,1536]{1,0:T(8,128)(2,1)S(1)}, u32[]{:S(2)}, u32[]{:S(2)}) collective-permute-start(bf16[288,1536]{1,0:T(8,128)(2,1)S(1)} %pad_maximum_fusion.7), channel_id=1, source_target_pairs={{0,2},{1,3},{2,0},{3,1},{4,6},{5,7},{6,4},{7,5},{8,10},{9,11},{10,... | collective-permute-start | bytes 2654216 | tf_op jit(solution)/shard_map/ppermute | solution.py:473
  56.2 30.8 %collective-permute-start.5 = (bf16[2,2,1,192,768]{4,3,2,1,0:T(8,128)(2,1)S(1)}, bf16[2,2,1,192,768]{4,3,2,1,0:T(8,128)(2,1)S(1)}, u32[]{:S(2)}, u32[]{:S(2)}) collective-permute-start(bf16[2,2,1,192,768]{4,3,2,1,0:T(8,128)(2,1)S(1)} %constant_dynamic-update-slice_fusion.12), channel_id=1, source_target_pairs={{0,1},{1,0},{2,3},{3,2},{4,5},{5,4},{6,7},{7,6},{8,9},{9,8},{10,11... | collective-permute-start | bytes 3538952 | tf_op jit(solution)/shard_map/ppermute | solution.py:49
  64.7 30.6 %collective-permute-start.3 = (bf16[2,2,2,192,512]{4,3,2,1,0:T(8,128)(2,1)S(1)}, bf16[2,2,2,192,512]{4,3,2,1,0:T(8,128)(2,1)S(1)}, u32[]{:S(2)}, u32[]{:S(2)}) collective-permute-start(bf16[2,2,2,192,512]{4,3,2,1,0:T(8,128)(2,1)S(1)} %constant_dynamic-update-slice_fusion.16), channel_id=1, source_target_pairs={{0,16},{16,0},{1,17},{17,1},{2,18},{18,2},{3,19},{19,3},{4,20},{20... | collective-permute-start | bytes 4718600 | tf_op jit(solution)/shard_map/ppermute | solution.py:49
  122.2 56.4 %all-to-all-start = ((bf16[16,48,1664]{2,1,0:T(8,128)(2,1)}), bf16[16,48,1664]{2,1,0:T(8,128)(2,1)}, u32[]{:S(2)}, u32[]{:S(2)}) async-start(bf16[16,48,1664]{2,1,0:T(8,128)(2,1)} %bitcast.11), calls=%async_computation | async-start | bytes 5111808 | tf_op jit(solution)/shard_map/all_to_all | solution.py:556
  126.7 51.9 %collective-permute-start.11 = (bf16[288,1536]{1,0:T(8,128)(2,1)}, bf16[288,1536]{1,0:T(8,128)(2,1)}, u32[]{:S(2)}, u32[]{:S(2)}) collective-permute-start(bf16[288,1536]{1,0:T(8,128)(2,1)} %pad_maximum_fusion.8), channel_id=1, source_target_pairs={{0,6},{1,7},{2,4},{3,5},{4,2},{5,3},{6,0},{7,1},{8,14},{9,15},{10,... | collective-permute-start | bytes 2654216 | tf_op jit(solution)/shard_map/ppermute | solution.py:473
  130.2 48.5 %collective-permute-start.12 = (bf16[288,1536]{1,0:T(8,128)(2,1)}, bf16[288,1536]{1,0:T(8,128)(2,1)}, u32[]{:S(2)}, u32[]{:S(2)}) collective-permute-start(bf16[288,1536]{1,0:T(8,128)(2,1)} %pad_maximum_fusion.9), channel_id=1, source_target_pairs={{0,1},{1,0},{2,3},{3,2},{4,5},{5,4},{6,7},{7,6},{8,9},{9,8},{10,11... | collective-permute-start | bytes 2654216 | tf_op jit(solution)/shard_map/ppermute | solution.py:473
  141.3 44.5 %collective-permute-start.14 = (bf16[1536,768]{1,0:T(8,128)(2,1)}, bf16[1536,768]{1,0:T(8,128)(2,1)}, u32[]{:S(2)}, u32[]{:S(2)}) collective-permute-start(bf16[1536,768]{1,0:T(8,128)(2,1)} %get-tuple-element.210), channel_id=1, source_target_pairs={{0,8},{8,0},{1,9},{9,1},{2,10},{10,2},{3,11},{11,3},{4,12},{12,4},... | collective-permute-start | bytes 7077896 | tf_op jit(solution)/shard_map/ppermute | solution.py:49
  178.6 56.8 %all-to-all-start.1 = ((bf16[16,48,1664]{2,1,0:T(8,128)(2,1)}), bf16[16,48,1664]{2,1,0:T(8,128)(2,1)}, u32[]{:S(2)}, u32[]{:S(2)}) async-start(bf16[16,48,1664]{2,1,0:T(8,128)(2,1)} %bitcast.23), calls=%async_computation.1 | async-start | bytes 5111808 | tf_op jit(solution)/shard_map/all_to_all | solution.py:556
  190.5 42.1 %collective-permute-start.15 = (bf16[288,1536]{1,0:T(8,128)(2,1)S(1)}, bf16[288,1536]{1,0:T(8,128)(2,1)}, u32[]{:S(2)}, u32[]{:S(2)}) collective-permute-start(bf16[288,1536]{1,0:T(8,128)(2,1)S(1)} %copy-done.73), channel_id=1, source_target_pairs={{0,5},{1,4},{2,7},{3,6},{4,1},{5,0},{6,3},{7,2},{8,13},{9,12},{10,... | collective-permute-start | bytes 2654216 | tf_op jit(solution)/shard_map/ppermute | solution.py:473
  235.4 63.1 %all-to-all-start.2 = ((bf16[16,48,1536]{2,1,0:T(8,128)(2,1)}), bf16[16,48,1536]{2,1,0:T(8,128)(2,1)}, u32[]{:S(2)}, u32[]{:S(2)}) async-start(bf16[16,48,1536]{2,1,0:T(8,128)(2,1)} %bitcast.245), calls=%async_computation.2 | async-start | bytes 4718592 | tf_op jit(solution)/shard_map/all_to_all | solution.py:556
  239.9 58.6 %collective-permute-start.16 = (bf16[288,1536]{1,0:T(8,128)(2,1)}, bf16[288,1536]{1,0:T(8,128)(2,1)}, u32[]{:S(2)}, u32[]{:S(2)}) collective-permute-start(bf16[288,1536]{1,0:T(8,128)(2,1)} %pad_maximum_fusion.11), channel_id=1, source_target_pairs={{0,7},{1,6},{2,5},{3,4},{4,3},{5,2},{6,1},{7,0},{8,15},{9,14},{10,... | collective-permute-start | bytes 2654216 | tf_op jit(solution)/shard_map/ppermute | solution.py:473
  298.5 36.9 %collective-permute-start.17 = (bf16[256,1536]{1,0:T(8,128)(2,1)S(1)}, bf16[256,1536]{1,0:T(8,128)(2,1)S(1)}, u32[]{:S(2)}, u32[]{:S(2)}) collective-permute-start(bf16[256,1536]{1,0:T(8,128)(2,1)S(1)} %copy-done.13), channel_id=1, source_target_pairs={{0,4},{4,0},{1,5},{5,1},{2,6},{6,2},{3,7},{7,3},{8,12},{12,8},{9,1... | collective-permute-start | bytes 2359304 | tf_op jit(solution)/shard_map/ppermute | solution.py:49
  298.5 40.1 %collective-permute-start.18 = (bf16[288,1536]{1,0:T(8,128)(2,1)}, bf16[288,1536]{1,0:T(8,128)(2,1)}, u32[]{:S(2)}, u32[]{:S(2)}) collective-permute-start(bf16[288,1536]{1,0:T(8,128)(2,1)} %pad_maximum_fusion.13), channel_id=1, source_target_pairs={{0,3},{1,2},{2,1},{3,0},{4,7},{5,6},{6,5},{7,4},{8,11},{9,10},{10,... | collective-permute-start | bytes 2654216 | tf_op jit(solution)/shard_map/ppermute | solution.py:473
  338.7 40.1 %all-to-all-start.3 = ((bf16[16,48,1536]{2,1,0:T(8,128)(2,1)}), bf16[16,48,1536]{2,1,0:T(8,128)(2,1)S(1)}, u32[]{:S(2)}, u32[]{:S(2)}) async-start(bf16[16,48,1536]{2,1,0:T(8,128)(2,1)} %bitcast.244), calls=%async_computation.3 | async-start | bytes 4718592 | tf_op jit(solution)/shard_map/all_to_all | solution.py:556
  380.1 38.1 %all-to-all-start.4 = ((bf16[16,48,1664]{2,1,0:T(8,128)(2,1)}), bf16[16,48,1664]{2,1,0:T(8,128)(2,1)}, u32[]{:S(2)}, u32[]{:S(2)}) async-start(bf16[16,48,1664]{2,1,0:T(8,128)(2,1)} %bitcast.253), calls=%async_computation.4 | async-start | bytes 5111808 | tf_op jit(solution)/shard_map/all_to_all | solution.py:556
  418.2 40.0 %all-to-all-start.5 = ((bf16[16,48,1664]{2,1,0:T(8,128)(2,1)}), bf16[16,48,1664]{2,1,0:T(8,128)(2,1)}, u32[]{:S(2)}, u32[]{:S(2)}) async-start(bf16[16,48,1664]{2,1,0:T(8,128)(2,1)} %bitcast.252), calls=%async_computation.5 | async-start | bytes 5111808 | tf_op jit(solution)/shard_map/all_to_all | solution.py:556
  461.8 40.8 %collective-permute-start.19 = (bf16[256,1664]{1,0:T(8,128)(2,1)}, bf16[256,1664]{1,0:T(8,128)(2,1)}, u32[]{:S(2)}, u32[]{:S(2)}) collective-permute-start(bf16[256,1664]{1,0:T(8,128)(2,1)} %fusion.2), channel_id=1, source_target_pairs={{0,4},{4,0},{1,5},{5,1},{2,6},{6,2},{3,7},{7,3},{8,12},{12,8},{9,1... | collective-permute-start | bytes 2555912 | tf_op jit(solution)/shard_map/ppermute | solution.py:49
  516.3 16.7 %collective-permute-start.20 = (bf16[256,768]{1,0:T(8,128)(2,1)S(1)}, bf16[256,768]{1,0:T(8,128)(2,1)S(1)}, u32[]{:S(2)}, u32[]{:S(2)}) collective-permute-start(bf16[256,768]{1,0:T(8,128)(2,1)S(1)} %get-tuple-element.265), channel_id=1, source_target_pairs={{0,8},{8,0},{1,9},{9,1},{2,10},{10,2},{3,11},{11,3},{4,12},{12,4},... | collective-permute-start | bytes 1179656 | tf_op jit(solution)/shard_map/ppermute | solution.py:49
  516.4 38.5 %collective-permute-start.21 = (bf16[256,768]{1,0:T(8,128)(2,1)}, bf16[256,768]{1,0:T(8,128)(2,1)}, u32[]{:S(2)}, u32[]{:S(2)}) collective-permute-start(bf16[256,768]{1,0:T(8,128)(2,1)} %get-tuple-element.263), channel_id=1, source_target_pairs={{0,8},{8,0},{1,9},{9,1},{2,10},{10,2},{3,11},{11,3},{4,12},{12,4},... | collective-permute-start | bytes 1179656 | tf_op jit(solution)/shard_map/ppermute | solution.py:49
  516.8 65.2 %all-to-all-start.6 = ((bf16[16,48,1536]{2,1,0:T(8,128)(2,1)}), bf16[16,48,1536]{2,1,0:T(8,128)(2,1)}, u32[]{:S(2)}, u32[]{:S(2)}) async-start(bf16[16,48,1536]{2,1,0:T(8,128)(2,1)} %bitcast.51), calls=%async_computation.6 | async-start | bytes 4718592 | tf_op jit(solution)/shard_map/all_to_all | solution.py:556
  527.0 125.8 %collective-permute-start.27 = (bf16[288,1536]{1,0:T(8,128)(2,1)}, bf16[288,1536]{1,0:T(8,128)(2,1)}, u32[]{:S(2)}, u32[]{:S(2)}) collective-permute-start(bf16[288,1536]{1,0:T(8,128)(2,1)} %pad_maximum_fusion.14), channel_id=1, source_target_pairs={{0,2},{1,3},{2,4},{3,5},{4,6},{5,7},{6,0},{7,1},{8,10},{9,11},{10,... | collective-permute-start | bytes 2654216 | tf_op jit(solution)/shard_map/ppermute | solution.py:534
  548.5 18.5 %collective-permute-start.26 = (f32[256,1536]{1,0:T(8,128)}, f32[256,1536]{1,0:T(8,128)S(1)}, u32[]{:S(2)}, u32[]{:S(2)}) collective-permute-start(f32[256,1536]{1,0:T(8,128)} %slice.204), channel_id=1, source_target_pairs={{0,8},{8,0},{1,9},{9,1},{2,10},{10,2},{3,11},{11,3},{4,12},{12,4},... | collective-permute-start | bytes 4718600 | tf_op jit(solution)/shard_map/ppermute | solution.py:49
  550.8 102.0 %collective-permute-start.28 = (bf16[288,1536]{1,0:T(8,128)(2,1)}, bf16[288,1536]{1,0:T(8,128)(2,1)}, u32[]{:S(2)}, u32[]{:S(2)}) collective-permute-start(bf16[288,1536]{1,0:T(8,128)(2,1)} %pad_maximum_fusion.15), channel_id=1, source_target_pairs={{0,6},{1,7},{2,0},{3,1},{4,2},{5,3},{6,4},{7,5},{8,14},{9,15},{10,... | collective-permute-start | bytes 2654216 | tf_op jit(solution)/shard_map/ppermute | solution.py:534
  562.2 19.9 %collective-permute-start.22 = (bf16[1536,256]{1,0:T(8,128)(2,1)S(1)}, bf16[1536,256]{1,0:T(8,128)(2,1)}, u32[]{:S(2)}, u32[]{:S(2)}) collective-permute-start(bf16[1536,256]{1,0:T(8,128)(2,1)S(1)} %convolution_convert_fusion.5), channel_id=1, source_target_pairs={{0,16},{16,0},{1,17},{17,1},{2,18},{18,2},{3,19},{19,3},{4,20},{20... | collective-permute-start | bytes 2359304 | tf_op jit(solution)/shard_map/ppermute | solution.py:49
  567.0 85.8 %collective-permute-start.29 = (bf16[288,1536]{1,0:T(8,128)(2,1)}, bf16[288,1536]{1,0:T(8,128)(2,1)}, u32[]{:S(2)}, u32[]{:S(2)}) collective-permute-start(bf16[288,1536]{1,0:T(8,128)(2,1)} %pad_maximum_fusion.16), channel_id=1, source_target_pairs={{0,4},{1,5},{2,6},{3,7},{4,0},{5,1},{6,2},{7,3},{8,12},{9,13},{10,... | collective-permute-start | bytes 2654216 | tf_op jit(solution)/shard_map/ppermute | solution.py:534
  582.1 70.7 %all-to-all-start.7 = ((bf16[16,48,1536]{2,1,0:T(8,128)(2,1)}), bf16[16,48,1536]{2,1,0:T(8,128)(2,1)}, u32[]{:S(2)}, u32[]{:S(2)}) async-start(bf16[16,48,1536]{2,1,0:T(8,128)(2,1)} %bitcast.254), calls=%async_computation.7 | async-start | bytes 4718592 | tf_op jit(solution)/shard_map/all_to_all | solution.py:556
  598.4 50.4 %collective-permute-start.24 = (bf16[1536,256]{1,0:T(8,128)(2,1)}, bf16[1536,256]{1,0:T(8,128)(2,1)}, u32[]{:S(2)}, u32[]{:S(2)}) collective-permute-start(bf16[1536,256]{1,0:T(8,128)(2,1)} %convolution_convert_fusion.4), channel_id=1, source_target_pairs={{0,16},{16,0},{1,17},{17,1},{2,18},{18,2},{3,19},{19,3},{4,20},{20... | collective-permute-start | bytes 2359304 | tf_op jit(solution)/shard_map/ppermute | solution.py:49
  601.9 32.5 %collective-permute-start.25 = (bf16[768,512]{1,0:T(8,128)(2,1)}, bf16[768,512]{1,0:T(8,128)(2,1)}, u32[]{:S(2)}, u32[]{:S(2)}) collective-permute-start(bf16[768,512]{1,0:T(8,128)(2,1)} %convolution_convert_fusion.7), channel_id=1, source_target_pairs={{0,1},{1,0},{2,3},{3,2},{4,5},{5,4},{6,7},{7,6},{8,9},{9,8},{10,11... | collective-permute-start | bytes 2359304 | tf_op jit(solution)/shard_map/ppermute | solution.py:49
  654.4 25.6 %collective-permute-start.31 = (bf16[2,2,1,192,384]{4,3,2,1,0:T(8,128)(2,1)S(1)}, bf16[2,2,1,192,384]{4,3,2,1,0:T(8,128)(2,1)S(1)}, u32[]{:S(2)}, u32[]{:S(2)}) collective-permute-start(bf16[2,2,1,192,384]{4,3,2,1,0:T(8,128)(2,1)S(1)} %dynamic-slice_convert_fusion.2), channel_id=1, source_target_pairs={{0,16},{16,0},{1,17},{17,1},{2,18},{18,2},{3,19},{19,3},{4,20},{20... | collective-permute-start | bytes 1769480 | tf_op jit(solution)/shard_map/ppermute | solution.py:49
  657.5 47.0 %collective-permute-start.30 = (bf16[2,2,1,192,512]{4,3,2,1,0:T(8,128)(2,1)S(1)}, bf16[2,2,1,192,512]{4,3,2,1,0:T(8,128)(2,1)S(1)}, u32[]{:S(2)}, u32[]{:S(2)}) collective-permute-start(bf16[2,2,1,192,512]{4,3,2,1,0:T(8,128)(2,1)S(1)} %dynamic-slice_convert_fusion), channel_id=1, source_target_pairs={{0,1},{1,0},{2,3},{3,2},{4,5},{5,4},{6,7},{7,6},{8,9},{9,8},{10,11... | collective-permute-start | bytes 2359304 | tf_op jit(solution)/shard_map/ppermute | solution.py:49
  657.6 14.4 %collective-permute-start.32 = (f32[34,1536]{1,0:T(8,128)S(1)}, f32[34,1536]{1,0:T(8,128)S(1)}, u32[]{:S(2)}, u32[]{:S(2)}) collective-permute-start(f32[34,1536]{1,0:T(8,128)S(1)} %copy-done.67), channel_id=1, source_target_pairs={{0,8},{8,0},{1,9},{9,1},{2,10},{10,2},{3,11},{11,3},{4,12},{12,4},... | collective-permute-start | bytes 626696 | tf_op jit(solution)/shard_map/ppermute | solution.py:49
  657.6 81.6 %collective-permute-start.36 = (bf16[256,1536]{1,0:T(8,128)(2,1)S(1)}, bf16[256,1536]{1,0:T(8,128)(2,1)S(1)}, u32[]{:S(2)}, u32[]{:S(2)}) collective-permute-start(bf16[256,1536]{1,0:T(8,128)(2,1)S(1)} %copy-done.77), channel_id=1, source_target_pairs={{0,4},{4,0},{1,5},{5,1},{2,6},{6,2},{3,7},{7,3},{8,12},{12,8},{9,1... | collective-permute-start | bytes 2359304 | tf_op jit(solution)/shard_map/ppermute | solution.py:49
  658.7 81.5 %collective-permute-start.37 = (bf16[288,1536]{1,0:T(8,128)(2,1)S(1)}, bf16[288,1536]{1,0:T(8,128)(2,1)}, u32[]{:S(2)}, u32[]{:S(2)}) collective-permute-start(bf16[288,1536]{1,0:T(8,128)(2,1)S(1)} %copy-done.72), channel_id=1, source_target_pairs={{0,5},{1,4},{2,7},{3,6},{4,1},{5,0},{6,3},{7,2},{8,13},{9,12},{10,... | collective-permute-start | bytes 2654216 | tf_op jit(solution)/shard_map/ppermute | solution.py:534
  686.8 51.7 %collective-permute-start.35 = (f32[34,1536]{1,0:T(8,128)S(1)}, f32[34,1536]{1,0:T(8,128)S(1)}, u32[]{:S(2)}, u32[]{:S(2)}) collective-permute-start(f32[34,1536]{1,0:T(8,128)S(1)} %add.661), channel_id=1, source_target_pairs={{0,2},{1,3},{2,0},{3,1},{4,6},{5,7},{6,4},{7,5},{8,10},{9,11},{10,... | collective-permute-start | bytes 626696 | tf_op jit(solution)/shard_map/ppermute | solution.py:49
  741.7 42.6 %collective-permute-start.38 = (bf16[2,1,1,192,896]{4,3,2,1,0:T(8,128)(2,1)S(1)}, bf16[2,1,1,192,896]{4,3,2,1,0:T(8,128)(2,1)S(1)}, u32[]{:S(2)}, u32[]{:S(2)}) collective-permute-start(bf16[2,1,1,192,896]{4,3,2,1,0:T(8,128)(2,1)S(1)} %dynamic-slice_convert_fusion.1), channel_id=1, source_target_pairs={{0,2},{1,3},{2,0},{3,1},{4,6},{5,7},{6,4},{7,5},{8,10},{9,11},{10,... | collective-permute-start | bytes 2064392 | tf_op jit(solution)/shard_map/ppermute | solution.py:49
  741.8 46.2 %collective-permute-start.40 = (f32[34,1536]{1,0:T(8,128)S(1)}, f32[34,1536]{1,0:T(8,128)S(1)}, u32[]{:S(2)}, u32[]{:S(2)}) collective-permute-start(f32[34,1536]{1,0:T(8,128)S(1)} %copy-done.68), channel_id=1, source_target_pairs={{0,4},{4,0},{1,5},{5,1},{2,6},{6,2},{3,7},{7,3},{8,12},{12,8},{9,1... | collective-permute-start | bytes 626696 | tf_op jit(solution)/shard_map/ppermute | solution.py:49
  744.3 63.6 %collective-permute-start.41 = (bf16[288,1536]{1,0:T(8,128)(2,1)S(1)}, bf16[288,1536]{1,0:T(8,128)(2,1)S(1)}, u32[]{:S(2)}, u32[]{:S(2)}) collective-permute-start(bf16[288,1536]{1,0:T(8,128)(2,1)S(1)} %copy-done.70), channel_id=1, source_target_pairs={{0,3},{1,2},{2,5},{3,4},{4,7},{5,6},{6,1},{7,0},{8,11},{9,10},{10,... | collective-permute-start | bytes 2654216 | tf_op jit(solution)/shard_map/ppermute | solution.py:534
  744.9 65.9 %collective-permute-start.42 = (bf16[288,1536]{1,0:T(8,128)(2,1)S(1)}, bf16[288,1536]{1,0:T(8,128)(2,1)S(1)}, u32[]{:S(2)}, u32[]{:S(2)}) collective-permute-start(bf16[288,1536]{1,0:T(8,128)(2,1)S(1)} %copy-done.69), channel_id=1, source_target_pairs={{0,7},{1,6},{2,1},{3,0},{4,3},{5,2},{6,5},{7,4},{8,15},{9,14},{10,... | collective-permute-start | bytes 2654216 | tf_op jit(solution)/shard_map/ppermute | solution.py:534
  749.0 61.8 %collective-permute-start.43 = (bf16[288,1536]{1,0:T(8,128)(2,1)S(1)}, bf16[288,1536]{1,0:T(8,128)(2,1)S(1)}, u32[]{:S(2)}, u32[]{:S(2)}) collective-permute-start(bf16[288,1536]{1,0:T(8,128)(2,1)S(1)} %copy-done.71), channel_id=1, source_target_pairs={{0,1},{1,0},{2,3},{3,2},{4,5},{5,4},{6,7},{7,6},{8,9},{9,8},{10,11... | collective-permute-start | bytes 2654216 | tf_op jit(solution)/shard_map/ppermute | solution.py:534
  784.5 23.3 %collective-permute-start.39 = (bf16[1,1,1,192,896]{4,3,2,1,0:T(8,128)(2,1)S(1)}, bf16[1,1,1,192,896]{4,3,2,1,0:T(8,128)(2,1)S(1)}, u32[]{:S(2)}, u32[]{:S(2)}) collective-permute-start(bf16[1,1,1,192,896]{4,3,2,1,0:T(8,128)(2,1)S(1)} %dynamic-slice_convert_fusion.3), channel_id=1, source_target_pairs={{0,4},{4,0},{1,5},{5,1},{2,6},{6,2},{3,7},{7,3},{8,12},{12,8},{9,1... | collective-permute-start | bytes 1032200 | tf_op jit(solution)/shard_map/ppermute | solution.py:49
  (130 other events, 909.3 us)

commit v3 on v2

--- a/solution.py
+++ b/solution.py
@@ -1,3 +1,5 @@
+import functools
+
 import jax
 import jax.numpy as jnp
 from jax import lax
@@ -11,11 +13,12 @@
 HEAD_DIM = 128
 FFE = 768
 EXPERTS = 32
-TOP = 4
 CAP = 48
 EPSILON = 1e-06
 VMEM_LIMIT = 56 * 1024 * 1024
 EXTRA = 128
+INWARD = [[(-1, 0), (-2, 0)], [(-3, 0), (0, 1)], [(-2, 1)], [(-3, 1)], [(-1, 1)]]
+OUTWARD = [[(1, 0), (3, 0)], [(2, 0)], [(2, 1)], [(1, 1), (3, 1), (0, 1)]]
 EXPERT = ("y", "c")
 FSDP = ("h", "r")
 BOTH = EXPERT + FSDP
@@ -38,10 +41,6 @@
 
 def rms_apply(values, gain):
     return values * lax.rsqrt(jnp.mean(values * values, axis=-1, keepdims=True) + EPSILON) * gain
-
-
-def reglu_smooth(projected):
-    return jax.nn.gelu(projected[..., :FFE]) * projected[..., FFE:]
 
 
 def swap(value, axis, bit=1):
@@ -151,34 +150,54 @@
     return jnp.concatenate(parts, axis=lane).reshape(whole_rows, columns)
 
 
+def product_kernel(width, place_ref, left_ref, right_ref, first_sent_ref, first_ref, last_sent_ref, last_ref):
+    rows = left_ref.shape[1] // 2
+    product = t_dot(left_ref[...], right_ref[...])
+    half = product.shape[1] // 2
+    lower = place_ref[0] == 0
+    mine = jnp.where(lower, product[:, :width], product[:, half : half + width])
+    other = jnp.where(lower, product[:, half : half + width], product[:, :width])
+    first_ref[...] = mine
+    first_sent_ref[...] = other.astype(bf16)
+    last = jnp.concatenate([product[:, width:half], product[:, half + width :]], axis=1)
+    near = place_ref[1] == 0
+    last_ref[...] = jnp.where(near, last[:rows], last[rows:])
+    last_sent_ref[...] = jnp.where(near, last[rows:], last[:rows]).astype(bf16)
+
+
 def scatter_sends(left, right):
     if lax.axis_size("y") != 2:
         return None
     x_step = fsdp_bits()[-1]
-    left_of, right_of, right_last = product_parts(left, right)
-    y_index, x_index = lax.axis_index("y"), bit_index(*x_step[:2])
-    return (
-        swap(t_dot(left, right_of(1 - y_index)).astype(bf16), "y"),
-        swap(t_dot(left_of(1 - x_index), right_last).astype(bf16), *x_step[:2]),
-    )
-
-
-def product_parts(left, right):
     tokens, whole_rows = left.shape
     columns = right.shape[1]
     rows = whole_rows // lax.axis_size(FSDP)
     width = split_width(columns // 2)[0]
-    left_blocks = left.reshape(tokens, -1, 2, rows)
-    cube = right.reshape(tokens, 2, columns // 2)
-    right_first, right_last = cube[:, :, :width], cube[:, :, width:].reshape(tokens, -1)
-
-    def left_of(index):
-        return lax.dynamic_index_in_dim(left_blocks, index, 2, keepdims=False).reshape(tokens, -1)
-
-    def right_of(index):
-        return lax.dynamic_index_in_dim(right_first, index, 1, keepdims=False)
-
-    return left_of, right_of, right_last
+    place = jnp.stack([lax.axis_index("y"), bit_index(*x_step[:2])]).astype(jnp.int32)
+
+    def out(count, wide, kind):
+        return pl.BlockSpec((count, wide), lambda i, *_: (i, 0)), jax.ShapeDtypeStruct(
+            (whole_rows // (2 * rows) * count, wide), kind
+        )
+
+    rest = columns - 2 * width
+    outs = [out(2 * rows, width, bf16), out(2 * rows, width, f32), out(rows, rest, bf16), out(rows, rest, f32)]
+    first_sent, first, last_sent, last = pl.pallas_call(
+        functools.partial(product_kernel, width),
+        grid_spec=pltpu.PrefetchScalarGridSpec(
+            num_scalar_prefetch=1,
+            grid=(whole_rows // (2 * rows),),
+            in_specs=[
+                pl.BlockSpec((tokens, 2 * rows), lambda i, *_: (0, i)),
+                pl.BlockSpec((tokens, columns), lambda i, *_: (0, 0)),
+            ],
+            out_specs=[spec for spec, _ in outs],
+        ),
+        out_shape=[shape for _, shape in outs],
+        compiler_params=pltpu.CompilerParams(vmem_limit_bytes=VMEM_LIMIT),
+        cost_estimate=pl.CostEstimate(flops=0, bytes_accessed=0, transcendentals=0),
+    )(place, left, right)
+    return first, swap(first_sent, "y"), last, swap(last_sent, *x_step[:2])
 
 
 def scatter_products(pairs, sends, rounds):
@@ -198,11 +217,10 @@
     y_step, x_step = ("y", 1, lane), steps[-1]
     y_index, x_index = lax.axis_index("y"), bit_index(*x_step[:2])
     firsts, lasts = [], []
-    for (left, right), (first_sent, last_sent) in zip(pairs, sends):
-        left_of, right_of, right_last = product_parts(left, right)
-        rows = left.shape[1] // size
-        first = t_dot(left, right_of(y_index)) + first_sent.astype(f32)
-        last = t_dot(left_of(x_index), right_last) + last_sent.astype(f32)
+    for first, first_sent, last, last_sent in sends:
+        rows = first.shape[0] // size
+        first = first + first_sent.astype(f32)
+        last = last + last_sent.astype(f32)
         firsts.append(first.reshape((2,) * len(steps) + (rows, -1)))
         lasts.append(last.reshape((2,) * (len(steps) - 1) + (1, rows, 2, last.shape[1] // 2)))
     widths = [block.shape[-1] for block in firsts + lasts]
@@ -398,6 +416,72 @@
         compiler_params=pltpu.CompilerParams(vmem_limit_bytes=VMEM_LIMIT),
         cost_estimate=pl.CostEstimate(flops=0, bytes_accessed=0, transcendentals=0),
     )(expert, received, grad_rows, router, up, down)
+
+
+def token_backward_kernel(
+    core_ref,
+    place_ref,
+    back_ref,
+    far_ref,
+    spread_ref,
+    gates_ref,
+    router_ref,
+    xn_ref,
+    hidden_ref,
+    gain_ref,
+    grad_ref,
+    weight_ref,
+    d_hidden_ref,
+    d_hidden_b_ref,
+    d_attended_ref,
+    small_ref,
+):
+    width = hidden_ref.shape[1]
+    part = EXPERTS // 2
+    wide = t_dot(place_ref[...], back_ref[...])
+    far = far_ref[...]
+    d_gates = jnp.zeros(gates_ref.shape, f32)
+    for number, extra in enumerate((wide[:, width:].astype(bf16), far[:, width:])):
+        for start in (0, part):
+            d_gates = d_gates + dot(extra[:, start : start + part], spread_ref[number])
+    gates = gates_ref[...]
+    d_chosen = gates * (d_gates - jnp.sum(gates * d_gates, axis=-1, keepdims=True))
+    d_logits = d_chosen.astype(bf16)
+    d_xn = dot_t(d_logits, router_ref[...]) + wide[:, :width] + far[:, :width].astype(f32)
+    hidden = hidden_ref[...]
+    scale = lax.rsqrt(jnp.mean(hidden * hidden, axis=-1, keepdims=True) + EPSILON)
+    normed = hidden * scale
+    scaled = d_xn * gain_ref[...]
+    d_hidden = grad_ref[...].astype(f32) + scale * (
+        scaled - normed * jnp.mean(scaled * normed, axis=-1, keepdims=True)
+    )
+    d_hidden_ref[...] = d_hidden
+    d_hidden_b = d_hidden.astype(bf16)
+    d_hidden_b_ref[...] = d_hidden_b
+    small_ref[:EXPERTS] = t_dot(d_logits, xn_ref[...])
+    small_ref[EXPERTS:] = jnp.broadcast_to(jnp.sum(d_xn * normed, axis=0, keepdims=True), (8, width))
+    d_attended = dot_t(d_hidden_b, weight_ref[...]).astype(bf16)
+    first, last = d_attended[:, : width // 2], d_attended[:, width // 2 :]
+    lower = core_ref[0] == 0
+    d_attended_ref[0] = jnp.where(lower, first, last)
+    d_attended_ref[1] = jnp.where(lower, last, first)
+
+
+def token_backward(core, place, back, far, spread, gates, router, xn, hidden, gain, grad, weight):
+    seq_len, width = hidden.shape
+    return pl.pallas_call(
+        token_backward_kernel,
+        in_specs=[pl.BlockSpec(memory_space=pltpu.SMEM)] + [pl.BlockSpec(memory_space=pltpu.VMEM)] * 11,
+        out_specs=[pl.BlockSpec(memory_space=pltpu.VMEM)] * 4,
+        out_shape=[
+            jax.ShapeDtypeStruct((seq_len, width), f32),
+            jax.ShapeDtypeStruct((seq_len, width), bf16),
+            jax.ShapeDtypeStruct((2, seq_len, width // 2), bf16),
+            jax.ShapeDtypeStruct((EXPERTS + 8, width), f32),
+        ],
+        compiler_params=pltpu.CompilerParams(vmem_limit_bytes=VMEM_LIMIT),
+        cost_estimate=pl.CostEstimate(flops=0, bytes_accessed=0, transcendentals=0),
+    )(core, place, back, far, spread, gates, router, xn, hidden, gain, grad, weight)
 
 
 def expert_weights_kernel(x_own, x_far, p_own, p_far, i_own, i_far, d_own, d_far, up_ref, down_ref):
@@ -469,9 +553,6 @@
         ]
     ).astype(jnp.int32)
 
-    def fsdp_partner(value, bit):
-        return lax.ppermute(value, FSDP, [(i, i ^ bit) for i in range(fsdp)])
-
     box = {}
 
     def tie(value, *names):
@@ -480,14 +561,22 @@
         return value
 
     up_width, down_width = gate_up.shape[1], down.shape[1]
-    even, odd = [list(range(fsdp // 2 + first, fsdp, 2)) for first in range(2)]
-    middle = len(even) // 2
-    turns = [even[:middle], even[middle:], odd[:middle], odd[middle:]]
-    near = [list(range(1, fsdp // 2))[turn::3] for turn in range(3)]
-
-    def fetch(bits, *names):
-        for bit in bits:
-            expert = (me ^ bit) // parts
+    columns = fsdp // 4
+
+    def target(index, move, sign=1):
+        step, cross = move
+        line = index // columns
+        line = (line + sign * step + 4) % 4 if step >= 0 else line ^ -step
+        return line * columns + (index % columns ^ cross)
+
+    def every(moves):
+        return [
+            (step, other) for step, cross in moves for other in (range(1, columns) if cross else range(1))
+        ]
+
+    def fetch(moves, *names):
+        for move in every(moves):
+            expert = target(me, move) // parts
             piece = jnp.concatenate(
                 [
                     lax.dynamic_index_in_dim(gate_up, expert, 0, keepdims=False),
@@ -495,33 +584,24 @@
                 ],
                 axis=0,
             )
-            box["in", bit] = fsdp_partner(tie(piece, *names), bit) if bit else piece
-
-    def coming(bits):
-        return [("in", bit) for bit in bits]
+            if move != (0, 0):
+                piece = lax.ppermute(tie(piece, *names), FSDP, [(i, target(i, move)) for i in range(fsdp)])
+            box["in", move] = piece
+
+    def coming(moves):
+        return [("in", move) for move in every(moves)]
 
     def assemble():
         up_full = jnp.zeros((fsdp * up_width, gate_up.shape[2]), gate_up.dtype)
         down_full = jnp.zeros((fsdp * down_width, down.shape[2]), down.dtype)
-        for bit in [0] + near[1] + turns[0] + near[0] + turns[1] + turns[2] + turns[3] + near[2]:
-            other, piece = me ^ bit, box["in", bit]
-            up_full = lax.dynamic_update_slice(up_full, piece[:up_width], (other * up_width, 0))
-            down_full = lax.dynamic_update_slice(down_full, piece[up_width:], (other * down_width, 0))
+        for move in every(sum(INWARD, [(0, 0)])):
+            source, piece = target(me, move, -1), box["in", move]
+            up_full = lax.dynamic_update_slice(up_full, piece[:up_width], (source * up_width, 0))
+            down_full = lax.dynamic_update_slice(down_full, piece[up_width:], (source * down_width, 0))
         return up_full, down_full
 
-    columns = fsdp // 4
-    stay = [(0, 0)]
-    same = [(1, 0), (3, 0), (2, 0)]
-    across = [(step, cross) for cross in range(1, columns) for step in (1, 3)]
-    opposite = [(2, cross) for cross in range(1, columns)]
-    level = [(0, cross) for cross in range(1, columns)]
-
-    def target(index, move, sign=1):
-        step, cross = move
-        return (index // columns + sign * step + 4) % 4 * columns + (index % columns ^ cross)
-
     def give(moves, up_grad, down_grad, *names):
-        for move in moves:
+        for move in every(moves):
             to = target(me, move)
             piece = jnp.concatenate(
                 [
@@ -535,12 +615,12 @@
             box["out", move] = piece
 
     def going(moves):
-        return [("out", move) for move in moves]
+        return [("out", move) for move in every(moves)]
 
     def collect():
         up_sum = jnp.zeros(gate_up.shape, f32)
         down_sum = jnp.zeros(down.shape, f32)
-        for move in stay + same + opposite + across + level:
+        for move in every(sum(OUTWARD, [(0, 0)])):
             expert = target(me, move, -1) // parts
             piece = box["out", move].astype(f32)[None]
             up_part, down_part = piece[:, :up_width], piece[:, up_width:]
@@ -565,12 +645,7 @@
         cube = table.reshape(table.shape[0], groups, 2, local_count // 2)
         return lax.dynamic_index_in_dim(cube, index, 2, keepdims=False).reshape(table.shape[0], half_experts)
 
-    def both_columns(mine, other):
-        shape = (mine.shape[0], groups, 1, local_count // 2)
-        return order_by(half, mine.reshape(shape), other.reshape(shape), 2).reshape(-1, EXPERTS)
-
     token_f = tokens.astype(f32)
-    grad_f = grad_output.astype(f32)
 
     qkv_mine = jnp.concatenate(
         [
@@ -601,7 +676,7 @@
         nonlocal gate_up, down
         sent, block, gate_up, down = together(grad_output, block, gate_up, down)
         box["grad_far"] = swap(sent, "h")
-        fetch(near[1] + turns[0])
+        fetch(INWARD[0])
         return mark(block)
 
     def send_rows(place, grad, mask):
@@ -615,10 +690,10 @@
     core_weights, xn_pair, own_sent = tie(
         (gather_shards(shard, first_done), xn_pair, send_rows(place_own, grad_output, mask_own)),
         "grad_far",
-        *coming(turns[0] + near[1]),
-    )
+        *coming(INWARD[0]),
+    )
+    fetch(INWARD[1], *coming(INWARD[0]))
     box["grad_rows_own"] = exchange(own_sent)
-    fetch(turns[1] + near[0], *coming(turns[0]))
     xn_pair = mark(xn_pair)
     qkv_width = query_half + 2 * kv_half
     qkv_core, out_core = core_weights[:, :qkv_width], core_weights[:, qkv_width:]
@@ -627,16 +702,15 @@
     out_full = order_by(core, out_core, swap(out_core, "c"), 1)
     attended_mine = attended_mine.reshape(2, seq_len, query_half)
     far_sent = send_rows(place_far, box["grad_far"], mask_far)
-    attended_mine, far_sent = tie((attended_mine, far_sent), "grad_rows_own", *coming(turns[1] + near[0]))
+    attended_mine, far_sent = tie((attended_mine, far_sent), "grad_rows_own", *coming(INWARD[1]))
+    fetch(INWARD[2], *coming(INWARD[1]))
     box["grad_rows_far"] = exchange(far_sent)
-    fetch(turns[2], *coming(turns[1]))
     attended_mine = mark(attended_mine)
     attended_other = swap(attended_mine, "c")
     attended = order_by(core, attended_mine[0], attended_other[1], 1)
     attended_next = order_by(core, attended_mine[1], attended_other[0], 1)
     hidden = token_f + dot(attended, out_full)
-    xn_second_f, norm_second_pull = jax.vjp(rms_apply, hidden, norm_moe)
-    xn_second = xn_second_f.astype(bf16)
+    xn_second = rms_apply(hidden, norm_moe).astype(bf16)
 
     def gating(values_b, mask):
         logits = dot(values_b, router_weight)
@@ -646,16 +720,16 @@
         return exponent / jnp.where(total > 0, total, 1.0)
 
     own_sent, xn_sent = tie(
-        (dot(place_own, xn_second).astype(bf16), xn_second), "grad_rows_far", *coming(turns[2])
-    )
-    fetch(turns[3], *coming(turns[2]))
+        (dot(place_own, xn_second).astype(bf16), xn_second), "grad_rows_far", *coming(INWARD[2])
+    )
+    fetch(INWARD[3], *coming(INWARD[2]))
     box["received_own"] = exchange(mark(own_sent))
-    fetch([0])
-    box["in", 0] = mark(tie(box["in", 0], *coming(turns[2])))
-    xn_sent = tie(xn_sent, "received_own", *coming(turns[3]))
+    fetch([(0, 0)])
+    box["in", (0, 0)] = mark(tie(box["in", (0, 0)], *coming(INWARD[2])))
+    xn_sent = tie(xn_sent, "received_own", *coming(INWARD[3]))
     box["xn_far"] = swap(xn_sent, "h")
-    fetch(near[2], *coming(turns[3]))
-    far_sent = tie(dot(place_far, box["xn_far"]).astype(bf16), *coming(near[2]))
+    fetch(INWARD[4], *coming(INWARD[3]))
+    far_sent = tie(dot(place_far, box["xn_far"]).astype(bf16), *coming(INWARD[4]))
     box["received_far"] = exchange(far_sent)
     gate_up_full, down_full = assemble()
     box["own"] = expert_part(
@@ -669,8 +743,6 @@
     box["far"] = expert_part(
         my_expert, box["received_far"], box["grad_rows_far"], router_weight, gate_up_full, down_full
     )
-    box["back_in_far"] = exchange(tie(box["far"][4], "back_in_own"))
-    box["d_in_sum_far"] = swap(t_dot(place_far, box["back_in_far"]).astype(bf16), "h")
     received, d_projected, inner, d_out = [
         list(pair)
         for pair in zip(
@@ -679,22 +751,30 @@
         )
     ]
     up_grad, down_grad = expert_weights(received, d_projected, inner, d_out)
-    give(stay, up_grad, down_grad)
-
-    d_in_sum = t_dot(place_own, box["back_in_own"])
-
-    def gate_columns(wide):
-        high = wide[:, model_width : model_width + half_experts]
-        low = wide[:, model_width + half_experts : model_width + 2 * half_experts]
-        return high.astype(f32) + low.astype(f32)
-
-    d_in_sum_far = box["d_in_sum_far"]
-    d_gates = both_columns(gate_columns(d_in_sum), gate_columns(d_in_sum_far))
-    d_in_sum = d_in_sum[:, :model_width] + d_in_sum_far[:, :model_width].astype(f32)
-    d_chosen = gates * (d_gates - jnp.sum(gates * d_gates, axis=-1, keepdims=True))
-    d_logits = d_chosen.astype(bf16)
-    router_local = t_dot(d_logits, xn_second)
-    d_xn_second = dot_t(d_logits, router_weight) + d_in_sum
+    sent, up_grad, down_grad = tie((box["far"][4], up_grad, down_grad), "back_in_own")
+    box["back_in_far"] = exchange(sent)
+    give(OUTWARD[0], up_grad, down_grad)
+    box["d_in_sum_far"] = swap(t_dot(place_far, box["back_in_far"]).astype(bf16), "h")
+    give([(0, 0)], up_grad, down_grad)
+
+    places = jnp.arange(EXPERTS) // local_count * (local_count // 2) + jnp.arange(EXPERTS) % (local_count // 2)
+    side = jnp.arange(EXPERTS) % local_count // (local_count // 2)
+    mine = (places[None, :] == jnp.arange(half_experts)[:, None]).astype(bf16)
+    spread = jnp.stack([mine * (side == half), mine * (side != half)]).astype(bf16)
+    d_hidden, d_hidden_b, d_attended, router_moe = token_backward(
+        core.reshape(1).astype(jnp.int32),
+        place_own,
+        box["back_in_own"],
+        box["d_in_sum_far"],
+        spread,
+        gates,
+        router_weight,
+        xn_second,
+        hidden,
+        norm_moe[None],
+        grad_output,
+        out_full,
+    )
 
     def mix(cube, gate, back):
         spread = jnp.where(cube, half_columns(gate, half).T[:, None, :], 0.0).reshape(rows, seq_len)
@@ -702,21 +782,15 @@
         low = (spread - high.astype(f32)).astype(bf16)
         return t_dot(high, back) + t_dot(low, back)
 
-    d_hidden_norm, gain_moe_local = norm_second_pull(d_xn_second)
-    d_hidden = grad_f + d_hidden_norm
-    d_hidden_b = d_hidden.astype(bf16)
-    d_hidden_b, out_far = together(d_hidden_b, box["far"][1])
+    d_hidden_b, up_grad, down_grad, out_far = together(d_hidden_b, up_grad, down_grad, box["far"][1])
+    give(OUTWARD[1], up_grad, down_grad)
     box["back_out_far"] = exchange(out_far)
-    d_hidden_b, up_grad, down_grad = together(d_hidden_b, up_grad, down_grad)
-    give(same, up_grad, down_grad)
-    d_attended = dot_t(d_hidden_b, out_full).astype(bf16)
 
     def halves(value):
         first, last = jnp.split(value, 2, axis=1)
         return jnp.where(core == 0, first, last), jnp.where(core == 0, last, first)
 
-    d_att_mine, d_att_send = halves(d_attended)
-    grad_heads = jnp.stack([d_att_mine, swap(d_att_send, "c")]).reshape(2 * seq_len, query_half)
+    grad_heads = jnp.stack([d_attended[0], swap(d_attended[1], "c")]).reshape(2 * seq_len, query_half)
     d_hid_mine, d_hid_send = halves(d_hidden_b)
     d_hid_next = swap(d_hid_send, "c")
     out_pair = (
@@ -726,31 +800,30 @@
     out_sends = scatter_sends(*out_pair)
     grad_heads = mark(grad_heads)
     grad_joint, d_xn_pair = attend_backward(joint, grad_heads, qkv_core, seq_len)
-    grad_joint, out_sends, out_own = tie((grad_joint, out_sends, box["own"][1]), "back_out_far")
+    grad_joint, out_own = tie((grad_joint, box["own"][1]), "back_out_far")
     box["back_out_own"] = exchange(out_own)
     moe_sent = mix(cube_far, gates_far, box["back_out_far"]).astype(bf16)
 
     def first_round(blocks):
-        blocks, sent = tie((blocks, moe_sent), "small", "back_out_own", *going(same))
+        blocks, sent, box["small"] = tie((blocks, moe_sent, box["small"]), *going(OUTWARD[0] + OUTWARD[1]))
+        give(OUTWARD[2], up_grad, down_grad)
         box["moe_far"] = swap(sent, "h")
-        give(opposite, up_grad, down_grad, *going(same))
-        box["small"] = sum_over(box["small"], ("c", "y", "r"))
-        return mark(blocks)
+        box["small"] = sum_over(box["small"], ("c", "y", "r", "h"))
+        return blocks
 
     def second_round(blocks):
-        blocks = tie(blocks, "small", "moe_far", *going(opposite))
-        give(across + level, up_grad, down_grad, *going(opposite))
-        box["small"] = sum_over(box["small"], ("h",))
-        return mark(blocks)
+        blocks = tie(blocks, "moe_far", *going(OUTWARD[2]))
+        give(OUTWARD[3], up_grad, down_grad, *going(OUTWARD[2]))
+        return blocks
 
     def third_round(blocks):
-        return tie(blocks, "small", *going(across + level))
+        return tie(blocks, *going(OUTWARD[3]))
 
     d_xn_first = d_xn_pair[:seq_len] + swap(d_xn_pair[seq_len:], "c")
     d_token_norm, gain_attn_local = norm_first_pull(d_xn_first)
     grad_tokens = d_hidden + d_token_norm
 
-    box["small"] = jnp.concatenate([router_local, gain_moe_local[None], gain_attn_local[None]], axis=0)
+    box["small"] = jnp.concatenate([router_moe[: EXPERTS + 1], gain_attn_local[None]], axis=0)
     qkv_grad, out_grad = scatter_products(
         ((xn_pair, grad_joint), out_pair),
         (scatter_sends(xn_pair, grad_joint), out_sends),

time: 835 us -> 802 us (0.960)
  matrix products: 55.1 us -> 26 us
  local copies, waits for them, and re-layouts: 135 us -> 110 us
  Pallas kernels: 73.8 us -> 95.1 us
  waiting for transfers between devices: 393 us -> 381 us
    dot_general x15 -> x5, matrix products: 34.5 us -> 10.9 us  [t_dot(): lax.dot_general(a, b, (((0,), (0,)), ((), ())), preferred_element_type=f32)]
    pallas_call x0 -> x3, Pallas kernels: none -> 21.4 us  [the longest x2 12.4 us: scatter_sends(): pl.pallas_call(functools.partial(product_kernel, width), grid_spec=pltpu....]
    ppermute x33, waiting for transfers between devices: 246 us -> 226 us  [swap(): return lax.ppermute(value, axis, [(i, i ^ bit) for i in range(size)])]
    ppermute x7, starting transfers between devices: 13 us -> 26.4 us  [give(): lax.ppermute(tie(piece, *names), FSDP, [(i, target(i, move)) for i in ran...]
    ppermute x33, starting transfers between devices: 48 us -> 36.1 us  [swap(): return lax.ppermute(value, axis, [(i, i ^ bit) for i in range(size)])]
    unnamed x253 -> x174, local copies, waits for them, and re-layouts: 15.7 us -> 16.7 us
  transfers between devices with their start and end apart: 55 -> 55, of which waited for: 28 -> 23; matrix products, arithmetic and copies ran while one was open for 25% -> 22% of each run, Pallas kernels for 9% -> 12%
where the time goes in v3:
time: 802 us; the launch traced here: 789 us
  waiting for transfers between devices  381 us (48%)
  starting transfers between devices  117 us (15%)
  local copies, waits for them, and re-layouts  110 us (14%)
  Pallas kernels  95.1 us (12%)
  other arithmetic  56.6 us (7%)
  matrix products  26 us (3%)
    ppermute x33, waiting for transfers between devices, swap(): return lax.ppermute(value, axis, [(i, i ^ bit) for i in range(size)])  226 us
    ppermute x7, waiting for transfers between devices, fetch(): lax.ppermute(tie(piece, *names), FSDP, [(i, target(i, move)) for i in ran...  135 us
    all_to_all x8, starting transfers between devices, exchange(): lax.all_to_all(buffer.reshape((half_devices, rows // half_devices) + shap...  38.7 us
    pallas_call x2, Pallas kernels, expert_part(): pl.pallas_call(expert_kernel, grid_spec=pltpu.PrefetchScalarGridSpec(num_...  37.6 us
    ppermute x33, starting transfers between devices, swap(): return lax.ppermute(value, axis, [(i, i ^ bit) for i in range(size)])  36.1 us
    ppermute x7, starting transfers between devices, give(): lax.ppermute(tie(piece, *names), FSDP, [(i, target(i, move)) for i in ran...  26.4 us
    all_to_all x8, waiting for transfers between devices, exchange(): lax.all_to_all(buffer.reshape((half_devices, rows // half_devices) + shap...  20.2 us
    pallas_call x1, Pallas kernels, expert_weights(): pl.pallas_call(expert_weights_kernel, grid=(steps,), in_specs=[columns(a)...  17.3 us
  transfers between devices with their start and end apart: 55, of which 23 were waited for; matrix products, arithmetic and copies ran while one was open for 22% of the time, Pallas kernels for 12%

profile of v3, /device:TPU:0, one launch (start us, length us, event | category | flops | bytes accessed | tf_op | source)
XLA Modules:
  0.0 789.3 jit_solution(7272767136866940603)
XLA Ops:
  3.1 4.1 collective-permute-start
  10.8 12.0 %collective-permute-done.10 = s32[256,4]{0,1:T(4,128)S(1)} collective-permute-done((s32[256,4]{0,1:T(4,128)S(1)}, s32[256,4]{0,1:T(4,128)S(1)}, u32[]{:S(2)}, u32[]{:S(2)}) %collective-permute-start.10) | collective-permute-done | bytes 4128 | tf_op jit(solution)/shard_map/ppermute | solution.py:48
  32.3 7.5 collective-permute-done.1
  57.5 7.1 collective-permute-done.2
  70.5 16.5 %collective-permute-done.5 = bf16[2,2,1,192,768]{4,3,2,1,0:T(8,128)(2,1)S(1)} collective-permute-done((bf16[2,2,1,192,768]{4,3,2,1,0:T(8,128)(2,1)S(1)}, bf16[2,2,1,192,768]{4,3,2,1,0:T(8,128)(2,1)S(1)}, u32[]{:S(2)}, u32[]{:S(2)}) %collective-permute-start.5) | collective-permute-done | bytes 1179680 | tf_op jit(solution)/shard_map/ppermute | solution.py:48
  87.5 7.8 collective-permute-done.3
  98.7 21.7 %collective-permute-done.9 = bf16[288,1536]{1,0:T(8,128)(2,1)S(1)} collective-permute-done((bf16[288,1536]{1,0:T(8,128)(2,1)S(1)}, bf16[288,1536]{1,0:T(8,128)(2,1)S(1)}, u32[]{:S(2)}, u32[]{:S(2)}) %collective-permute-start.9) | collective-permute-done | bytes 884768 | tf_op jit(solution)/shard_map/ppermute | solution.py:588
  121.4 4.5 all-to-all-start
  129.9 3.9 slice.146.weight_ref
  136.2 4.2 fusion.55
  140.3 7.1 shard_map.171
  149.8 27.9 %collective-permute-done.11 = bf16[288,1536]{1,0:T(8,128)(2,1)} collective-permute-done((bf16[288,1536]{1,0:T(8,128)(2,1)}, bf16[288,1536]{1,0:T(8,128)(2,1)}, u32[]{:S(2)}, u32[]{:S(2)}) %collective-permute-start.11) | collective-permute-done | bytes 884768 | tf_op jit(solution)/shard_map/ppermute | solution.py:588
  177.8 5.0 all-to-all-start.1
  190.2 4.0 multiply_reduce_fusion
  197.5 34.3 %collective-permute-done.15 = bf16[288,1536]{1,0:T(8,128)(2,1)} collective-permute-done((bf16[288,1536]{1,0:T(8,128)(2,1)S(1)}, bf16[288,1536]{1,0:T(8,128)(2,1)}, u32[]{:S(2)}, u32[]{:S(2)}) %collective-permute-start.15) | collective-permute-done | bytes 884768 | tf_op jit(solution)/shard_map/ppermute | solution.py:588
  234.4 4.4 all-to-all-start.2
  238.8 3.5 collective-permute-start.16
  246.5 51.0 %collective-permute-done.16 = bf16[288,1536]{1,0:T(8,128)(2,1)} collective-permute-done((bf16[288,1536]{1,0:T(8,128)(2,1)}, bf16[288,1536]{1,0:T(8,128)(2,1)}, u32[]{:S(2)}, u32[]{:S(2)}) %collective-permute-start.16) | collective-permute-done | bytes 884768 | tf_op jit(solution)/shard_map/ppermute | solution.py:588
  297.5 3.6 collective-permute-start.18
  305.5 28.9 %collective-permute-done.17 = bf16[256,1536]{1,0:T(8,128)(2,1)S(1)} collective-permute-done((bf16[256,1536]{1,0:T(8,128)(2,1)S(1)}, bf16[256,1536]{1,0:T(8,128)(2,1)S(1)}, u32[]{:S(2)}, u32[]{:S(2)}) %collective-permute-start.17) | collective-permute-done | bytes 786464 | tf_op jit(solution)/shard_map/ppermute | solution.py:48
  337.7 3.7 all-to-all-start.3
  358.9 18.8 %shard_map.175 = (bf16[768,768]{1,0:T(8,128)(2,1)}, bf16[768,1536]{1,0:T(8,128)(2,1)}, bf16[768,1536]{1,0:T(8,128)(2,1)}, bf16[768,1536]{1,0:T(8,128)(2,1)}, bf16[768,1664]{1,0:T(8,128)(2,1)}) custom-call(s32[2]{0:T(128)} %pad_add_fusion.expert_ref, bf16[768,1536]{1,0:T(8,128)(2,1)} %bitcast.28.rows_ref.x_own, bf16[768,1664]{1,0:T(8,128)(2,1)} %bitcast.12.grad_ref, ...), custom_call_target="tpu_custom_call" | custom-call | tf_op jit(solution)/shard_map/pallas_call | solution.py:401
  379.2 5.3 all-to-all-start.4
  384.4 18.8 %shard_map.176 = (bf16[768,768]{1,0:T(8,128)(2,1)}, bf16[768,1536]{1,0:T(8,128)(2,1)}, bf16[768,1536]{1,0:T(8,128)(2,1)}, bf16[768,1536]{1,0:T(8,128)(2,1)}, bf16[768,1664]{1,0:T(8,128)(2,1)}) custom-call(s32[2]{0:T(128)} %pad_add_fusion.expert_ref, bf16[768,1536]{1,0:T(8,128)(2,1)} %bitcast.187, bf16[768,1664]{1,0:T(8,128)(2,1)} %bitcast.24.grad_ref, ...), custom_call_target="tpu_custom_call" | custom-call | tf_op jit(solution)/shard_map/pallas_call | solution.py:401
  403.2 17.3 %shard_map.177 = (bf16[1536,1536]{1,0:T(8,128)(2,1)}, bf16[768,1536]{1,0:T(8,128)(2,1)}) custom-call(bf16[768,1536]{1,0:T(8,128)(2,1)} %bitcast.28.rows_ref.x_own, bf16[768,1536]{1,0:T(8,128)(2,1)} %bitcast.188, bf16[768,1536]{1,0:T(8,128)(2,1)} %get-tuple-element.153.p_own, bf16[768,1536]{1,0:T(8,128)(2,1)} %get-tuple-element.154.p_far, ...), custom_call_target="tpu_custom_call" | custom-call | tf_op jit(solution)/shard_map/pallas_call | solution.py:502
  420.6 5.4 all-to-all-start.5
  441.3 17.6 %all-to-all-done.5 = bf16[16,48,1664]{2,1,0:T(8,128)(2,1)} async-done(((bf16[16,48,1664]{2,1,0:T(8,128)(2,1)}), bf16[16,48,1664]{2,1,0:T(8,128)(2,1)}, u32[]{:S(2)}, u32[]{:S(2)}) %all-to-all-start.5) | async-done | bytes 2555936 | tf_op jit(solution)/shard_map/all_to_all | solution.py:636
  467.0 4.9 broadcast_in_dim.170
  473.0 43.3 %collective-permute-done.19.far_ref = bf16[256,1664]{1,0:T(8,128)(2,1)S(1)} collective-permute-done((bf16[256,1664]{1,0:T(8,128)(2,1)S(1)}, bf16[256,1664]{1,0:T(8,128)(2,1)S(1)}, u32[]{:S(2)}, u32[]{:S(2)}) %collective-permute-start.19) | collective-permute-done | bytes 852000 | tf_op jit(solution)/shard_map/ppermute | solution.py:48
  517.2 8.9 %shard_map.178 = (f32[256,1536]{1,0:T(8,128)}, bf16[256,1536]{1,0:T(8,128)(2,1)}, bf16[2,256,768]{2,1,0:T(8,128)(2,1)}, f32[40,1536]{1,0:T(8,128)}) custom-call(s32[1]{0:T(128)} %bitcast.20.core_ref, bf16[768,256]{1,0:T(8,128)(2,1)} %get-tuple-element.275.place_ref, bf16[768,1664]{1,0:T(8,128)(2,1)} %bitcast.38.back_ref, bf16[256,1664]{1,0:T(8,128)(2,1)} %copy-done.53, ...), custom_call_target="tpu_custom_call" | custom-call | tf_op jit(solution)/shard_map/pallas_call | solution.py:472
  528.0 6.3 all-to-all-start.6
  547.7 5.9 shard_map.182
  555.3 11.8 %shard_map.180 = (bf16[512,1024]{1,0:T(8,128)(2,1)}, f32[512,1536]{1,0:T(8,128)}) custom-call(bf16[512,1024]{1,0:T(8,128)(2,1)} %get-tuple-element.125.joint_ref, bf16[512,768]{1,0:T(8,128)(2,1)} %shard_map.179.grad_ref, bf16[1536,1024]{1,0:T(8,128)(2,1)} %slice.146.weight_ref), custom_call_target="tpu_custom_call" | custom-call | tf_op jit(solution)/shard_map/pallas_call | solution.py:317
  574.6 8.0 %collective-permute-done.25 = bf16[768,256]{1,0:T(8,128)(2,1)S(1)} collective-permute-done((bf16[768,256]{1,0:T(8,128)(2,1)S(1)}, bf16[768,256]{1,0:T(8,128)(2,1)S(1)}, u32[]{:S(2)}, u32[]{:S(2)}) %collective-permute-start.25) | collective-permute-done | bytes 393248 | tf_op jit(solution)/shard_map/ppermute | solution.py:48
  592.5 6.5 shard_map.181
  601.2 4.1 all-to-all-start.7
  613.3 6.5 collective-permute-done.24
  619.8 13.5 %collective-permute-start.33 = (bf16[288,1536]{1,0:T(8,128)(2,1)}, bf16[288,1536]{1,0:T(8,128)(2,1)}, u32[]{:S(2)}, u32[]{:S(2)}) collective-permute-start(bf16[288,1536]{1,0:T(8,128)(2,1)} %pad_maximum_fusion.17), channel_id=1, source_target_pairs={{0,5},{1,4},{2,7},{3,6},{4,1},{5,0},{6,3},{7,2},{8,13},{9,12},{10,... | collective-permute-start | bytes 2654216 | tf_op jit(solution)/shard_map/ppermute | solution.py:614
  639.0 4.0 pad_maximum_fusion.3
  642.9 4.2 reshape.414
  664.7 8.0 %collective-permute-done.35 = f32[34,1536]{1,0:T(8,128)S(1)} collective-permute-done((f32[34,1536]{1,0:T(8,128)S(1)}, f32[34,1536]{1,0:T(8,128)S(1)}, u32[]{:S(2)}, u32[]{:S(2)}) %collective-permute-start.35) | collective-permute-done | bytes 208928 | tf_op jit(solution)/shard_map/ppermute | solution.py:48
  673.0 16.4 %collective-permute-done.36 = f32[34,1536]{1,0:T(8,128)S(1)} collective-permute-done((f32[34,1536]{1,0:T(8,128)S(1)}, f32[34,1536]{1,0:T(8,128)S(1)}, u32[]{:S(2)}, u32[]{:S(2)}) %collective-permute-start.36) | collective-permute-done | bytes 208928 | tf_op jit(solution)/shard_map/ppermute | solution.py:48
  690.1 6.3 collective-permute-done.32
  696.5 3.9 collective-permute-start.39
  700.4 5.0 collective-permute-start.42
  710.9 44.8 %collective-permute-done.38 = f32[34,1536]{1,0:T(8,128)S(1)} collective-permute-done((f32[34,1536]{1,0:T(8,128)S(1)}, f32[34,1536]{1,0:T(8,128)S(1)}, u32[]{:S(2)}, u32[]{:S(2)}) %collective-permute-start.38) | collective-permute-done | bytes 208928 | tf_op jit(solution)/shard_map/ppermute | solution.py:48
  756.5 3.5 collective-permute-start.40
  760.7 9.0 %collective-permute-done.40 = bf16[1,1,1,192,896]{4,3,2,1,0:T(8,128)(2,1)S(1)} collective-permute-done((bf16[1,1,1,192,896]{4,3,2,1,0:T(8,128)(2,1)S(1)}, bf16[1,1,1,192,896]{4,3,2,1,0:T(8,128)(2,1)S(1)}, u32[]{:S(2)}, u32[]{:S(2)}) %collective-permute-start.40) | collective-permute-done | bytes 344096 | tf_op jit(solution)/shard_map/ppermute | solution.py:48
  (457 shorter events, 215.4 us)
Async XLA Ops:
  3.1 20.0 %collective-permute-start = (bf16[1,1,1,192,896]{4,3,2,1,0:T(8,128)(2,1)S(1)}, bf16[1,1,1,192,896]{4,3,2,1,0:T(8,128)(2,1)S(1)}, u32[]{:S(2)}, u32[]{:S(2)}) collective-permute-start(bf16[1,1,1,192,896]{4,3,2,1,0:T(8,128)(2,1)S(1)} %get-tuple-element.214), channel_id=1, source_target_pairs={{0,4},{4,0},{1,5},{5,1},{2,6},{6,2},{3,7},{7,3},{8,12},{12,8},{9,1... | collective-permute-start | bytes 1032200 | tf_op jit(solution)/shard_map/ppermute | solution.py:48
  7.7 22.2 %collective-permute-start.6 = (bf16[256,1536]{1,0:T(8,128)(2,1)S(1)}, bf16[256,1536]{1,0:T(8,128)(2,1)}, u32[]{:S(2)}, u32[]{:S(2)}) collective-permute-start(bf16[256,1536]{1,0:T(8,128)(2,1)S(1)} %fusion.5), channel_id=1, source_target_pairs={{0,8},{8,0},{1,9},{9,1},{2,10},{10,2},{3,11},{11,3},{4,12},{12,4},... | collective-permute-start | bytes 2359304 | tf_op jit(solution)/shard_map/ppermute | solution.py:48
  7.8 15.0 %collective-permute-start.10 = (s32[256,4]{0,1:T(4,128)S(1)}, s32[256,4]{0,1:T(4,128)S(1)}, u32[]{:S(2)}, u32[]{:S(2)}) collective-permute-start(s32[256,4]{0,1:T(4,128)S(1)} %copy-done.82), channel_id=1, source_target_pairs={{0,4},{4,0},{1,5},{5,1},{2,6},{6,2},{3,7},{7,3},{8,12},{12,8},{9,1... | collective-permute-start | bytes 12296 | tf_op jit(solution)/shard_map/ppermute | solution.py:48
  23.2 16.7 %collective-permute-start.1 = (bf16[2,1,1,192,896]{4,3,2,1,0:T(8,128)(2,1)S(1)}, bf16[2,1,1,192,896]{4,3,2,1,0:T(8,128)(2,1)S(1)}, u32[]{:S(2)}, u32[]{:S(2)}) collective-permute-start(bf16[2,1,1,192,896]{4,3,2,1,0:T(8,128)(2,1)S(1)} %constant_dynamic-update-slice_fusion.14), channel_id=1, source_target_pairs={{0,2},{1,3},{2,0},{3,1},{4,6},{5,7},{6,4},{7,5},{8,10},{9,11},{10,... | collective-permute-start | bytes 2064392 | tf_op jit(solution)/shard_map/ppermute | solution.py:48
  42.5 13.7 %collective-permute-start.4 = (bf16[2,2,1,192,384]{4,3,2,1,0:T(8,128)(2,1)S(1)}, bf16[2,2,1,192,384]{4,3,2,1,0:T(8,128)(2,1)S(1)}, u32[]{:S(2)}, u32[]{:S(2)}) collective-permute-start(bf16[2,2,1,192,384]{4,3,2,1,0:T(8,128)(2,1)S(1)} %get-tuple-element.255), channel_id=1, source_target_pairs={{0,16},{16,0},{1,17},{17,1},{2,18},{18,2},{3,19},{19,3},{4,20},{20... | collective-permute-start | bytes 1769480 | tf_op jit(solution)/shard_map/ppermute | solution.py:48
  44.1 20.5 %collective-permute-start.2 = (bf16[2,2,1,192,512]{4,3,2,1,0:T(8,128)(2,1)S(1)}, bf16[2,2,1,192,512]{4,3,2,1,0:T(8,128)(2,1)S(1)}, u32[]{:S(2)}, u32[]{:S(2)}) collective-permute-start(bf16[2,2,1,192,512]{4,3,2,1,0:T(8,128)(2,1)S(1)} %get-tuple-element.253), channel_id=1, source_target_pairs={{0,1},{1,0},{2,3},{3,2},{4,5},{5,4},{6,7},{7,6},{8,9},{9,8},{10,11... | collective-permute-start | bytes 2359304 | tf_op jit(solution)/shard_map/ppermute | solution.py:48
  45.7 53.1 %collective-permute-start.7 = (bf16[256,1536]{1,0:T(8,128)(2,1)S(1)}, bf16[256,1536]{1,0:T(8,128)(2,1)S(1)}, u32[]{:S(2)}, u32[]{:S(2)}) collective-permute-start(bf16[256,1536]{1,0:T(8,128)(2,1)S(1)} %copy-done.23), channel_id=1, source_target_pairs={{0,4},{4,0},{1,5},{5,1},{2,6},{6,2},{3,7},{7,3},{8,12},{12,8},{9,1... | collective-permute-start | bytes 2359304 | tf_op jit(solution)/shard_map/ppermute | solution.py:48
  49.6 49.1 %collective-permute-start.8 = (bf16[288,1536]{1,0:T(8,128)(2,1)S(1)}, bf16[288,1536]{1,0:T(8,128)(2,1)S(1)}, u32[]{:S(2)}, u32[]{:S(2)}) collective-permute-start(bf16[288,1536]{1,0:T(8,128)(2,1)S(1)} %pad_maximum_fusion.6), channel_id=1, source_target_pairs={{0,2},{1,3},{2,0},{3,1},{4,6},{5,7},{6,4},{7,5},{8,10},{9,11},{10,... | collective-permute-start | bytes 2654216 | tf_op jit(solution)/shard_map/ppermute | solution.py:588
  51.5 69.0 %collective-permute-start.9 = (bf16[288,1536]{1,0:T(8,128)(2,1)S(1)}, bf16[288,1536]{1,0:T(8,128)(2,1)S(1)}, u32[]{:S(2)}, u32[]{:S(2)}) collective-permute-start(bf16[288,1536]{1,0:T(8,128)(2,1)S(1)} %pad_maximum_fusion.7), channel_id=1, source_target_pairs={{0,4},{1,5},{2,6},{3,7},{4,0},{5,1},{6,2},{7,3},{8,12},{9,13},{10,... | collective-permute-start | bytes 2654216 | tf_op jit(solution)/shard_map/ppermute | solution.py:588
  56.2 30.8 %collective-permute-start.5 = (bf16[2,2,1,192,768]{4,3,2,1,0:T(8,128)(2,1)S(1)}, bf16[2,2,1,192,768]{4,3,2,1,0:T(8,128)(2,1)S(1)}, u32[]{:S(2)}, u32[]{:S(2)}) collective-permute-start(bf16[2,2,1,192,768]{4,3,2,1,0:T(8,128)(2,1)S(1)} %constant_dynamic-update-slice_fusion.6), channel_id=1, source_target_pairs={{0,1},{1,0},{2,3},{3,2},{4,5},{5,4},{6,7},{7,6},{8,9},{9,8},{10,11... | collective-permute-start | bytes 3538952 | tf_op jit(solution)/shard_map/ppermute | solution.py:48
  64.7 30.6 %collective-permute-start.3 = (bf16[2,2,2,192,512]{4,3,2,1,0:T(8,128)(2,1)S(1)}, bf16[2,2,2,192,512]{4,3,2,1,0:T(8,128)(2,1)S(1)}, u32[]{:S(2)}, u32[]{:S(2)}) collective-permute-start(bf16[2,2,2,192,512]{4,3,2,1,0:T(8,128)(2,1)S(1)} %constant_dynamic-update-slice_fusion.10), channel_id=1, source_target_pairs={{0,16},{16,0},{1,17},{17,1},{2,18},{18,2},{3,19},{19,3},{4,20},{20... | collective-permute-start | bytes 4718600 | tf_op jit(solution)/shard_map/ppermute | solution.py:48
  121.4 56.4 %all-to-all-start = ((bf16[16,48,1664]{2,1,0:T(8,128)(2,1)}), bf16[16,48,1664]{2,1,0:T(8,128)(2,1)}, u32[]{:S(2)}, u32[]{:S(2)}) async-start(bf16[16,48,1664]{2,1,0:T(8,128)(2,1)} %bitcast.11), calls=%async_computation | async-start | bytes 5111808 | tf_op jit(solution)/shard_map/all_to_all | solution.py:636
  125.8 51.9 %collective-permute-start.11 = (bf16[288,1536]{1,0:T(8,128)(2,1)}, bf16[288,1536]{1,0:T(8,128)(2,1)}, u32[]{:S(2)}, u32[]{:S(2)}) collective-permute-start(bf16[288,1536]{1,0:T(8,128)(2,1)} %pad_maximum_fusion.8), channel_id=1, source_target_pairs={{0,6},{1,7},{2,4},{3,5},{4,2},{5,3},{6,0},{7,1},{8,14},{9,15},{10,... | collective-permute-start | bytes 2654216 | tf_op jit(solution)/shard_map/ppermute | solution.py:588
  129.3 48.4 %collective-permute-start.12 = (bf16[288,1536]{1,0:T(8,128)(2,1)}, bf16[288,1536]{1,0:T(8,128)(2,1)}, u32[]{:S(2)}, u32[]{:S(2)}) collective-permute-start(bf16[288,1536]{1,0:T(8,128)(2,1)} %pad_maximum_fusion.9), channel_id=1, source_target_pairs={{0,1},{1,0},{2,3},{3,2},{4,5},{5,4},{6,7},{7,6},{8,9},{9,8},{10,11... | collective-permute-start | bytes 2654216 | tf_op jit(solution)/shard_map/ppermute | solution.py:588
  140.3 42.9 %collective-permute-start.14 = (bf16[1536,768]{1,0:T(8,128)(2,1)}, bf16[1536,768]{1,0:T(8,128)(2,1)}, u32[]{:S(2)}, u32[]{:S(2)}) collective-permute-start(bf16[1536,768]{1,0:T(8,128)(2,1)} %get-tuple-element.215), channel_id=1, source_target_pairs={{0,8},{8,0},{1,9},{9,1},{2,10},{10,2},{3,11},{11,3},{4,12},{12,4},... | collective-permute-start | bytes 7077896 | tf_op jit(solution)/shard_map/ppermute | solution.py:48
  177.8 56.6 %all-to-all-start.1 = ((bf16[16,48,1664]{2,1,0:T(8,128)(2,1)}), bf16[16,48,1664]{2,1,0:T(8,128)(2,1)}, u32[]{:S(2)}, u32[]{:S(2)}) async-start(bf16[16,48,1664]{2,1,0:T(8,128)(2,1)} %bitcast.23), calls=%async_computation.1 | async-start | bytes 5111808 | tf_op jit(solution)/shard_map/all_to_all | solution.py:636
  186.6 45.2 %collective-permute-start.15 = (bf16[288,1536]{1,0:T(8,128)(2,1)S(1)}, bf16[288,1536]{1,0:T(8,128)(2,1)}, u32[]{:S(2)}, u32[]{:S(2)}) collective-permute-start(bf16[288,1536]{1,0:T(8,128)(2,1)S(1)} %copy-done.47), channel_id=1, source_target_pairs={{0,5},{1,4},{2,7},{3,6},{4,1},{5,0},{6,3},{7,2},{8,13},{9,12},{10,... | collective-permute-start | bytes 2654216 | tf_op jit(solution)/shard_map/ppermute | solution.py:588
  234.4 63.1 %all-to-all-start.2 = ((bf16[16,48,1536]{2,1,0:T(8,128)(2,1)}), bf16[16,48,1536]{2,1,0:T(8,128)(2,1)}, u32[]{:S(2)}, u32[]{:S(2)}) async-start(bf16[16,48,1536]{2,1,0:T(8,128)(2,1)} %bitcast.190), calls=%async_computation.2 | async-start | bytes 4718592 | tf_op jit(solution)/shard_map/all_to_all | solution.py:636
  238.8 58.7 %collective-permute-start.16 = (bf16[288,1536]{1,0:T(8,128)(2,1)}, bf16[288,1536]{1,0:T(8,128)(2,1)}, u32[]{:S(2)}, u32[]{:S(2)}) collective-permute-start(bf16[288,1536]{1,0:T(8,128)(2,1)} %pad_maximum_fusion.11), channel_id=1, source_target_pairs={{0,7},{1,6},{2,5},{3,4},{4,3},{5,2},{6,1},{7,0},{8,15},{9,14},{10,... | collective-permute-start | bytes 2654216 | tf_op jit(solution)/shard_map/ppermute | solution.py:588
  297.5 36.9 %collective-permute-start.17 = (bf16[256,1536]{1,0:T(8,128)(2,1)S(1)}, bf16[256,1536]{1,0:T(8,128)(2,1)S(1)}, u32[]{:S(2)}, u32[]{:S(2)}) collective-permute-start(bf16[256,1536]{1,0:T(8,128)(2,1)S(1)} %copy-done.8), channel_id=1, source_target_pairs={{0,4},{4,0},{1,5},{5,1},{2,6},{6,2},{3,7},{7,3},{8,12},{12,8},{9,1... | collective-permute-start | bytes 2359304 | tf_op jit(solution)/shard_map/ppermute | solution.py:48
  297.5 40.2 %collective-permute-start.18 = (bf16[288,1536]{1,0:T(8,128)(2,1)}, bf16[288,1536]{1,0:T(8,128)(2,1)}, u32[]{:S(2)}, u32[]{:S(2)}) collective-permute-start(bf16[288,1536]{1,0:T(8,128)(2,1)} %pad_maximum_fusion.13), channel_id=1, source_target_pairs={{0,3},{1,2},{2,1},{3,0},{4,7},{5,6},{6,5},{7,4},{8,11},{9,10},{10,... | collective-permute-start | bytes 2654216 | tf_op jit(solution)/shard_map/ppermute | solution.py:588
  337.7 40.1 %all-to-all-start.3 = ((bf16[16,48,1536]{2,1,0:T(8,128)(2,1)}), bf16[16,48,1536]{2,1,0:T(8,128)(2,1)S(1)}, u32[]{:S(2)}, u32[]{:S(2)}) async-start(bf16[16,48,1536]{2,1,0:T(8,128)(2,1)} %bitcast.189), calls=%async_computation.3 | async-start | bytes 4718592 | tf_op jit(solution)/shard_map/all_to_all | solution.py:636
  379.2 41.3 %all-to-all-start.4 = ((bf16[16,48,1664]{2,1,0:T(8,128)(2,1)}), bf16[16,48,1664]{2,1,0:T(8,128)(2,1)}, u32[]{:S(2)}, u32[]{:S(2)}) async-start(bf16[16,48,1664]{2,1,0:T(8,128)(2,1)} %bitcast.194), calls=%async_computation.4 | async-start | bytes 5111808 | tf_op jit(solution)/shard_map/all_to_all | solution.py:636
  420.6 38.4 %all-to-all-start.5 = ((bf16[16,48,1664]{2,1,0:T(8,128)(2,1)}), bf16[16,48,1664]{2,1,0:T(8,128)(2,1)}, u32[]{:S(2)}, u32[]{:S(2)}) async-start(bf16[16,48,1664]{2,1,0:T(8,128)(2,1)} %bitcast.39), calls=%async_computation.5 | async-start | bytes 5111808 | tf_op jit(solution)/shard_map/all_to_all | solution.py:636
  436.3 213.4 %collective-permute-start.27 = (bf16[288,1536]{1,0:T(8,128)(2,1)}, bf16[288,1536]{1,0:T(8,128)(2,1)}, u32[]{:S(2)}, u32[]{:S(2)}) collective-permute-start(bf16[288,1536]{1,0:T(8,128)(2,1)} %pad_maximum_fusion.14), channel_id=1, source_target_pairs={{0,2},{1,3},{2,4},{3,5},{4,6},{5,7},{6,0},{7,1},{8,10},{9,11},{10,... | collective-permute-start | bytes 2654216 | tf_op jit(solution)/shard_map/ppermute | solution.py:614
  439.2 210.6 %collective-permute-start.28 = (bf16[288,1536]{1,0:T(8,128)(2,1)}, bf16[288,1536]{1,0:T(8,128)(2,1)}, u32[]{:S(2)}, u32[]{:S(2)}) collective-permute-start(bf16[288,1536]{1,0:T(8,128)(2,1)} %pad_maximum_fusion.15), channel_id=1, source_target_pairs={{0,6},{1,7},{2,0},{3,1},{4,2},{5,3},{6,4},{7,5},{8,14},{9,15},{10,... | collective-permute-start | bytes 2654216 | tf_op jit(solution)/shard_map/ppermute | solution.py:614
  461.6 54.7 %collective-permute-start.19 = (bf16[256,1664]{1,0:T(8,128)(2,1)S(1)}, bf16[256,1664]{1,0:T(8,128)(2,1)S(1)}, u32[]{:S(2)}, u32[]{:S(2)}) collective-permute-start(bf16[256,1664]{1,0:T(8,128)(2,1)S(1)} %fusion.1), channel_id=1, source_target_pairs={{0,4},{4,0},{1,5},{5,1},{2,6},{6,2},{3,7},{7,3},{8,12},{12,8},{9,1... | collective-permute-start | bytes 2555912 | tf_op jit(solution)/shard_map/ppermute | solution.py:48
  528.0 14.8 %collective-permute-start.20 = (bf16[256,768]{1,0:T(8,128)(2,1)}, bf16[256,768]{1,0:T(8,128)(2,1)}, u32[]{:S(2)}, u32[]{:S(2)}) collective-permute-start(bf16[256,768]{1,0:T(8,128)(2,1)} %get-tuple-element.264), channel_id=1, source_target_pairs={{0,8},{8,0},{1,9},{9,1},{2,10},{10,2},{3,11},{11,3},{4,12},{12,4},... | collective-permute-start | bytes 1179656 | tf_op jit(solution)/shard_map/ppermute | solution.py:48
  528.0 64.5 %all-to-all-start.6 = ((bf16[16,48,1536]{2,1,0:T(8,128)(2,1)}), bf16[16,48,1536]{2,1,0:T(8,128)(2,1)}, u32[]{:S(2)}, u32[]{:S(2)}) async-start(bf16[16,48,1536]{2,1,0:T(8,128)(2,1)} %bitcast.196), calls=%async_computation.6 | async-start | bytes 4718592 | tf_op jit(solution)/shard_map/all_to_all | solution.py:636
  553.6 32.8 %collective-permute-start.23 = (bf16[1536,256]{1,0:T(8,128)(2,1)}, bf16[1536,256]{1,0:T(8,128)(2,1)}, u32[]{:S(2)}, u32[]{:S(2)}) collective-permute-start(bf16[1536,256]{1,0:T(8,128)(2,1)} %get-tuple-element.178), channel_id=1, source_target_pairs={{0,16},{16,0},{1,17},{17,1},{2,18},{18,2},{3,19},{19,3},{4,20},{20... | collective-permute-start | bytes 2359304 | tf_op jit(solution)/shard_map/ppermute | solution.py:48
  570.0 19.5 %collective-permute-start.26 = (f32[256,1536]{1,0:T(8,128)}, f32[256,1536]{1,0:T(8,128)S(1)}, u32[]{:S(2)}, u32[]{:S(2)}) collective-permute-start(f32[256,1536]{1,0:T(8,128)} %slice.172), channel_id=1, source_target_pairs={{0,8},{8,0},{1,9},{9,1},{2,10},{10,2},{3,11},{11,3},{4,12},{12,4},... | collective-permute-start | bytes 4718600 | tf_op jit(solution)/shard_map/ppermute | solution.py:48
  571.0 11.5 %collective-permute-start.25 = (bf16[768,256]{1,0:T(8,128)(2,1)S(1)}, bf16[768,256]{1,0:T(8,128)(2,1)S(1)}, u32[]{:S(2)}, u32[]{:S(2)}) collective-permute-start(bf16[768,256]{1,0:T(8,128)(2,1)S(1)} %copy-done.83), channel_id=1, source_target_pairs={{0,1},{1,0},{2,3},{3,2},{4,5},{5,4},{6,7},{7,6},{8,9},{9,8},{10,11... | collective-permute-start | bytes 1179656 | tf_op jit(solution)/shard_map/ppermute | solution.py:48
  582.5 67.3 %collective-permute-start.29 = (bf16[288,1536]{1,0:T(8,128)(2,1)}, bf16[288,1536]{1,0:T(8,128)(2,1)}, u32[]{:S(2)}, u32[]{:S(2)}) collective-permute-start(bf16[288,1536]{1,0:T(8,128)(2,1)} %pad_maximum_fusion.16), channel_id=1, source_target_pairs={{0,4},{1,5},{2,6},{3,7},{4,0},{5,1},{6,2},{7,3},{8,12},{9,13},{10,... | collective-permute-start | bytes 2654216 | tf_op jit(solution)/shard_map/ppermute | solution.py:614
  599.0 20.8 %collective-permute-start.24 = (bf16[768,512]{1,0:T(8,128)(2,1)}, bf16[768,512]{1,0:T(8,128)(2,1)}, u32[]{:S(2)}, u32[]{:S(2)}) collective-permute-start(bf16[768,512]{1,0:T(8,128)(2,1)} %get-tuple-element.180), channel_id=1, source_target_pairs={{0,1},{1,0},{2,3},{3,2},{4,5},{5,4},{6,7},{7,6},{8,9},{9,8},{10,11... | collective-permute-start | bytes 2359304 | tf_op jit(solution)/shard_map/ppermute | solution.py:48
  601.2 183.0 %all-to-all-start.7 = ((bf16[16,48,1536]{2,1,0:T(8,128)(2,1)}), bf16[16,48,1536]{2,1,0:T(8,128)(2,1)S(1)}, u32[]{:S(2)}, u32[]{:S(2)}) async-start(bf16[16,48,1536]{2,1,0:T(8,128)(2,1)} %bitcast.195), calls=%async_computation.7 | async-start | bytes 4718592 | tf_op jit(solution)/shard_map/all_to_all | solution.py:636
  605.4 41.8 %collective-permute-start.21 = (bf16[1536,256]{1,0:T(8,128)(2,1)}, bf16[1536,256]{1,0:T(8,128)(2,1)}, u32[]{:S(2)}, u32[]{:S(2)}) collective-permute-start(bf16[1536,256]{1,0:T(8,128)(2,1)} %get-tuple-element.175), channel_id=1, source_target_pairs={{0,16},{16,0},{1,17},{17,1},{2,18},{18,2},{3,19},{19,3},{4,20},{20... | collective-permute-start | bytes 2359304 | tf_op jit(solution)/shard_map/ppermute | solution.py:48
  619.8 70.2 %collective-permute-start.33 = (bf16[288,1536]{1,0:T(8,128)(2,1)}, bf16[288,1536]{1,0:T(8,128)(2,1)}, u32[]{:S(2)}, u32[]{:S(2)}) collective-permute-start(bf16[288,1536]{1,0:T(8,128)(2,1)} %pad_maximum_fusion.17), channel_id=1, source_target_pairs={{0,5},{1,4},{2,7},{3,6},{4,1},{5,0},{6,3},{7,2},{8,13},{9,12},{10,... | collective-permute-start | bytes 2654216 | tf_op jit(solution)/shard_map/ppermute | solution.py:614
  651.0 21.8 %collective-permute-start.31 = (bf16[2,2,1,192,384]{4,3,2,1,0:T(8,128)(2,1)S(1)}, bf16[2,2,1,192,384]{4,3,2,1,0:T(8,128)(2,1)S(1)}, u32[]{:S(2)}, u32[]{:S(2)}) collective-permute-start(bf16[2,2,1,192,384]{4,3,2,1,0:T(8,128)(2,1)S(1)} %dynamic-slice_convert_fusion.2), channel_id=1, source_target_pairs={{0,16},{16,0},{1,17},{17,1},{2,18},{18,2},{3,19},{19,3},{4,20},{20... | collective-permute-start | bytes 1769480 | tf_op jit(solution)/shard_map/ppermute | solution.py:48
  651.7 37.8 %collective-permute-start.30 = (bf16[2,2,1,192,512]{4,3,2,1,0:T(8,128)(2,1)S(1)}, bf16[2,2,1,192,512]{4,3,2,1,0:T(8,128)(2,1)S(1)}, u32[]{:S(2)}, u32[]{:S(2)}) collective-permute-start(bf16[2,2,1,192,512]{4,3,2,1,0:T(8,128)(2,1)S(1)} %dynamic-slice_convert_fusion), channel_id=1, source_target_pairs={{0,1},{1,0},{2,3},{3,2},{4,5},{5,4},{6,7},{7,6},{8,9},{9,8},{10,11... | collective-permute-start | bytes 2359304 | tf_op jit(solution)/shard_map/ppermute | solution.py:48
  651.8 44.5 %collective-permute-start.32 = (bf16[256,1536]{1,0:T(8,128)(2,1)S(1)}, bf16[256,1536]{1,0:T(8,128)(2,1)S(1)}, u32[]{:S(2)}, u32[]{:S(2)}) collective-permute-start(bf16[256,1536]{1,0:T(8,128)(2,1)S(1)} %copy-done.56), channel_id=1, source_target_pairs={{0,4},{4,0},{1,5},{5,1},{2,6},{6,2},{3,7},{7,3},{8,12},{12,8},{9,1... | collective-permute-start | bytes 2359304 | tf_op jit(solution)/shard_map/ppermute | solution.py:48
  672.7 16.7 %collective-permute-start.36 = (f32[34,1536]{1,0:T(8,128)S(1)}, f32[34,1536]{1,0:T(8,128)S(1)}, u32[]{:S(2)}, u32[]{:S(2)}) collective-permute-start(f32[34,1536]{1,0:T(8,128)S(1)} %add.719), channel_id=1, source_target_pairs={{0,1},{1,0},{2,3},{3,2},{4,5},{5,4},{6,7},{7,6},{8,9},{9,8},{10,11... | collective-permute-start | bytes 626696 | tf_op jit(solution)/shard_map/ppermute | solution.py:48
  689.4 19.0 %collective-permute-start.37 = (f32[34,1536]{1,0:T(8,128)S(1)}, f32[34,1536]{1,0:T(8,128)S(1)}, u32[]{:S(2)}, u32[]{:S(2)}) collective-permute-start(f32[34,1536]{1,0:T(8,128)S(1)} %add.720), channel_id=1, source_target_pairs={{0,2},{1,3},{2,0},{3,1},{4,6},{5,7},{6,4},{7,5},{8,10},{9,11},{10,... | collective-permute-start | bytes 626696 | tf_op jit(solution)/shard_map/ppermute | solution.py:48
  696.5 59.9 %collective-permute-start.39 = (bf16[2,1,1,192,896]{4,3,2,1,0:T(8,128)(2,1)S(1)}, bf16[2,1,1,192,896]{4,3,2,1,0:T(8,128)(2,1)S(1)}, u32[]{:S(2)}, u32[]{:S(2)}) collective-permute-start(bf16[2,1,1,192,896]{4,3,2,1,0:T(8,128)(2,1)S(1)} %dynamic-slice_convert_fusion.1), channel_id=1, source_target_pairs={{0,2},{1,3},{2,0},{3,1},{4,6},{5,7},{6,4},{7,5},{8,10},{9,11},{10,... | collective-permute-start | bytes 2064392 | tf_op jit(solution)/shard_map/ppermute | solution.py:48
  700.4 69.4 %collective-permute-start.41 = (bf16[288,1536]{1,0:T(8,128)(2,1)S(1)}, bf16[288,1536]{1,0:T(8,128)(2,1)S(1)}, u32[]{:S(2)}, u32[]{:S(2)}) collective-permute-start(bf16[288,1536]{1,0:T(8,128)(2,1)S(1)} %copy-done.44), channel_id=1, source_target_pairs={{0,3},{1,2},{2,5},{3,4},{4,7},{5,6},{6,1},{7,0},{8,11},{9,10},{10,... | collective-permute-start | bytes 2654216 | tf_op jit(solution)/shard_map/ppermute | solution.py:614
  700.4 69.4 %collective-permute-start.42 = (bf16[288,1536]{1,0:T(8,128)(2,1)S(1)}, bf16[288,1536]{1,0:T(8,128)(2,1)S(1)}, u32[]{:S(2)}, u32[]{:S(2)}) collective-permute-start(bf16[288,1536]{1,0:T(8,128)(2,1)S(1)} %copy-done.45), channel_id=1, source_target_pairs={{0,7},{1,6},{2,1},{3,0},{4,3},{5,2},{6,5},{7,4},{8,15},{9,14},{10,... | collective-permute-start | bytes 2654216 | tf_op jit(solution)/shard_map/ppermute | solution.py:614
  705.4 64.4 %collective-permute-start.43 = (bf16[288,1536]{1,0:T(8,128)(2,1)S(1)}, bf16[288,1536]{1,0:T(8,128)(2,1)S(1)}, u32[]{:S(2)}, u32[]{:S(2)}) collective-permute-start(bf16[288,1536]{1,0:T(8,128)(2,1)S(1)} %copy-done.46), channel_id=1, source_target_pairs={{0,1},{1,0},{2,3},{3,2},{4,5},{5,4},{6,7},{7,6},{8,9},{9,8},{10,11... | collective-permute-start | bytes 2654216 | tf_op jit(solution)/shard_map/ppermute | solution.py:614
  708.4 47.3 %collective-permute-start.38 = (f32[34,1536]{1,0:T(8,128)S(1)}, f32[34,1536]{1,0:T(8,128)S(1)}, u32[]{:S(2)}, u32[]{:S(2)}) collective-permute-start(f32[34,1536]{1,0:T(8,128)S(1)} %add.721), channel_id=1, source_target_pairs={{0,4},{4,0},{1,5},{5,1},{2,6},{6,2},{3,7},{7,3},{8,12},{12,8},{9,1... | collective-permute-start | bytes 626696 | tf_op jit(solution)/shard_map/ppermute | solution.py:48
  756.5 13.2 %collective-permute-start.40 = (bf16[1,1,1,192,896]{4,3,2,1,0:T(8,128)(2,1)S(1)}, bf16[1,1,1,192,896]{4,3,2,1,0:T(8,128)(2,1)S(1)}, u32[]{:S(2)}, u32[]{:S(2)}) collective-permute-start(bf16[1,1,1,192,896]{4,3,2,1,0:T(8,128)(2,1)S(1)} %dynamic-slice_convert_fusion.3), channel_id=1, source_target_pairs={{0,4},{4,0},{1,5},{5,1},{2,6},{6,2},{3,7},{7,3},{8,12},{12,8},{9,1... | collective-permute-start | bytes 1032200 | tf_op jit(solution)/shard_map/ppermute | solution.py:48
  (91 other events, 585.2 us)

commit v4 on v3

--- a/solution.py
+++ b/solution.py
@@ -18,7 +18,7 @@
 VMEM_LIMIT = 56 * 1024 * 1024
 EXTRA = 128
 INWARD = [[(-1, 0), (-2, 0)], [(-3, 0), (0, 1)], [(-2, 1)], [(-3, 1)], [(-1, 1)]]
-OUTWARD = [[(1, 0), (3, 0)], [(2, 0)], [(2, 1)], [(1, 1), (3, 1), (0, 1)]]
+OUTWARD = [[(1, 0)], [(3, 0), (2, 0)], [(2, 1)], [(1, 1), (3, 1), (0, 1)]]
 EXPERT = ("y", "c")
 FSDP = ("h", "r")
 BOTH = EXPERT + FSDP
@@ -784,7 +784,7 @@
 
     d_hidden_b, up_grad, down_grad, out_far = together(d_hidden_b, up_grad, down_grad, box["far"][1])
     give(OUTWARD[1], up_grad, down_grad)
-    box["back_out_far"] = exchange(out_far)
+    box["back_out_far"] = exchange(mark(out_far))
 
     def halves(value):
         first, last = jnp.split(value, 2, axis=1)

time: 802 us -> 797 us (level)
    unnamed x174 -> x180, local copies, waits for them, and re-layouts: 16.7 us -> 17.4 us
  transfers between devices with their start and end apart: 55 -> 55, of which waited for: 23 -> 22; matrix products, arithmetic and copies ran while one was open for 22% -> 22% of each run, Pallas kernels for 12% -> 12%
where the time goes in v4:
time: 797 us; the launch traced here: 784 us
  waiting for transfers between devices  381 us (48%)
  starting transfers between devices  114 us (14%)
  local copies, waits for them, and re-layouts  110 us (14%)
  Pallas kernels  95 us (12%)
  other arithmetic  55.3 us (7%)
  matrix products  26 us (3%)
    ppermute x33, waiting for transfers between devices, swap(): return lax.ppermute(value, axis, [(i, i ^ bit) for i in range(size)])  224 us
    ppermute x7, waiting for transfers between devices, fetch(): lax.ppermute(tie(piece, *names), FSDP, [(i, target(i, move)) for i in ran...  135 us
    pallas_call x2, Pallas kernels, expert_part(): pl.pallas_call(expert_kernel, grid_spec=pltpu.PrefetchScalarGridSpec(num_...  37.6 us
    all_to_all x8, starting transfers between devices, exchange(): lax.all_to_all(buffer.reshape((half_devices, rows // half_devices) + shap...  37.1 us
    ppermute x33, starting transfers between devices, swap(): return lax.ppermute(value, axis, [(i, i ^ bit) for i in range(size)])  34.8 us
    ppermute x7, starting transfers between devices, give(): lax.ppermute(tie(piece, *names), FSDP, [(i, target(i, move)) for i in ran...  26.2 us
    all_to_all x8, waiting for transfers between devices, exchange(): lax.all_to_all(buffer.reshape((half_devices, rows // half_devices) + shap...  22.4 us
    unnamed x180, local copies, waits for them, and re-layouts  17.4 us
  transfers between devices with their start and end apart: 55, of which 22 were waited for; matrix products, arithmetic and copies ran while one was open for 22% of the time, Pallas kernels for 12%

profile of v4, /device:TPU:0, one launch (start us, length us, event | category | flops | bytes accessed | tf_op | source)
XLA Modules:
  0.0 784.5 jit_solution(9007425407145609599)
XLA Ops:
  3.1 4.1 collective-permute-start
  10.7 12.1 %collective-permute-done.10 = s32[256,4]{0,1:T(4,128)S(1)} collective-permute-done((s32[256,4]{0,1:T(4,128)S(1)}, s32[256,4]{0,1:T(4,128)S(1)}, u32[]{:S(2)}, u32[]{:S(2)}) %collective-permute-start.10) | collective-permute-done | bytes 4128 | tf_op jit(solution)/shard_map/ppermute | solution.py:48
  32.3 7.5 collective-permute-done.1
  57.5 7.1 collective-permute-done.2
  70.4 16.6 %collective-permute-done.5 = bf16[2,2,1,192,768]{4,3,2,1,0:T(8,128)(2,1)S(1)} collective-permute-done((bf16[2,2,1,192,768]{4,3,2,1,0:T(8,128)(2,1)S(1)}, bf16[2,2,1,192,768]{4,3,2,1,0:T(8,128)(2,1)S(1)}, u32[]{:S(2)}, u32[]{:S(2)}) %collective-permute-start.5) | collective-permute-done | bytes 1179680 | tf_op jit(solution)/shard_map/ppermute | solution.py:48
  87.5 7.8 collective-permute-done.3
  98.7 21.7 %collective-permute-done.9 = bf16[288,1536]{1,0:T(8,128)(2,1)S(1)} collective-permute-done((bf16[288,1536]{1,0:T(8,128)(2,1)S(1)}, bf16[288,1536]{1,0:T(8,128)(2,1)S(1)}, u32[]{:S(2)}, u32[]{:S(2)}) %collective-permute-start.9) | collective-permute-done | bytes 884768 | tf_op jit(solution)/shard_map/ppermute | solution.py:588
  121.4 4.5 all-to-all-start
  125.8 3.5 collective-permute-start.11
  129.9 3.9 slice.146.weight_ref
  136.2 4.2 fusion.55
  140.4 7.1 shard_map.171
  149.9 27.8 %collective-permute-done.11 = bf16[288,1536]{1,0:T(8,128)(2,1)} collective-permute-done((bf16[288,1536]{1,0:T(8,128)(2,1)}, bf16[288,1536]{1,0:T(8,128)(2,1)}, u32[]{:S(2)}, u32[]{:S(2)}) %collective-permute-start.11) | collective-permute-done | bytes 884768 | tf_op jit(solution)/shard_map/ppermute | solution.py:588
  177.8 5.0 all-to-all-start.1
  183.3 3.4 constant_dynamic-update-slice_fusion.2.weight_ref
  190.3 4.0 multiply_reduce_fusion
  197.6 34.2 %collective-permute-done.15 = bf16[288,1536]{1,0:T(8,128)(2,1)} collective-permute-done((bf16[288,1536]{1,0:T(8,128)(2,1)S(1)}, bf16[288,1536]{1,0:T(8,128)(2,1)}, u32[]{:S(2)}, u32[]{:S(2)}) %collective-permute-start.15) | collective-permute-done | bytes 884768 | tf_op jit(solution)/shard_map/ppermute | solution.py:588
  234.4 4.4 all-to-all-start.2
  246.5 51.0 %collective-permute-done.16 = bf16[288,1536]{1,0:T(8,128)(2,1)} collective-permute-done((bf16[288,1536]{1,0:T(8,128)(2,1)}, bf16[288,1536]{1,0:T(8,128)(2,1)}, u32[]{:S(2)}, u32[]{:S(2)}) %collective-permute-start.16) | collective-permute-done | bytes 884768 | tf_op jit(solution)/shard_map/ppermute | solution.py:588
  297.5 3.6 collective-permute-start.18
  305.5 28.9 %collective-permute-done.17 = bf16[256,1536]{1,0:T(8,128)(2,1)S(1)} collective-permute-done((bf16[256,1536]{1,0:T(8,128)(2,1)S(1)}, bf16[256,1536]{1,0:T(8,128)(2,1)S(1)}, u32[]{:S(2)}, u32[]{:S(2)}) %collective-permute-start.17) | collective-permute-done | bytes 786464 | tf_op jit(solution)/shard_map/ppermute | solution.py:48
  337.7 3.7 all-to-all-start.3
  359.0 18.8 %shard_map.175 = (bf16[768,768]{1,0:T(8,128)(2,1)}, bf16[768,1536]{1,0:T(8,128)(2,1)}, bf16[768,1536]{1,0:T(8,128)(2,1)}, bf16[768,1536]{1,0:T(8,128)(2,1)}, bf16[768,1664]{1,0:T(8,128)(2,1)}) custom-call(s32[2]{0:T(128)} %pad_add_fusion.expert_ref, bf16[768,1536]{1,0:T(8,128)(2,1)} %bitcast.28.rows_ref.x_own, bf16[768,1664]{1,0:T(8,128)(2,1)} %bitcast.12.grad_ref, ...), custom_call_target="tpu_custom_call" | custom-call | tf_op jit(solution)/shard_map/pallas_call | solution.py:401
  379.2 5.3 all-to-all-start.4
  384.5 18.8 %shard_map.176 = (bf16[768,768]{1,0:T(8,128)(2,1)}, bf16[768,1536]{1,0:T(8,128)(2,1)}, bf16[768,1536]{1,0:T(8,128)(2,1)}, bf16[768,1536]{1,0:T(8,128)(2,1)}, bf16[768,1664]{1,0:T(8,128)(2,1)}) custom-call(s32[2]{0:T(128)} %pad_add_fusion.expert_ref, bf16[768,1536]{1,0:T(8,128)(2,1)} %bitcast.187, bf16[768,1664]{1,0:T(8,128)(2,1)} %bitcast.24.grad_ref, ...), custom_call_target="tpu_custom_call" | custom-call | tf_op jit(solution)/shard_map/pallas_call | solution.py:401
  403.3 17.3 %shard_map.177 = (bf16[1536,1536]{1,0:T(8,128)(2,1)}, bf16[768,1536]{1,0:T(8,128)(2,1)}) custom-call(bf16[768,1536]{1,0:T(8,128)(2,1)} %bitcast.28.rows_ref.x_own, bf16[768,1536]{1,0:T(8,128)(2,1)} %bitcast.188, bf16[768,1536]{1,0:T(8,128)(2,1)} %get-tuple-element.153.p_own, bf16[768,1536]{1,0:T(8,128)(2,1)} %get-tuple-element.154.p_far, ...), custom_call_target="tpu_custom_call" | custom-call | tf_op jit(solution)/shard_map/pallas_call | solution.py:502
  420.6 5.4 all-to-all-start.5
  439.2 19.8 %all-to-all-done.5 = bf16[16,48,1664]{2,1,0:T(8,128)(2,1)} async-done(((bf16[16,48,1664]{2,1,0:T(8,128)(2,1)}), bf16[16,48,1664]{2,1,0:T(8,128)(2,1)}, u32[]{:S(2)}, u32[]{:S(2)}) %all-to-all-start.5) | async-done | bytes 2555936 | tf_op jit(solution)/shard_map/all_to_all | solution.py:636
  467.0 4.9 broadcast_in_dim.170
  473.0 41.6 %collective-permute-done.19.far_ref = bf16[256,1664]{1,0:T(8,128)(2,1)S(1)} collective-permute-done((bf16[256,1664]{1,0:T(8,128)(2,1)S(1)}, bf16[256,1664]{1,0:T(8,128)(2,1)S(1)}, u32[]{:S(2)}, u32[]{:S(2)}) %collective-permute-start.19) | collective-permute-done | bytes 852000 | tf_op jit(solution)/shard_map/ppermute | solution.py:48
  515.5 8.9 %shard_map.178 = (f32[256,1536]{1,0:T(8,128)}, bf16[256,1536]{1,0:T(8,128)(2,1)}, bf16[2,256,768]{2,1,0:T(8,128)(2,1)}, f32[40,1536]{1,0:T(8,128)}) custom-call(s32[1]{0:T(128)} %bitcast.20.core_ref, bf16[768,256]{1,0:T(8,128)(2,1)} %get-tuple-element.275.place_ref, bf16[768,1664]{1,0:T(8,128)(2,1)} %bitcast.38.back_ref, bf16[256,1664]{1,0:T(8,128)(2,1)} %copy-done.55, ...), custom_call_target="tpu_custom_call" | custom-call | tf_op jit(solution)/shard_map/pallas_call | solution.py:472
  526.5 4.7 all-to-all-start.6
  544.3 5.9 shard_map.183
  551.6 11.8 %shard_map.180 = (bf16[512,1024]{1,0:T(8,128)(2,1)}, f32[512,1536]{1,0:T(8,128)}) custom-call(bf16[512,1024]{1,0:T(8,128)(2,1)} %get-tuple-element.125.joint_ref, bf16[512,768]{1,0:T(8,128)(2,1)} %shard_map.179.grad_ref, bf16[1536,1024]{1,0:T(8,128)(2,1)} %slice.146.weight_ref), custom_call_target="tpu_custom_call" | custom-call | tf_op jit(solution)/shard_map/pallas_call | solution.py:317
  570.8 8.0 %collective-permute-done.25 = bf16[768,256]{1,0:T(8,128)(2,1)S(1)} collective-permute-done((bf16[768,256]{1,0:T(8,128)(2,1)S(1)}, bf16[768,256]{1,0:T(8,128)(2,1)S(1)}, u32[]{:S(2)}, u32[]{:S(2)}) %collective-permute-start.25) | collective-permute-done | bytes 393248 | tf_op jit(solution)/shard_map/ppermute | solution.py:48
  588.0 6.5 shard_map.182
  596.7 4.1 all-to-all-start.7
  605.3 3.5 fusion.2
  608.8 6.5 collective-permute-done.24
  615.3 14.0 %collective-permute-start.33 = (bf16[288,1536]{1,0:T(8,128)(2,1)}, bf16[288,1536]{1,0:T(8,128)(2,1)}, u32[]{:S(2)}, u32[]{:S(2)}) collective-permute-start(bf16[288,1536]{1,0:T(8,128)(2,1)} %pad_maximum_fusion.17), channel_id=1, source_target_pairs={{0,5},{1,4},{2,7},{3,6},{4,1},{5,0},{6,3},{7,2},{8,13},{9,12},{10,... | collective-permute-start | bytes 2654216 | tf_op jit(solution)/shard_map/ppermute | solution.py:614
  634.8 4.0 pad_maximum_fusion.3
  638.8 4.2 reshape.414
  660.3 8.3 %collective-permute-done.35 = f32[34,1536]{1,0:T(8,128)S(1)} collective-permute-done((f32[34,1536]{1,0:T(8,128)S(1)}, f32[34,1536]{1,0:T(8,128)S(1)}, u32[]{:S(2)}, u32[]{:S(2)}) %collective-permute-start.35) | collective-permute-done | bytes 208928 | tf_op jit(solution)/shard_map/ppermute | solution.py:48
  668.8 16.4 %collective-permute-done.36 = f32[34,1536]{1,0:T(8,128)S(1)} collective-permute-done((f32[34,1536]{1,0:T(8,128)S(1)}, f32[34,1536]{1,0:T(8,128)S(1)}, u32[]{:S(2)}, u32[]{:S(2)}) %collective-permute-start.36) | collective-permute-done | bytes 208928 | tf_op jit(solution)/shard_map/ppermute | solution.py:48
  685.9 7.1 collective-permute-done.32
  704.9 45.5 %collective-permute-done.38 = f32[34,1536]{1,0:T(8,128)S(1)} collective-permute-done((f32[34,1536]{1,0:T(8,128)S(1)}, f32[34,1536]{1,0:T(8,128)S(1)}, u32[]{:S(2)}, u32[]{:S(2)}) %collective-permute-start.38) | collective-permute-done | bytes 208928 | tf_op jit(solution)/shard_map/ppermute | solution.py:48
  751.3 3.5 collective-permute-start.40
  755.4 7.9 %collective-permute-done.40 = bf16[1,1,1,192,896]{4,3,2,1,0:T(8,128)(2,1)S(1)} collective-permute-done((bf16[1,1,1,192,896]{4,3,2,1,0:T(8,128)(2,1)S(1)}, bf16[1,1,1,192,896]{4,3,2,1,0:T(8,128)(2,1)S(1)}, u32[]{:S(2)}, u32[]{:S(2)}) %collective-permute-start.40) | collective-permute-done | bytes 344096 | tf_op jit(solution)/shard_map/ppermute | solution.py:48
  (464 shorter events, 212.5 us)
Async XLA Ops:
  3.1 20.0 %collective-permute-start = (bf16[1,1,1,192,896]{4,3,2,1,0:T(8,128)(2,1)S(1)}, bf16[1,1,1,192,896]{4,3,2,1,0:T(8,128)(2,1)S(1)}, u32[]{:S(2)}, u32[]{:S(2)}) collective-permute-start(bf16[1,1,1,192,896]{4,3,2,1,0:T(8,128)(2,1)S(1)} %get-tuple-element.214), channel_id=1, source_target_pairs={{0,4},{4,0},{1,5},{5,1},{2,6},{6,2},{3,7},{7,3},{8,12},{12,8},{9,1... | collective-permute-start | bytes 1032200 | tf_op jit(solution)/shard_map/ppermute | solution.py:48
  7.7 22.3 %collective-permute-start.6 = (bf16[256,1536]{1,0:T(8,128)(2,1)S(1)}, bf16[256,1536]{1,0:T(8,128)(2,1)}, u32[]{:S(2)}, u32[]{:S(2)}) collective-permute-start(bf16[256,1536]{1,0:T(8,128)(2,1)S(1)} %fusion.5), channel_id=1, source_target_pairs={{0,8},{8,0},{1,9},{9,1},{2,10},{10,2},{3,11},{11,3},{4,12},{12,4},... | collective-permute-start | bytes 2359304 | tf_op jit(solution)/shard_map/ppermute | solution.py:48
  7.8 15.0 %collective-permute-start.10 = (s32[256,4]{0,1:T(4,128)S(1)}, s32[256,4]{0,1:T(4,128)S(1)}, u32[]{:S(2)}, u32[]{:S(2)}) collective-permute-start(s32[256,4]{0,1:T(4,128)S(1)} %copy-done.85), channel_id=1, source_target_pairs={{0,4},{4,0},{1,5},{5,1},{2,6},{6,2},{3,7},{7,3},{8,12},{12,8},{9,1... | collective-permute-start | bytes 12296 | tf_op jit(solution)/shard_map/ppermute | solution.py:48
  23.2 16.7 %collective-permute-start.1 = (bf16[2,1,1,192,896]{4,3,2,1,0:T(8,128)(2,1)S(1)}, bf16[2,1,1,192,896]{4,3,2,1,0:T(8,128)(2,1)S(1)}, u32[]{:S(2)}, u32[]{:S(2)}) collective-permute-start(bf16[2,1,1,192,896]{4,3,2,1,0:T(8,128)(2,1)S(1)} %constant_dynamic-update-slice_fusion.14), channel_id=1, source_target_pairs={{0,2},{1,3},{2,0},{3,1},{4,6},{5,7},{6,4},{7,5},{8,10},{9,11},{10,... | collective-permute-start | bytes 2064392 | tf_op jit(solution)/shard_map/ppermute | solution.py:48
  42.5 13.7 %collective-permute-start.4 = (bf16[2,2,1,192,384]{4,3,2,1,0:T(8,128)(2,1)S(1)}, bf16[2,2,1,192,384]{4,3,2,1,0:T(8,128)(2,1)S(1)}, u32[]{:S(2)}, u32[]{:S(2)}) collective-permute-start(bf16[2,2,1,192,384]{4,3,2,1,0:T(8,128)(2,1)S(1)} %get-tuple-element.255), channel_id=1, source_target_pairs={{0,16},{16,0},{1,17},{17,1},{2,18},{18,2},{3,19},{19,3},{4,20},{20... | collective-permute-start | bytes 1769480 | tf_op jit(solution)/shard_map/ppermute | solution.py:48
  44.1 20.5 %collective-permute-start.2 = (bf16[2,2,1,192,512]{4,3,2,1,0:T(8,128)(2,1)S(1)}, bf16[2,2,1,192,512]{4,3,2,1,0:T(8,128)(2,1)S(1)}, u32[]{:S(2)}, u32[]{:S(2)}) collective-permute-start(bf16[2,2,1,192,512]{4,3,2,1,0:T(8,128)(2,1)S(1)} %get-tuple-element.253), channel_id=1, source_target_pairs={{0,1},{1,0},{2,3},{3,2},{4,5},{5,4},{6,7},{7,6},{8,9},{9,8},{10,11... | collective-permute-start | bytes 2359304 | tf_op jit(solution)/shard_map/ppermute | solution.py:48
  45.7 53.1 %collective-permute-start.7 = (bf16[256,1536]{1,0:T(8,128)(2,1)S(1)}, bf16[256,1536]{1,0:T(8,128)(2,1)S(1)}, u32[]{:S(2)}, u32[]{:S(2)}) collective-permute-start(bf16[256,1536]{1,0:T(8,128)(2,1)S(1)} %copy-done.24), channel_id=1, source_target_pairs={{0,4},{4,0},{1,5},{5,1},{2,6},{6,2},{3,7},{7,3},{8,12},{12,8},{9,1... | collective-permute-start | bytes 2359304 | tf_op jit(solution)/shard_map/ppermute | solution.py:48
  49.6 49.1 %collective-permute-start.8 = (bf16[288,1536]{1,0:T(8,128)(2,1)S(1)}, bf16[288,1536]{1,0:T(8,128)(2,1)S(1)}, u32[]{:S(2)}, u32[]{:S(2)}) collective-permute-start(bf16[288,1536]{1,0:T(8,128)(2,1)S(1)} %pad_maximum_fusion.6), channel_id=1, source_target_pairs={{0,2},{1,3},{2,0},{3,1},{4,6},{5,7},{6,4},{7,5},{8,10},{9,11},{10,... | collective-permute-start | bytes 2654216 | tf_op jit(solution)/shard_map/ppermute | solution.py:588
  51.5 69.0 %collective-permute-start.9 = (bf16[288,1536]{1,0:T(8,128)(2,1)S(1)}, bf16[288,1536]{1,0:T(8,128)(2,1)S(1)}, u32[]{:S(2)}, u32[]{:S(2)}) collective-permute-start(bf16[288,1536]{1,0:T(8,128)(2,1)S(1)} %pad_maximum_fusion.7), channel_id=1, source_target_pairs={{0,4},{1,5},{2,6},{3,7},{4,0},{5,1},{6,2},{7,3},{8,12},{9,13},{10,... | collective-permute-start | bytes 2654216 | tf_op jit(solution)/shard_map/ppermute | solution.py:588
  56.2 30.8 %collective-permute-start.5 = (bf16[2,2,1,192,768]{4,3,2,1,0:T(8,128)(2,1)S(1)}, bf16[2,2,1,192,768]{4,3,2,1,0:T(8,128)(2,1)S(1)}, u32[]{:S(2)}, u32[]{:S(2)}) collective-permute-start(bf16[2,2,1,192,768]{4,3,2,1,0:T(8,128)(2,1)S(1)} %constant_dynamic-update-slice_fusion.6), channel_id=1, source_target_pairs={{0,1},{1,0},{2,3},{3,2},{4,5},{5,4},{6,7},{7,6},{8,9},{9,8},{10,11... | collective-permute-start | bytes 3538952 | tf_op jit(solution)/shard_map/ppermute | solution.py:48
  64.7 30.6 %collective-permute-start.3 = (bf16[2,2,2,192,512]{4,3,2,1,0:T(8,128)(2,1)S(1)}, bf16[2,2,2,192,512]{4,3,2,1,0:T(8,128)(2,1)S(1)}, u32[]{:S(2)}, u32[]{:S(2)}) collective-permute-start(bf16[2,2,2,192,512]{4,3,2,1,0:T(8,128)(2,1)S(1)} %constant_dynamic-update-slice_fusion.10), channel_id=1, source_target_pairs={{0,16},{16,0},{1,17},{17,1},{2,18},{18,2},{3,19},{19,3},{4,20},{20... | collective-permute-start | bytes 4718600 | tf_op jit(solution)/shard_map/ppermute | solution.py:48
  121.4 56.4 %all-to-all-start = ((bf16[16,48,1664]{2,1,0:T(8,128)(2,1)}), bf16[16,48,1664]{2,1,0:T(8,128)(2,1)}, u32[]{:S(2)}, u32[]{:S(2)}) async-start(bf16[16,48,1664]{2,1,0:T(8,128)(2,1)} %bitcast.11), calls=%async_computation | async-start | bytes 5111808 | tf_op jit(solution)/shard_map/all_to_all | solution.py:636
  125.8 51.9 %collective-permute-start.11 = (bf16[288,1536]{1,0:T(8,128)(2,1)}, bf16[288,1536]{1,0:T(8,128)(2,1)}, u32[]{:S(2)}, u32[]{:S(2)}) collective-permute-start(bf16[288,1536]{1,0:T(8,128)(2,1)} %pad_maximum_fusion.8), channel_id=1, source_target_pairs={{0,6},{1,7},{2,4},{3,5},{4,2},{5,3},{6,0},{7,1},{8,14},{9,15},{10,... | collective-permute-start | bytes 2654216 | tf_op jit(solution)/shard_map/ppermute | solution.py:588
  129.3 48.5 %collective-permute-start.12 = (bf16[288,1536]{1,0:T(8,128)(2,1)}, bf16[288,1536]{1,0:T(8,128)(2,1)}, u32[]{:S(2)}, u32[]{:S(2)}) collective-permute-start(bf16[288,1536]{1,0:T(8,128)(2,1)} %pad_maximum_fusion.9), channel_id=1, source_target_pairs={{0,1},{1,0},{2,3},{3,2},{4,5},{5,4},{6,7},{7,6},{8,9},{9,8},{10,11... | collective-permute-start | bytes 2654216 | tf_op jit(solution)/shard_map/ppermute | solution.py:588
  140.4 42.8 %collective-permute-start.14 = (bf16[1536,768]{1,0:T(8,128)(2,1)}, bf16[1536,768]{1,0:T(8,128)(2,1)}, u32[]{:S(2)}, u32[]{:S(2)}) collective-permute-start(bf16[1536,768]{1,0:T(8,128)(2,1)} %get-tuple-element.215), channel_id=1, source_target_pairs={{0,8},{8,0},{1,9},{9,1},{2,10},{10,2},{3,11},{11,3},{4,12},{12,4},... | collective-permute-start | bytes 7077896 | tf_op jit(solution)/shard_map/ppermute | solution.py:48
  177.8 56.6 %all-to-all-start.1 = ((bf16[16,48,1664]{2,1,0:T(8,128)(2,1)}), bf16[16,48,1664]{2,1,0:T(8,128)(2,1)}, u32[]{:S(2)}, u32[]{:S(2)}) async-start(bf16[16,48,1664]{2,1,0:T(8,128)(2,1)} %bitcast.23), calls=%async_computation.1 | async-start | bytes 5111808 | tf_op jit(solution)/shard_map/all_to_all | solution.py:636
  186.7 45.1 %collective-permute-start.15 = (bf16[288,1536]{1,0:T(8,128)(2,1)S(1)}, bf16[288,1536]{1,0:T(8,128)(2,1)}, u32[]{:S(2)}, u32[]{:S(2)}) collective-permute-start(bf16[288,1536]{1,0:T(8,128)(2,1)S(1)} %copy-done.49), channel_id=1, source_target_pairs={{0,5},{1,4},{2,7},{3,6},{4,1},{5,0},{6,3},{7,2},{8,13},{9,12},{10,... | collective-permute-start | bytes 2654216 | tf_op jit(solution)/shard_map/ppermute | solution.py:588
  234.4 63.1 %all-to-all-start.2 = ((bf16[16,48,1536]{2,1,0:T(8,128)(2,1)}), bf16[16,48,1536]{2,1,0:T(8,128)(2,1)}, u32[]{:S(2)}, u32[]{:S(2)}) async-start(bf16[16,48,1536]{2,1,0:T(8,128)(2,1)} %bitcast.190), calls=%async_computation.2 | async-start | bytes 4718592 | tf_op jit(solution)/shard_map/all_to_all | solution.py:636
  238.8 58.7 %collective-permute-start.16 = (bf16[288,1536]{1,0:T(8,128)(2,1)}, bf16[288,1536]{1,0:T(8,128)(2,1)}, u32[]{:S(2)}, u32[]{:S(2)}) collective-permute-start(bf16[288,1536]{1,0:T(8,128)(2,1)} %pad_maximum_fusion.11), channel_id=1, source_target_pairs={{0,7},{1,6},{2,5},{3,4},{4,3},{5,2},{6,1},{7,0},{8,15},{9,14},{10,... | collective-permute-start | bytes 2654216 | tf_op jit(solution)/shard_map/ppermute | solution.py:588
  297.5 36.9 %collective-permute-start.17 = (bf16[256,1536]{1,0:T(8,128)(2,1)S(1)}, bf16[256,1536]{1,0:T(8,128)(2,1)S(1)}, u32[]{:S(2)}, u32[]{:S(2)}) collective-permute-start(bf16[256,1536]{1,0:T(8,128)(2,1)S(1)} %copy-done.8), channel_id=1, source_target_pairs={{0,4},{4,0},{1,5},{5,1},{2,6},{6,2},{3,7},{7,3},{8,12},{12,8},{9,1... | collective-permute-start | bytes 2359304 | tf_op jit(solution)/shard_map/ppermute | solution.py:48
  297.5 40.1 %collective-permute-start.18 = (bf16[288,1536]{1,0:T(8,128)(2,1)}, bf16[288,1536]{1,0:T(8,128)(2,1)}, u32[]{:S(2)}, u32[]{:S(2)}) collective-permute-start(bf16[288,1536]{1,0:T(8,128)(2,1)} %pad_maximum_fusion.13), channel_id=1, source_target_pairs={{0,3},{1,2},{2,1},{3,0},{4,7},{5,6},{6,5},{7,4},{8,11},{9,10},{10,... | collective-permute-start | bytes 2654216 | tf_op jit(solution)/shard_map/ppermute | solution.py:588
  337.7 40.1 %all-to-all-start.3 = ((bf16[16,48,1536]{2,1,0:T(8,128)(2,1)}), bf16[16,48,1536]{2,1,0:T(8,128)(2,1)S(1)}, u32[]{:S(2)}, u32[]{:S(2)}) async-start(bf16[16,48,1536]{2,1,0:T(8,128)(2,1)} %bitcast.189), calls=%async_computation.3 | async-start | bytes 4718592 | tf_op jit(solution)/shard_map/all_to_all | solution.py:636
  379.2 41.3 %all-to-all-start.4 = ((bf16[16,48,1664]{2,1,0:T(8,128)(2,1)}), bf16[16,48,1664]{2,1,0:T(8,128)(2,1)}, u32[]{:S(2)}, u32[]{:S(2)}) async-start(bf16[16,48,1664]{2,1,0:T(8,128)(2,1)} %bitcast.194), calls=%async_computation.4 | async-start | bytes 5111808 | tf_op jit(solution)/shard_map/all_to_all | solution.py:636
  420.6 38.4 %all-to-all-start.5 = ((bf16[16,48,1664]{2,1,0:T(8,128)(2,1)}), bf16[16,48,1664]{2,1,0:T(8,128)(2,1)}, u32[]{:S(2)}, u32[]{:S(2)}) async-start(bf16[16,48,1664]{2,1,0:T(8,128)(2,1)} %bitcast.39), calls=%async_computation.5 | async-start | bytes 5111808 | tf_op jit(solution)/shard_map/all_to_all | solution.py:636
  437.1 208.5 %collective-permute-start.27 = (bf16[288,1536]{1,0:T(8,128)(2,1)}, bf16[288,1536]{1,0:T(8,128)(2,1)}, u32[]{:S(2)}, u32[]{:S(2)}) collective-permute-start(bf16[288,1536]{1,0:T(8,128)(2,1)} %pad_maximum_fusion.14), channel_id=1, source_target_pairs={{0,2},{1,3},{2,4},{3,5},{4,6},{5,7},{6,0},{7,1},{8,10},{9,11},{10,... | collective-permute-start | bytes 2654216 | tf_op jit(solution)/shard_map/ppermute | solution.py:614
  461.6 53.0 %collective-permute-start.19 = (bf16[256,1664]{1,0:T(8,128)(2,1)S(1)}, bf16[256,1664]{1,0:T(8,128)(2,1)S(1)}, u32[]{:S(2)}, u32[]{:S(2)}) collective-permute-start(bf16[256,1664]{1,0:T(8,128)(2,1)S(1)} %fusion.1), channel_id=1, source_target_pairs={{0,4},{4,0},{1,5},{5,1},{2,6},{6,2},{3,7},{7,3},{8,12},{12,8},{9,1... | collective-permute-start | bytes 2555912 | tf_op jit(solution)/shard_map/ppermute | solution.py:48
  526.5 12.9 %collective-permute-start.20 = (bf16[256,768]{1,0:T(8,128)(2,1)}, bf16[256,768]{1,0:T(8,128)(2,1)}, u32[]{:S(2)}, u32[]{:S(2)}) collective-permute-start(bf16[256,768]{1,0:T(8,128)(2,1)} %get-tuple-element.264), channel_id=1, source_target_pairs={{0,8},{8,0},{1,9},{9,1},{2,10},{10,2},{3,11},{11,3},{4,12},{12,4},... | collective-permute-start | bytes 1179656 | tf_op jit(solution)/shard_map/ppermute | solution.py:48
  526.5 61.5 %all-to-all-start.6 = ((bf16[16,48,1536]{2,1,0:T(8,128)(2,1)}), bf16[16,48,1536]{2,1,0:T(8,128)(2,1)}, u32[]{:S(2)}, u32[]{:S(2)}) async-start(bf16[16,48,1536]{2,1,0:T(8,128)(2,1)} %bitcast.196), calls=%async_computation.6 | async-start | bytes 4718592 | tf_op jit(solution)/shard_map/all_to_all | solution.py:636
  536.5 109.2 %collective-permute-start.28 = (bf16[288,1536]{1,0:T(8,128)(2,1)}, bf16[288,1536]{1,0:T(8,128)(2,1)}, u32[]{:S(2)}, u32[]{:S(2)}) collective-permute-start(bf16[288,1536]{1,0:T(8,128)(2,1)} %pad_maximum_fusion.15), channel_id=1, source_target_pairs={{0,6},{1,7},{2,0},{3,1},{4,2},{5,3},{6,4},{7,5},{8,14},{9,15},{10,... | collective-permute-start | bytes 2654216 | tf_op jit(solution)/shard_map/ppermute | solution.py:614
  550.1 31.7 %collective-permute-start.23 = (bf16[1536,256]{1,0:T(8,128)(2,1)}, bf16[1536,256]{1,0:T(8,128)(2,1)}, u32[]{:S(2)}, u32[]{:S(2)}) collective-permute-start(bf16[1536,256]{1,0:T(8,128)(2,1)} %get-tuple-element.178), channel_id=1, source_target_pairs={{0,16},{16,0},{1,17},{17,1},{2,18},{18,2},{3,19},{19,3},{4,20},{20... | collective-permute-start | bytes 2359304 | tf_op jit(solution)/shard_map/ppermute | solution.py:48
  566.3 18.7 %collective-permute-start.26 = (f32[256,1536]{1,0:T(8,128)}, f32[256,1536]{1,0:T(8,128)S(1)}, u32[]{:S(2)}, u32[]{:S(2)}) collective-permute-start(f32[256,1536]{1,0:T(8,128)} %slice.172), channel_id=1, source_target_pairs={{0,8},{8,0},{1,9},{9,1},{2,10},{10,2},{3,11},{11,3},{4,12},{12,4},... | collective-permute-start | bytes 4718600 | tf_op jit(solution)/shard_map/ppermute | solution.py:48
  567.3 11.5 %collective-permute-start.25 = (bf16[768,256]{1,0:T(8,128)(2,1)S(1)}, bf16[768,256]{1,0:T(8,128)(2,1)S(1)}, u32[]{:S(2)}, u32[]{:S(2)}) collective-permute-start(bf16[768,256]{1,0:T(8,128)(2,1)S(1)} %copy-done.86), channel_id=1, source_target_pairs={{0,1},{1,0},{2,3},{3,2},{4,5},{5,4},{6,7},{7,6},{8,9},{9,8},{10,11... | collective-permute-start | bytes 1179656 | tf_op jit(solution)/shard_map/ppermute | solution.py:48
  578.8 66.8 %collective-permute-start.29 = (bf16[288,1536]{1,0:T(8,128)(2,1)}, bf16[288,1536]{1,0:T(8,128)(2,1)}, u32[]{:S(2)}, u32[]{:S(2)}) collective-permute-start(bf16[288,1536]{1,0:T(8,128)(2,1)} %pad_maximum_fusion.16), channel_id=1, source_target_pairs={{0,4},{1,5},{2,6},{3,7},{4,0},{5,1},{6,2},{7,3},{8,12},{9,13},{10,... | collective-permute-start | bytes 2654216 | tf_op jit(solution)/shard_map/ppermute | solution.py:614
  594.5 20.8 %collective-permute-start.24 = (bf16[768,512]{1,0:T(8,128)(2,1)}, bf16[768,512]{1,0:T(8,128)(2,1)}, u32[]{:S(2)}, u32[]{:S(2)}) collective-permute-start(bf16[768,512]{1,0:T(8,128)(2,1)} %get-tuple-element.180), channel_id=1, source_target_pairs={{0,1},{1,0},{2,3},{3,2},{4,5},{5,4},{6,7},{7,6},{8,9},{9,8},{10,11... | collective-permute-start | bytes 2359304 | tf_op jit(solution)/shard_map/ppermute | solution.py:48
  596.7 182.8 %all-to-all-start.7 = ((bf16[16,48,1536]{2,1,0:T(8,128)(2,1)}), bf16[16,48,1536]{2,1,0:T(8,128)(2,1)S(1)}, u32[]{:S(2)}, u32[]{:S(2)}) async-start(bf16[16,48,1536]{2,1,0:T(8,128)(2,1)} %bitcast.195), calls=%async_computation.7 | async-start | bytes 4718592 | tf_op jit(solution)/shard_map/all_to_all | solution.py:636
  600.8 42.2 %collective-permute-start.21 = (bf16[1536,256]{1,0:T(8,128)(2,1)}, bf16[1536,256]{1,0:T(8,128)(2,1)}, u32[]{:S(2)}, u32[]{:S(2)}) collective-permute-start(bf16[1536,256]{1,0:T(8,128)(2,1)} %get-tuple-element.175), channel_id=1, source_target_pairs={{0,16},{16,0},{1,17},{17,1},{2,18},{18,2},{3,19},{19,3},{4,20},{20... | collective-permute-start | bytes 2359304 | tf_op jit(solution)/shard_map/ppermute | solution.py:48
  615.3 70.6 %collective-permute-start.33 = (bf16[288,1536]{1,0:T(8,128)(2,1)}, bf16[288,1536]{1,0:T(8,128)(2,1)}, u32[]{:S(2)}, u32[]{:S(2)}) collective-permute-start(bf16[288,1536]{1,0:T(8,128)(2,1)} %pad_maximum_fusion.17), channel_id=1, source_target_pairs={{0,5},{1,4},{2,7},{3,6},{4,1},{5,0},{6,3},{7,2},{8,13},{9,12},{10,... | collective-permute-start | bytes 2654216 | tf_op jit(solution)/shard_map/ppermute | solution.py:614
  646.9 21.8 %collective-permute-start.31 = (bf16[2,2,1,192,384]{4,3,2,1,0:T(8,128)(2,1)S(1)}, bf16[2,2,1,192,384]{4,3,2,1,0:T(8,128)(2,1)S(1)}, u32[]{:S(2)}, u32[]{:S(2)}) collective-permute-start(bf16[2,2,1,192,384]{4,3,2,1,0:T(8,128)(2,1)S(1)} %dynamic-slice_convert_fusion.2), channel_id=1, source_target_pairs={{0,16},{16,0},{1,17},{17,1},{2,18},{18,2},{3,19},{19,3},{4,20},{20... | collective-permute-start | bytes 1769480 | tf_op jit(solution)/shard_map/ppermute | solution.py:48
  647.6 37.7 %collective-permute-start.30 = (bf16[2,2,1,192,512]{4,3,2,1,0:T(8,128)(2,1)S(1)}, bf16[2,2,1,192,512]{4,3,2,1,0:T(8,128)(2,1)S(1)}, u32[]{:S(2)}, u32[]{:S(2)}) collective-permute-start(bf16[2,2,1,192,512]{4,3,2,1,0:T(8,128)(2,1)S(1)} %dynamic-slice_convert_fusion), channel_id=1, source_target_pairs={{0,1},{1,0},{2,3},{3,2},{4,5},{5,4},{6,7},{7,6},{8,9},{9,8},{10,11... | collective-permute-start | bytes 2359304 | tf_op jit(solution)/shard_map/ppermute | solution.py:48
  647.7 45.3 %collective-permute-start.32 = (bf16[256,1536]{1,0:T(8,128)(2,1)S(1)}, bf16[256,1536]{1,0:T(8,128)(2,1)S(1)}, u32[]{:S(2)}, u32[]{:S(2)}) collective-permute-start(bf16[256,1536]{1,0:T(8,128)(2,1)S(1)} %copy-done.58), channel_id=1, source_target_pairs={{0,4},{4,0},{1,5},{5,1},{2,6},{6,2},{3,7},{7,3},{8,12},{12,8},{9,1... | collective-permute-start | bytes 2359304 | tf_op jit(solution)/shard_map/ppermute | solution.py:48
  668.6 16.6 %collective-permute-start.36 = (f32[34,1536]{1,0:T(8,128)S(1)}, f32[34,1536]{1,0:T(8,128)S(1)}, u32[]{:S(2)}, u32[]{:S(2)}) collective-permute-start(f32[34,1536]{1,0:T(8,128)S(1)} %add.719), channel_id=1, source_target_pairs={{0,1},{1,0},{2,3},{3,2},{4,5},{5,4},{6,7},{7,6},{8,9},{9,8},{10,11... | collective-permute-start | bytes 626696 | tf_op jit(solution)/shard_map/ppermute | solution.py:48
  685.2 17.1 %collective-permute-start.37 = (f32[34,1536]{1,0:T(8,128)S(1)}, f32[34,1536]{1,0:T(8,128)S(1)}, u32[]{:S(2)}, u32[]{:S(2)}) collective-permute-start(f32[34,1536]{1,0:T(8,128)S(1)} %add.720), channel_id=1, source_target_pairs={{0,2},{1,3},{2,0},{3,1},{4,6},{5,7},{6,4},{7,5},{8,10},{9,11},{10,... | collective-permute-start | bytes 626696 | tf_op jit(solution)/shard_map/ppermute | solution.py:48
  693.1 58.0 %collective-permute-start.39 = (bf16[2,1,1,192,896]{4,3,2,1,0:T(8,128)(2,1)S(1)}, bf16[2,1,1,192,896]{4,3,2,1,0:T(8,128)(2,1)S(1)}, u32[]{:S(2)}, u32[]{:S(2)}) collective-permute-start(bf16[2,1,1,192,896]{4,3,2,1,0:T(8,128)(2,1)S(1)} %dynamic-slice_convert_fusion.1), channel_id=1, source_target_pairs={{0,2},{1,3},{2,0},{3,1},{4,6},{5,7},{6,4},{7,5},{8,10},{9,11},{10,... | collective-permute-start | bytes 2064392 | tf_op jit(solution)/shard_map/ppermute | solution.py:48
  693.2 70.2 %collective-permute-start.41 = (bf16[288,1536]{1,0:T(8,128)(2,1)S(1)}, bf16[288,1536]{1,0:T(8,128)(2,1)S(1)}, u32[]{:S(2)}, u32[]{:S(2)}) collective-permute-start(bf16[288,1536]{1,0:T(8,128)(2,1)S(1)} %copy-done.46), channel_id=1, source_target_pairs={{0,3},{1,2},{2,5},{3,4},{4,7},{5,6},{6,1},{7,0},{8,11},{9,10},{10,... | collective-permute-start | bytes 2654216 | tf_op jit(solution)/shard_map/ppermute | solution.py:614
  696.1 67.3 %collective-permute-start.42 = (bf16[288,1536]{1,0:T(8,128)(2,1)S(1)}, bf16[288,1536]{1,0:T(8,128)(2,1)S(1)}, u32[]{:S(2)}, u32[]{:S(2)}) collective-permute-start(bf16[288,1536]{1,0:T(8,128)(2,1)S(1)} %copy-done.47), channel_id=1, source_target_pairs={{0,7},{1,6},{2,1},{3,0},{4,3},{5,2},{6,5},{7,4},{8,15},{9,14},{10,... | collective-permute-start | bytes 2654216 | tf_op jit(solution)/shard_map/ppermute | solution.py:614
  698.3 65.2 %collective-permute-start.43 = (bf16[288,1536]{1,0:T(8,128)(2,1)S(1)}, bf16[288,1536]{1,0:T(8,128)(2,1)S(1)}, u32[]{:S(2)}, u32[]{:S(2)}) collective-permute-start(bf16[288,1536]{1,0:T(8,128)(2,1)S(1)} %copy-done.48), channel_id=1, source_target_pairs={{0,1},{1,0},{2,3},{3,2},{4,5},{5,4},{6,7},{7,6},{8,9},{9,8},{10,11... | collective-permute-start | bytes 2654216 | tf_op jit(solution)/shard_map/ppermute | solution.py:614
  702.4 48.0 %collective-permute-start.38 = (f32[34,1536]{1,0:T(8,128)S(1)}, f32[34,1536]{1,0:T(8,128)S(1)}, u32[]{:S(2)}, u32[]{:S(2)}) collective-permute-start(f32[34,1536]{1,0:T(8,128)S(1)} %add.721), channel_id=1, source_target_pairs={{0,4},{4,0},{1,5},{5,1},{2,6},{6,2},{3,7},{7,3},{8,12},{12,8},{9,1... | collective-permute-start | bytes 626696 | tf_op jit(solution)/shard_map/ppermute | solution.py:48
  751.3 12.1 %collective-permute-start.40 = (bf16[1,1,1,192,896]{4,3,2,1,0:T(8,128)(2,1)S(1)}, bf16[1,1,1,192,896]{4,3,2,1,0:T(8,128)(2,1)S(1)}, u32[]{:S(2)}, u32[]{:S(2)}) collective-permute-start(bf16[1,1,1,192,896]{4,3,2,1,0:T(8,128)(2,1)S(1)} %dynamic-slice_convert_fusion.3), channel_id=1, source_target_pairs={{0,4},{4,0},{1,5},{5,1},{2,6},{6,2},{3,7},{7,3},{8,12},{12,8},{9,1... | collective-permute-start | bytes 1032200 | tf_op jit(solution)/shard_map/ppermute | solution.py:48
  (94 other events, 591.7 us)

commit v5 on v4

--- a/solution.py
+++ b/solution.py
@@ -17,7 +17,7 @@
 EPSILON = 1e-06
 VMEM_LIMIT = 56 * 1024 * 1024
 EXTRA = 128
-INWARD = [[(-1, 0), (-2, 0)], [(-3, 0), (0, 1)], [(-2, 1)], [(-3, 1)], [(-1, 1)]]
+INWARD = [[(-1, 0), (-2, 0), (0, 1)], [(-3, 0)], [(-2, 1)], [(-3, 1)], [(-1, 1)]]
 OUTWARD = [[(1, 0)], [(3, 0), (2, 0)], [(2, 1)], [(1, 1), (3, 1), (0, 1)]]
 EXPERT = ("y", "c")
 FSDP = ("h", "r")

time: 797 us -> 796 us (level)
    unnamed x180 -> x184, local copies, waits for them, and re-layouts: 17.4 us -> 17.7 us
where the time goes in v5:
time: 796 us; the launch traced here: 784 us
  waiting for transfers between devices  382 us (48%)
  starting transfers between devices  114 us (14%)
  local copies, waits for them, and re-layouts  109 us (14%)
  Pallas kernels  95.1 us (12%)
  other arithmetic  54.4 us (7%)
  matrix products  26 us (3%)
    ppermute x33, waiting for transfers between devices, swap(): return lax.ppermute(value, axis, [(i, i ^ bit) for i in range(size)])  223 us
    ppermute x7, waiting for transfers between devices, fetch(): lax.ppermute(tie(piece, *names), FSDP, [(i, target(i, move)) for i in ran...  136 us
    pallas_call x2, Pallas kernels, expert_part(): pl.pallas_call(expert_kernel, grid_spec=pltpu.PrefetchScalarGridSpec(num_...  37.6 us
    all_to_all x8, starting transfers between devices, exchange(): lax.all_to_all(buffer.reshape((half_devices, rows // half_devices) + shap...  37.1 us
    ppermute x33, starting transfers between devices, swap(): return lax.ppermute(value, axis, [(i, i ^ bit) for i in range(size)])  34.6 us
    ppermute x7, starting transfers between devices, give(): lax.ppermute(tie(piece, *names), FSDP, [(i, target(i, move)) for i in ran...  26.3 us
    all_to_all x8, waiting for transfers between devices, exchange(): lax.all_to_all(buffer.reshape((half_devices, rows // half_devices) + shap...  22.3 us
    unnamed x184, local copies, waits for them, and re-layouts  17.7 us
  transfers between devices with their start and end apart: 55, of which 22 were waited for; matrix products, arithmetic and copies ran while one was open for 22% of the time, Pallas kernels for 12%

profile of v5, /device:TPU:0, one launch (start us, length us, event | category | flops | bytes accessed | tf_op | source)
XLA Modules:
  0.0 783.6 jit_solution(12576657250099407079)
XLA Ops:
  3.1 4.1 collective-permute-start
  10.7 12.0 %collective-permute-done.11 = s32[256,4]{0,1:T(4,128)S(1)} collective-permute-done((s32[256,4]{0,1:T(4,128)S(1)}, s32[256,4]{0,1:T(4,128)S(1)}, u32[]{:S(2)}, u32[]{:S(2)}) %collective-permute-start.11) | collective-permute-done | bytes 4128 | tf_op jit(solution)/shard_map/ppermute | solution.py:48
  32.3 7.5 collective-permute-done.1
  57.5 7.1 collective-permute-done.2
  70.4 16.8 %collective-permute-done.5 = bf16[2,2,1,192,768]{4,3,2,1,0:T(8,128)(2,1)S(1)} collective-permute-done((bf16[2,2,1,192,768]{4,3,2,1,0:T(8,128)(2,1)S(1)}, bf16[2,2,1,192,768]{4,3,2,1,0:T(8,128)(2,1)S(1)}, u32[]{:S(2)}, u32[]{:S(2)}) %collective-permute-start.5) | collective-permute-done | bytes 1179680 | tf_op jit(solution)/shard_map/ppermute | solution.py:48
  89.1 6.2 collective-permute-done.3
  98.7 21.7 %collective-permute-done.9 = bf16[288,1536]{1,0:T(8,128)(2,1)S(1)} collective-permute-done((bf16[288,1536]{1,0:T(8,128)(2,1)S(1)}, bf16[288,1536]{1,0:T(8,128)(2,1)S(1)}, u32[]{:S(2)}, u32[]{:S(2)}) %collective-permute-start.9) | collective-permute-done | bytes 884768 | tf_op jit(solution)/shard_map/ppermute | solution.py:588
  121.7 4.5 all-to-all-start
  126.1 3.5 collective-permute-start.12
  129.6 3.9 slice.146.weight_ref
  135.9 4.2 fusion.55
  140.1 7.1 shard_map.171
  149.6 28.5 %collective-permute-done.12 = bf16[288,1536]{1,0:T(8,128)(2,1)} collective-permute-done((bf16[288,1536]{1,0:T(8,128)(2,1)}, bf16[288,1536]{1,0:T(8,128)(2,1)}, u32[]{:S(2)}, u32[]{:S(2)}) %collective-permute-start.12) | collective-permute-done | bytes 884768 | tf_op jit(solution)/shard_map/ppermute | solution.py:588
  178.1 5.0 all-to-all-start.1
  183.6 3.4 constant_dynamic-update-slice_fusion.2.weight_ref
  189.8 4.0 multiply_reduce_fusion
  197.1 35.0 %collective-permute-done.15 = bf16[288,1536]{1,0:T(8,128)(2,1)} collective-permute-done((bf16[288,1536]{1,0:T(8,128)(2,1)S(1)}, bf16[288,1536]{1,0:T(8,128)(2,1)}, u32[]{:S(2)}, u32[]{:S(2)}) %collective-permute-start.15) | collective-permute-done | bytes 884768 | tf_op jit(solution)/shard_map/ppermute | solution.py:588
  234.7 4.4 all-to-all-start.2
  246.6 51.2 %collective-permute-done.16 = bf16[288,1536]{1,0:T(8,128)(2,1)} collective-permute-done((bf16[288,1536]{1,0:T(8,128)(2,1)}, bf16[288,1536]{1,0:T(8,128)(2,1)}, u32[]{:S(2)}, u32[]{:S(2)}) %collective-permute-start.16) | collective-permute-done | bytes 884768 | tf_op jit(solution)/shard_map/ppermute | solution.py:588
  297.8 3.6 collective-permute-start.18
  305.8 28.9 %collective-permute-done.17 = bf16[256,1536]{1,0:T(8,128)(2,1)S(1)} collective-permute-done((bf16[256,1536]{1,0:T(8,128)(2,1)S(1)}, bf16[256,1536]{1,0:T(8,128)(2,1)S(1)}, u32[]{:S(2)}, u32[]{:S(2)}) %collective-permute-start.17) | collective-permute-done | bytes 786464 | tf_op jit(solution)/shard_map/ppermute | solution.py:48
  337.9 3.7 all-to-all-start.3
  358.2 18.8 %shard_map.175 = (bf16[768,768]{1,0:T(8,128)(2,1)}, bf16[768,1536]{1,0:T(8,128)(2,1)}, bf16[768,1536]{1,0:T(8,128)(2,1)}, bf16[768,1536]{1,0:T(8,128)(2,1)}, bf16[768,1664]{1,0:T(8,128)(2,1)}) custom-call(s32[2]{0:T(128)} %pad_add_fusion.expert_ref, bf16[768,1536]{1,0:T(8,128)(2,1)} %bitcast.28.rows_ref.x_own, bf16[768,1664]{1,0:T(8,128)(2,1)} %bitcast.14.grad_ref, ...), custom_call_target="tpu_custom_call" | custom-call | tf_op jit(solution)/shard_map/pallas_call | solution.py:401
  378.5 5.3 all-to-all-start.4
  383.7 18.8 %shard_map.176 = (bf16[768,768]{1,0:T(8,128)(2,1)}, bf16[768,1536]{1,0:T(8,128)(2,1)}, bf16[768,1536]{1,0:T(8,128)(2,1)}, bf16[768,1536]{1,0:T(8,128)(2,1)}, bf16[768,1664]{1,0:T(8,128)(2,1)}) custom-call(s32[2]{0:T(128)} %pad_add_fusion.expert_ref, bf16[768,1536]{1,0:T(8,128)(2,1)} %bitcast.187, bf16[768,1664]{1,0:T(8,128)(2,1)} %bitcast.24.grad_ref, ...), custom_call_target="tpu_custom_call" | custom-call | tf_op jit(solution)/shard_map/pallas_call | solution.py:401
  402.5 17.3 %shard_map.177 = (bf16[1536,1536]{1,0:T(8,128)(2,1)}, bf16[768,1536]{1,0:T(8,128)(2,1)}) custom-call(bf16[768,1536]{1,0:T(8,128)(2,1)} %bitcast.28.rows_ref.x_own, bf16[768,1536]{1,0:T(8,128)(2,1)} %bitcast.188, bf16[768,1536]{1,0:T(8,128)(2,1)} %get-tuple-element.147.p_own, bf16[768,1536]{1,0:T(8,128)(2,1)} %get-tuple-element.148.p_far, ...), custom_call_target="tpu_custom_call" | custom-call | tf_op jit(solution)/shard_map/pallas_call | solution.py:502
  419.9 5.4 all-to-all-start.5
  438.5 19.8 %all-to-all-done.5 = bf16[16,48,1664]{2,1,0:T(8,128)(2,1)} async-done(((bf16[16,48,1664]{2,1,0:T(8,128)(2,1)}), bf16[16,48,1664]{2,1,0:T(8,128)(2,1)}, u32[]{:S(2)}, u32[]{:S(2)}) %all-to-all-start.5) | async-done | bytes 2555936 | tf_op jit(solution)/shard_map/all_to_all | solution.py:636
  466.3 4.9 broadcast_in_dim.170
  472.3 41.6 %collective-permute-done.19.far_ref = bf16[256,1664]{1,0:T(8,128)(2,1)S(1)} collective-permute-done((bf16[256,1664]{1,0:T(8,128)(2,1)S(1)}, bf16[256,1664]{1,0:T(8,128)(2,1)S(1)}, u32[]{:S(2)}, u32[]{:S(2)}) %collective-permute-start.19) | collective-permute-done | bytes 852000 | tf_op jit(solution)/shard_map/ppermute | solution.py:48
  514.8 8.9 %shard_map.178 = (f32[256,1536]{1,0:T(8,128)}, bf16[256,1536]{1,0:T(8,128)(2,1)}, bf16[2,256,768]{2,1,0:T(8,128)(2,1)}, f32[40,1536]{1,0:T(8,128)}) custom-call(s32[1]{0:T(128)} %bitcast.20.core_ref, bf16[768,256]{1,0:T(8,128)(2,1)} %get-tuple-element.269.place_ref, bf16[768,1664]{1,0:T(8,128)(2,1)} %bitcast.38.back_ref, bf16[256,1664]{1,0:T(8,128)(2,1)} %copy-done.57, ...), custom_call_target="tpu_custom_call" | custom-call | tf_op jit(solution)/shard_map/pallas_call | solution.py:472
  525.8 4.7 all-to-all-start.6
  543.5 5.9 shard_map.183
  550.9 11.8 %shard_map.180 = (bf16[512,1024]{1,0:T(8,128)(2,1)}, f32[512,1536]{1,0:T(8,128)}) custom-call(bf16[512,1024]{1,0:T(8,128)(2,1)} %get-tuple-element.120.joint_ref, bf16[512,768]{1,0:T(8,128)(2,1)} %shard_map.179.grad_ref, bf16[1536,1024]{1,0:T(8,128)(2,1)} %slice.146.weight_ref), custom_call_target="tpu_custom_call" | custom-call | tf_op jit(solution)/shard_map/pallas_call | solution.py:317
  570.0 8.0 %collective-permute-done.25 = bf16[768,256]{1,0:T(8,128)(2,1)S(1)} collective-permute-done((bf16[768,256]{1,0:T(8,128)(2,1)S(1)}, bf16[768,256]{1,0:T(8,128)(2,1)S(1)}, u32[]{:S(2)}, u32[]{:S(2)}) %collective-permute-start.25) | collective-permute-done | bytes 393248 | tf_op jit(solution)/shard_map/ppermute | solution.py:48
  587.2 6.5 shard_map.182
  595.9 4.1 all-to-all-start.7
  604.6 3.5 fusion.2
  608.0 6.5 collective-permute-done.24
  614.5 14.0 %collective-permute-start.33 = (bf16[288,1536]{1,0:T(8,128)(2,1)}, bf16[288,1536]{1,0:T(8,128)(2,1)}, u32[]{:S(2)}, u32[]{:S(2)}) collective-permute-start(bf16[288,1536]{1,0:T(8,128)(2,1)} %pad_maximum_fusion.17), channel_id=1, source_target_pairs={{0,5},{1,4},{2,7},{3,6},{4,1},{5,0},{6,3},{7,2},{8,13},{9,12},{10,... | collective-permute-start | bytes 2654216 | tf_op jit(solution)/shard_map/ppermute | solution.py:614
  634.1 4.0 pad_maximum_fusion.3
  638.1 4.3 reshape.414
  659.6 8.2 %collective-permute-done.35 = f32[34,1536]{1,0:T(8,128)S(1)} collective-permute-done((f32[34,1536]{1,0:T(8,128)S(1)}, f32[34,1536]{1,0:T(8,128)S(1)}, u32[]{:S(2)}, u32[]{:S(2)}) %collective-permute-start.35) | collective-permute-done | bytes 208928 | tf_op jit(solution)/shard_map/ppermute | solution.py:48
  668.1 16.4 %collective-permute-done.36 = f32[34,1536]{1,0:T(8,128)S(1)} collective-permute-done((f32[34,1536]{1,0:T(8,128)S(1)}, f32[34,1536]{1,0:T(8,128)S(1)}, u32[]{:S(2)}, u32[]{:S(2)}) %collective-permute-start.36) | collective-permute-done | bytes 208928 | tf_op jit(solution)/shard_map/ppermute | solution.py:48
  685.1 7.2 collective-permute-done.32
  704.2 45.4 %collective-permute-done.38 = f32[34,1536]{1,0:T(8,128)S(1)} collective-permute-done((f32[34,1536]{1,0:T(8,128)S(1)}, f32[34,1536]{1,0:T(8,128)S(1)}, u32[]{:S(2)}, u32[]{:S(2)}) %collective-permute-start.38) | collective-permute-done | bytes 208928 | tf_op jit(solution)/shard_map/ppermute | solution.py:48
  750.4 3.5 collective-permute-start.40
  754.6 8.0 %collective-permute-done.40 = bf16[1,1,1,192,896]{4,3,2,1,0:T(8,128)(2,1)S(1)} collective-permute-done((bf16[1,1,1,192,896]{4,3,2,1,0:T(8,128)(2,1)S(1)}, bf16[1,1,1,192,896]{4,3,2,1,0:T(8,128)(2,1)S(1)}, u32[]{:S(2)}, u32[]{:S(2)}) %collective-permute-start.40) | collective-permute-done | bytes 344096 | tf_op jit(solution)/shard_map/ppermute | solution.py:48
  (468 shorter events, 211.6 us)
Async XLA Ops:
  3.1 20.0 %collective-permute-start = (bf16[1,1,1,192,896]{4,3,2,1,0:T(8,128)(2,1)S(1)}, bf16[1,1,1,192,896]{4,3,2,1,0:T(8,128)(2,1)S(1)}, u32[]{:S(2)}, u32[]{:S(2)}) collective-permute-start(bf16[1,1,1,192,896]{4,3,2,1,0:T(8,128)(2,1)S(1)} %get-tuple-element.208), channel_id=1, source_target_pairs={{0,4},{4,0},{1,5},{5,1},{2,6},{6,2},{3,7},{7,3},{8,12},{12,8},{9,1... | collective-permute-start | bytes 1032200 | tf_op jit(solution)/shard_map/ppermute | solution.py:48
  7.7 22.2 %collective-permute-start.6 = (bf16[256,1536]{1,0:T(8,128)(2,1)S(1)}, bf16[256,1536]{1,0:T(8,128)(2,1)}, u32[]{:S(2)}, u32[]{:S(2)}) collective-permute-start(bf16[256,1536]{1,0:T(8,128)(2,1)S(1)} %fusion.5), channel_id=1, source_target_pairs={{0,8},{8,0},{1,9},{9,1},{2,10},{10,2},{3,11},{11,3},{4,12},{12,4},... | collective-permute-start | bytes 2359304 | tf_op jit(solution)/shard_map/ppermute | solution.py:48
  7.8 15.0 %collective-permute-start.11 = (s32[256,4]{0,1:T(4,128)S(1)}, s32[256,4]{0,1:T(4,128)S(1)}, u32[]{:S(2)}, u32[]{:S(2)}) collective-permute-start(s32[256,4]{0,1:T(4,128)S(1)} %copy-done.87), channel_id=1, source_target_pairs={{0,4},{4,0},{1,5},{5,1},{2,6},{6,2},{3,7},{7,3},{8,12},{12,8},{9,1... | collective-permute-start | bytes 12296 | tf_op jit(solution)/shard_map/ppermute | solution.py:48
  23.2 16.7 %collective-permute-start.1 = (bf16[2,1,1,192,896]{4,3,2,1,0:T(8,128)(2,1)S(1)}, bf16[2,1,1,192,896]{4,3,2,1,0:T(8,128)(2,1)S(1)}, u32[]{:S(2)}, u32[]{:S(2)}) collective-permute-start(bf16[2,1,1,192,896]{4,3,2,1,0:T(8,128)(2,1)S(1)} %constant_dynamic-update-slice_fusion.14), channel_id=1, source_target_pairs={{0,2},{1,3},{2,0},{3,1},{4,6},{5,7},{6,4},{7,5},{8,10},{9,11},{10,... | collective-permute-start | bytes 2064392 | tf_op jit(solution)/shard_map/ppermute | solution.py:48
  42.5 13.7 %collective-permute-start.4 = (bf16[2,2,1,192,384]{4,3,2,1,0:T(8,128)(2,1)S(1)}, bf16[2,2,1,192,384]{4,3,2,1,0:T(8,128)(2,1)S(1)}, u32[]{:S(2)}, u32[]{:S(2)}) collective-permute-start(bf16[2,2,1,192,384]{4,3,2,1,0:T(8,128)(2,1)S(1)} %get-tuple-element.249), channel_id=1, source_target_pairs={{0,16},{16,0},{1,17},{17,1},{2,18},{18,2},{3,19},{19,3},{4,20},{20... | collective-permute-start | bytes 1769480 | tf_op jit(solution)/shard_map/ppermute | solution.py:48
  44.1 20.5 %collective-permute-start.2 = (bf16[2,2,1,192,512]{4,3,2,1,0:T(8,128)(2,1)S(1)}, bf16[2,2,1,192,512]{4,3,2,1,0:T(8,128)(2,1)S(1)}, u32[]{:S(2)}, u32[]{:S(2)}) collective-permute-start(bf16[2,2,1,192,512]{4,3,2,1,0:T(8,128)(2,1)S(1)} %get-tuple-element.247), channel_id=1, source_target_pairs={{0,1},{1,0},{2,3},{3,2},{4,5},{5,4},{6,7},{7,6},{8,9},{9,8},{10,11... | collective-permute-start | bytes 2359304 | tf_op jit(solution)/shard_map/ppermute | solution.py:48
  45.7 53.1 %collective-permute-start.7 = (bf16[256,1536]{1,0:T(8,128)(2,1)S(1)}, bf16[256,1536]{1,0:T(8,128)(2,1)S(1)}, u32[]{:S(2)}, u32[]{:S(2)}) collective-permute-start(bf16[256,1536]{1,0:T(8,128)(2,1)S(1)} %copy-done.24), channel_id=1, source_target_pairs={{0,4},{4,0},{1,5},{5,1},{2,6},{6,2},{3,7},{7,3},{8,12},{12,8},{9,1... | collective-permute-start | bytes 2359304 | tf_op jit(solution)/shard_map/ppermute | solution.py:48
  49.6 49.1 %collective-permute-start.8 = (bf16[288,1536]{1,0:T(8,128)(2,1)S(1)}, bf16[288,1536]{1,0:T(8,128)(2,1)S(1)}, u32[]{:S(2)}, u32[]{:S(2)}) collective-permute-start(bf16[288,1536]{1,0:T(8,128)(2,1)S(1)} %pad_maximum_fusion.6), channel_id=1, source_target_pairs={{0,2},{1,3},{2,0},{3,1},{4,6},{5,7},{6,4},{7,5},{8,10},{9,11},{10,... | collective-permute-start | bytes 2654216 | tf_op jit(solution)/shard_map/ppermute | solution.py:588
  51.5 69.0 %collective-permute-start.9 = (bf16[288,1536]{1,0:T(8,128)(2,1)S(1)}, bf16[288,1536]{1,0:T(8,128)(2,1)S(1)}, u32[]{:S(2)}, u32[]{:S(2)}) collective-permute-start(bf16[288,1536]{1,0:T(8,128)(2,1)S(1)} %pad_maximum_fusion.7), channel_id=1, source_target_pairs={{0,4},{1,5},{2,6},{3,7},{4,0},{5,1},{6,2},{7,3},{8,12},{9,13},{10,... | collective-permute-start | bytes 2654216 | tf_op jit(solution)/shard_map/ppermute | solution.py:588
  56.2 30.9 %collective-permute-start.5 = (bf16[2,2,1,192,768]{4,3,2,1,0:T(8,128)(2,1)S(1)}, bf16[2,2,1,192,768]{4,3,2,1,0:T(8,128)(2,1)S(1)}, u32[]{:S(2)}, u32[]{:S(2)}) collective-permute-start(bf16[2,2,1,192,768]{4,3,2,1,0:T(8,128)(2,1)S(1)} %constant_dynamic-update-slice_fusion.6), channel_id=1, source_target_pairs={{0,1},{1,0},{2,3},{3,2},{4,5},{5,4},{6,7},{7,6},{8,9},{9,8},{10,11... | collective-permute-start | bytes 3538952 | tf_op jit(solution)/shard_map/ppermute | solution.py:48
  64.7 30.6 %collective-permute-start.3 = (bf16[2,2,2,192,512]{4,3,2,1,0:T(8,128)(2,1)S(1)}, bf16[2,2,2,192,512]{4,3,2,1,0:T(8,128)(2,1)S(1)}, u32[]{:S(2)}, u32[]{:S(2)}) collective-permute-start(bf16[2,2,2,192,512]{4,3,2,1,0:T(8,128)(2,1)S(1)} %constant_dynamic-update-slice_fusion.10), channel_id=1, source_target_pairs={{0,16},{16,0},{1,17},{17,1},{2,18},{18,2},{3,19},{19,3},{4,20},{20... | collective-permute-start | bytes 4718600 | tf_op jit(solution)/shard_map/ppermute | solution.py:48
  87.2 33.3 %collective-permute-start.10 = (bf16[288,1536]{1,0:T(8,128)(2,1)S(1)}, bf16[288,1536]{1,0:T(8,128)(2,1)S(1)}, u32[]{:S(2)}, u32[]{:S(2)}) collective-permute-start(bf16[288,1536]{1,0:T(8,128)(2,1)S(1)} %pad_maximum_fusion.8), channel_id=1, source_target_pairs={{0,1},{1,0},{2,3},{3,2},{4,5},{5,4},{6,7},{7,6},{8,9},{9,8},{10,11... | collective-permute-start | bytes 2654216 | tf_op jit(solution)/shard_map/ppermute | solution.py:588
  121.7 56.4 %all-to-all-start = ((bf16[16,48,1664]{2,1,0:T(8,128)(2,1)}), bf16[16,48,1664]{2,1,0:T(8,128)(2,1)}, u32[]{:S(2)}, u32[]{:S(2)}) async-start(bf16[16,48,1664]{2,1,0:T(8,128)(2,1)} %bitcast.13), calls=%async_computation | async-start | bytes 5111808 | tf_op jit(solution)/shard_map/all_to_all | solution.py:636
  126.1 51.9 %collective-permute-start.12 = (bf16[288,1536]{1,0:T(8,128)(2,1)}, bf16[288,1536]{1,0:T(8,128)(2,1)}, u32[]{:S(2)}, u32[]{:S(2)}) collective-permute-start(bf16[288,1536]{1,0:T(8,128)(2,1)} %pad_maximum_fusion.9), channel_id=1, source_target_pairs={{0,6},{1,7},{2,4},{3,5},{4,2},{5,3},{6,0},{7,1},{8,14},{9,15},{10,... | collective-permute-start | bytes 2654216 | tf_op jit(solution)/shard_map/ppermute | solution.py:588
  140.1 43.5 %collective-permute-start.14 = (bf16[1536,768]{1,0:T(8,128)(2,1)}, bf16[1536,768]{1,0:T(8,128)(2,1)}, u32[]{:S(2)}, u32[]{:S(2)}) collective-permute-start(bf16[1536,768]{1,0:T(8,128)(2,1)} %get-tuple-element.209), channel_id=1, source_target_pairs={{0,8},{8,0},{1,9},{9,1},{2,10},{10,2},{3,11},{11,3},{4,12},{12,4},... | collective-permute-start | bytes 7077896 | tf_op jit(solution)/shard_map/ppermute | solution.py:48
  178.1 56.6 %all-to-all-start.1 = ((bf16[16,48,1664]{2,1,0:T(8,128)(2,1)}), bf16[16,48,1664]{2,1,0:T(8,128)(2,1)}, u32[]{:S(2)}, u32[]{:S(2)}) async-start(bf16[16,48,1664]{2,1,0:T(8,128)(2,1)} %bitcast.23), calls=%async_computation.1 | async-start | bytes 5111808 | tf_op jit(solution)/shard_map/all_to_all | solution.py:636
  187.0 45.1 %collective-permute-start.15 = (bf16[288,1536]{1,0:T(8,128)(2,1)S(1)}, bf16[288,1536]{1,0:T(8,128)(2,1)}, u32[]{:S(2)}, u32[]{:S(2)}) collective-permute-start(bf16[288,1536]{1,0:T(8,128)(2,1)S(1)} %copy-done.49), channel_id=1, source_target_pairs={{0,5},{1,4},{2,7},{3,6},{4,1},{5,0},{6,3},{7,2},{8,13},{9,12},{10,... | collective-permute-start | bytes 2654216 | tf_op jit(solution)/shard_map/ppermute | solution.py:588
  234.7 63.1 %all-to-all-start.2 = ((bf16[16,48,1536]{2,1,0:T(8,128)(2,1)}), bf16[16,48,1536]{2,1,0:T(8,128)(2,1)}, u32[]{:S(2)}, u32[]{:S(2)}) async-start(bf16[16,48,1536]{2,1,0:T(8,128)(2,1)} %bitcast.190), calls=%async_computation.2 | async-start | bytes 4718592 | tf_op jit(solution)/shard_map/all_to_all | solution.py:636
  239.1 58.6 %collective-permute-start.16 = (bf16[288,1536]{1,0:T(8,128)(2,1)}, bf16[288,1536]{1,0:T(8,128)(2,1)}, u32[]{:S(2)}, u32[]{:S(2)}) collective-permute-start(bf16[288,1536]{1,0:T(8,128)(2,1)} %pad_maximum_fusion.11), channel_id=1, source_target_pairs={{0,7},{1,6},{2,5},{3,4},{4,3},{5,2},{6,1},{7,0},{8,15},{9,14},{10,... | collective-permute-start | bytes 2654216 | tf_op jit(solution)/shard_map/ppermute | solution.py:588
  297.8 36.9 %collective-permute-start.17 = (bf16[256,1536]{1,0:T(8,128)(2,1)S(1)}, bf16[256,1536]{1,0:T(8,128)(2,1)S(1)}, u32[]{:S(2)}, u32[]{:S(2)}) collective-permute-start(bf16[256,1536]{1,0:T(8,128)(2,1)S(1)} %copy-done.8), channel_id=1, source_target_pairs={{0,4},{4,0},{1,5},{5,1},{2,6},{6,2},{3,7},{7,3},{8,12},{12,8},{9,1... | collective-permute-start | bytes 2359304 | tf_op jit(solution)/shard_map/ppermute | solution.py:48
  297.8 40.1 %collective-permute-start.18 = (bf16[288,1536]{1,0:T(8,128)(2,1)}, bf16[288,1536]{1,0:T(8,128)(2,1)}, u32[]{:S(2)}, u32[]{:S(2)}) collective-permute-start(bf16[288,1536]{1,0:T(8,128)(2,1)} %pad_maximum_fusion.13), channel_id=1, source_target_pairs={{0,3},{1,2},{2,1},{3,0},{4,7},{5,6},{6,5},{7,4},{8,11},{9,10},{10,... | collective-permute-start | bytes 2654216 | tf_op jit(solution)/shard_map/ppermute | solution.py:588
  337.9 39.1 %all-to-all-start.3 = ((bf16[16,48,1536]{2,1,0:T(8,128)(2,1)}), bf16[16,48,1536]{2,1,0:T(8,128)(2,1)S(1)}, u32[]{:S(2)}, u32[]{:S(2)}) async-start(bf16[16,48,1536]{2,1,0:T(8,128)(2,1)} %bitcast.189), calls=%async_computation.3 | async-start | bytes 4718592 | tf_op jit(solution)/shard_map/all_to_all | solution.py:636
  378.5 41.3 %all-to-all-start.4 = ((bf16[16,48,1664]{2,1,0:T(8,128)(2,1)}), bf16[16,48,1664]{2,1,0:T(8,128)(2,1)}, u32[]{:S(2)}, u32[]{:S(2)}) async-start(bf16[16,48,1664]{2,1,0:T(8,128)(2,1)} %bitcast.194), calls=%async_computation.4 | async-start | bytes 5111808 | tf_op jit(solution)/shard_map/all_to_all | solution.py:636
  419.9 38.4 %all-to-all-start.5 = ((bf16[16,48,1664]{2,1,0:T(8,128)(2,1)}), bf16[16,48,1664]{2,1,0:T(8,128)(2,1)}, u32[]{:S(2)}, u32[]{:S(2)}) async-start(bf16[16,48,1664]{2,1,0:T(8,128)(2,1)} %bitcast.39), calls=%async_computation.5 | async-start | bytes 5111808 | tf_op jit(solution)/shard_map/all_to_all | solution.py:636
  436.4 208.5 %collective-permute-start.27 = (bf16[288,1536]{1,0:T(8,128)(2,1)}, bf16[288,1536]{1,0:T(8,128)(2,1)}, u32[]{:S(2)}, u32[]{:S(2)}) collective-permute-start(bf16[288,1536]{1,0:T(8,128)(2,1)} %pad_maximum_fusion.14), channel_id=1, source_target_pairs={{0,2},{1,3},{2,4},{3,5},{4,6},{5,7},{6,0},{7,1},{8,10},{9,11},{10,... | collective-permute-start | bytes 2654216 | tf_op jit(solution)/shard_map/ppermute | solution.py:614
  460.9 53.0 %collective-permute-start.19 = (bf16[256,1664]{1,0:T(8,128)(2,1)S(1)}, bf16[256,1664]{1,0:T(8,128)(2,1)S(1)}, u32[]{:S(2)}, u32[]{:S(2)}) collective-permute-start(bf16[256,1664]{1,0:T(8,128)(2,1)S(1)} %fusion.1), channel_id=1, source_target_pairs={{0,4},{4,0},{1,5},{5,1},{2,6},{6,2},{3,7},{7,3},{8,12},{12,8},{9,1... | collective-permute-start | bytes 2555912 | tf_op jit(solution)/shard_map/ppermute | solution.py:48
  525.8 12.9 %collective-permute-start.20 = (bf16[256,768]{1,0:T(8,128)(2,1)}, bf16[256,768]{1,0:T(8,128)(2,1)}, u32[]{:S(2)}, u32[]{:S(2)}) collective-permute-start(bf16[256,768]{1,0:T(8,128)(2,1)} %get-tuple-element.258), channel_id=1, source_target_pairs={{0,8},{8,0},{1,9},{9,1},{2,10},{10,2},{3,11},{11,3},{4,12},{12,4},... | collective-permute-start | bytes 1179656 | tf_op jit(solution)/shard_map/ppermute | solution.py:48
  525.8 61.5 %all-to-all-start.6 = ((bf16[16,48,1536]{2,1,0:T(8,128)(2,1)}), bf16[16,48,1536]{2,1,0:T(8,128)(2,1)}, u32[]{:S(2)}, u32[]{:S(2)}) async-start(bf16[16,48,1536]{2,1,0:T(8,128)(2,1)} %bitcast.196), calls=%async_computation.6 | async-start | bytes 4718592 | tf_op jit(solution)/shard_map/all_to_all | solution.py:636
  535.7 109.2 %collective-permute-start.28 = (bf16[288,1536]{1,0:T(8,128)(2,1)}, bf16[288,1536]{1,0:T(8,128)(2,1)}, u32[]{:S(2)}, u32[]{:S(2)}) collective-permute-start(bf16[288,1536]{1,0:T(8,128)(2,1)} %pad_maximum_fusion.15), channel_id=1, source_target_pairs={{0,6},{1,7},{2,0},{3,1},{4,2},{5,3},{6,4},{7,5},{8,14},{9,15},{10,... | collective-permute-start | bytes 2654216 | tf_op jit(solution)/shard_map/ppermute | solution.py:614
  549.4 31.7 %collective-permute-start.23 = (bf16[1536,256]{1,0:T(8,128)(2,1)}, bf16[1536,256]{1,0:T(8,128)(2,1)}, u32[]{:S(2)}, u32[]{:S(2)}) collective-permute-start(bf16[1536,256]{1,0:T(8,128)(2,1)} %get-tuple-element.172), channel_id=1, source_target_pairs={{0,16},{16,0},{1,17},{17,1},{2,18},{18,2},{3,19},{19,3},{4,20},{20... | collective-permute-start | bytes 2359304 | tf_op jit(solution)/shard_map/ppermute | solution.py:48
  565.5 18.7 %collective-permute-start.26 = (f32[256,1536]{1,0:T(8,128)}, f32[256,1536]{1,0:T(8,128)S(1)}, u32[]{:S(2)}, u32[]{:S(2)}) collective-permute-start(f32[256,1536]{1,0:T(8,128)} %slice.172), channel_id=1, source_target_pairs={{0,8},{8,0},{1,9},{9,1},{2,10},{10,2},{3,11},{11,3},{4,12},{12,4},... | collective-permute-start | bytes 4718600 | tf_op jit(solution)/shard_map/ppermute | solution.py:48
  566.5 11.5 %collective-permute-start.25 = (bf16[768,256]{1,0:T(8,128)(2,1)S(1)}, bf16[768,256]{1,0:T(8,128)(2,1)S(1)}, u32[]{:S(2)}, u32[]{:S(2)}) collective-permute-start(bf16[768,256]{1,0:T(8,128)(2,1)S(1)} %copy-done.88), channel_id=1, source_target_pairs={{0,1},{1,0},{2,3},{3,2},{4,5},{5,4},{6,7},{7,6},{8,9},{9,8},{10,11... | collective-permute-start | bytes 1179656 | tf_op jit(solution)/shard_map/ppermute | solution.py:48
  578.1 66.9 %collective-permute-start.29 = (bf16[288,1536]{1,0:T(8,128)(2,1)}, bf16[288,1536]{1,0:T(8,128)(2,1)}, u32[]{:S(2)}, u32[]{:S(2)}) collective-permute-start(bf16[288,1536]{1,0:T(8,128)(2,1)} %pad_maximum_fusion.16), channel_id=1, source_target_pairs={{0,4},{1,5},{2,6},{3,7},{4,0},{5,1},{6,2},{7,3},{8,12},{9,13},{10,... | collective-permute-start | bytes 2654216 | tf_op jit(solution)/shard_map/ppermute | solution.py:614
  593.7 20.8 %collective-permute-start.24 = (bf16[768,512]{1,0:T(8,128)(2,1)}, bf16[768,512]{1,0:T(8,128)(2,1)}, u32[]{:S(2)}, u32[]{:S(2)}) collective-permute-start(bf16[768,512]{1,0:T(8,128)(2,1)} %get-tuple-element.174), channel_id=1, source_target_pairs={{0,1},{1,0},{2,3},{3,2},{4,5},{5,4},{6,7},{7,6},{8,9},{9,8},{10,11... | collective-permute-start | bytes 2359304 | tf_op jit(solution)/shard_map/ppermute | solution.py:48
  595.9 182.7 %all-to-all-start.7 = ((bf16[16,48,1536]{2,1,0:T(8,128)(2,1)}), bf16[16,48,1536]{2,1,0:T(8,128)(2,1)S(1)}, u32[]{:S(2)}, u32[]{:S(2)}) async-start(bf16[16,48,1536]{2,1,0:T(8,128)(2,1)} %bitcast.195), calls=%async_computation.7 | async-start | bytes 4718592 | tf_op jit(solution)/shard_map/all_to_all | solution.py:636
  600.1 42.3 %collective-permute-start.21 = (bf16[1536,256]{1,0:T(8,128)(2,1)}, bf16[1536,256]{1,0:T(8,128)(2,1)}, u32[]{:S(2)}, u32[]{:S(2)}) collective-permute-start(bf16[1536,256]{1,0:T(8,128)(2,1)} %get-tuple-element.169), channel_id=1, source_target_pairs={{0,16},{16,0},{1,17},{17,1},{2,18},{18,2},{3,19},{19,3},{4,20},{20... | collective-permute-start | bytes 2359304 | tf_op jit(solution)/shard_map/ppermute | solution.py:48
  614.5 70.6 %collective-permute-start.33 = (bf16[288,1536]{1,0:T(8,128)(2,1)}, bf16[288,1536]{1,0:T(8,128)(2,1)}, u32[]{:S(2)}, u32[]{:S(2)}) collective-permute-start(bf16[288,1536]{1,0:T(8,128)(2,1)} %pad_maximum_fusion.17), channel_id=1, source_target_pairs={{0,5},{1,4},{2,7},{3,6},{4,1},{5,0},{6,3},{7,2},{8,13},{9,12},{10,... | collective-permute-start | bytes 2654216 | tf_op jit(solution)/shard_map/ppermute | solution.py:614
  646.2 21.7 %collective-permute-start.31 = (bf16[2,2,1,192,384]{4,3,2,1,0:T(8,128)(2,1)S(1)}, bf16[2,2,1,192,384]{4,3,2,1,0:T(8,128)(2,1)S(1)}, u32[]{:S(2)}, u32[]{:S(2)}) collective-permute-start(bf16[2,2,1,192,384]{4,3,2,1,0:T(8,128)(2,1)S(1)} %dynamic-slice_convert_fusion.2), channel_id=1, source_target_pairs={{0,16},{16,0},{1,17},{17,1},{2,18},{18,2},{3,19},{19,3},{4,20},{20... | collective-permute-start | bytes 1769480 | tf_op jit(solution)/shard_map/ppermute | solution.py:48
  646.9 37.7 %collective-permute-start.30 = (bf16[2,2,1,192,512]{4,3,2,1,0:T(8,128)(2,1)S(1)}, bf16[2,2,1,192,512]{4,3,2,1,0:T(8,128)(2,1)S(1)}, u32[]{:S(2)}, u32[]{:S(2)}) collective-permute-start(bf16[2,2,1,192,512]{4,3,2,1,0:T(8,128)(2,1)S(1)} %dynamic-slice_convert_fusion), channel_id=1, source_target_pairs={{0,1},{1,0},{2,3},{3,2},{4,5},{5,4},{6,7},{7,6},{8,9},{9,8},{10,11... | collective-permute-start | bytes 2359304 | tf_op jit(solution)/shard_map/ppermute | solution.py:48
  647.0 45.3 %collective-permute-start.32 = (bf16[256,1536]{1,0:T(8,128)(2,1)S(1)}, bf16[256,1536]{1,0:T(8,128)(2,1)S(1)}, u32[]{:S(2)}, u32[]{:S(2)}) collective-permute-start(bf16[256,1536]{1,0:T(8,128)(2,1)S(1)} %copy-done.60), channel_id=1, source_target_pairs={{0,4},{4,0},{1,5},{5,1},{2,6},{6,2},{3,7},{7,3},{8,12},{12,8},{9,1... | collective-permute-start | bytes 2359304 | tf_op jit(solution)/shard_map/ppermute | solution.py:48
  667.8 16.6 %collective-permute-start.36 = (f32[34,1536]{1,0:T(8,128)S(1)}, f32[34,1536]{1,0:T(8,128)S(1)}, u32[]{:S(2)}, u32[]{:S(2)}) collective-permute-start(f32[34,1536]{1,0:T(8,128)S(1)} %add.719), channel_id=1, source_target_pairs={{0,1},{1,0},{2,3},{3,2},{4,5},{5,4},{6,7},{7,6},{8,9},{9,8},{10,11... | collective-permute-start | bytes 626696 | tf_op jit(solution)/shard_map/ppermute | solution.py:48
  684.5 17.2 %collective-permute-start.37 = (f32[34,1536]{1,0:T(8,128)S(1)}, f32[34,1536]{1,0:T(8,128)S(1)}, u32[]{:S(2)}, u32[]{:S(2)}) collective-permute-start(f32[34,1536]{1,0:T(8,128)S(1)} %add.720), channel_id=1, source_target_pairs={{0,2},{1,3},{2,0},{3,1},{4,6},{5,7},{6,4},{7,5},{8,10},{9,11},{10,... | collective-permute-start | bytes 626696 | tf_op jit(solution)/shard_map/ppermute | solution.py:48
  692.4 57.9 %collective-permute-start.39 = (bf16[2,1,1,192,896]{4,3,2,1,0:T(8,128)(2,1)S(1)}, bf16[2,1,1,192,896]{4,3,2,1,0:T(8,128)(2,1)S(1)}, u32[]{:S(2)}, u32[]{:S(2)}) collective-permute-start(bf16[2,1,1,192,896]{4,3,2,1,0:T(8,128)(2,1)S(1)} %dynamic-slice_convert_fusion.1), channel_id=1, source_target_pairs={{0,2},{1,3},{2,0},{3,1},{4,6},{5,7},{6,4},{7,5},{8,10},{9,11},{10,... | collective-permute-start | bytes 2064392 | tf_op jit(solution)/shard_map/ppermute | solution.py:48
  692.4 70.2 %collective-permute-start.41 = (bf16[288,1536]{1,0:T(8,128)(2,1)S(1)}, bf16[288,1536]{1,0:T(8,128)(2,1)S(1)}, u32[]{:S(2)}, u32[]{:S(2)}) collective-permute-start(bf16[288,1536]{1,0:T(8,128)(2,1)S(1)} %copy-done.46), channel_id=1, source_target_pairs={{0,3},{1,2},{2,5},{3,4},{4,7},{5,6},{6,1},{7,0},{8,11},{9,10},{10,... | collective-permute-start | bytes 2654216 | tf_op jit(solution)/shard_map/ppermute | solution.py:614
  695.4 67.3 %collective-permute-start.42 = (bf16[288,1536]{1,0:T(8,128)(2,1)S(1)}, bf16[288,1536]{1,0:T(8,128)(2,1)S(1)}, u32[]{:S(2)}, u32[]{:S(2)}) collective-permute-start(bf16[288,1536]{1,0:T(8,128)(2,1)S(1)} %copy-done.47), channel_id=1, source_target_pairs={{0,7},{1,6},{2,1},{3,0},{4,3},{5,2},{6,5},{7,4},{8,15},{9,14},{10,... | collective-permute-start | bytes 2654216 | tf_op jit(solution)/shard_map/ppermute | solution.py:614
  697.5 65.2 %collective-permute-start.43 = (bf16[288,1536]{1,0:T(8,128)(2,1)S(1)}, bf16[288,1536]{1,0:T(8,128)(2,1)S(1)}, u32[]{:S(2)}, u32[]{:S(2)}) collective-permute-start(bf16[288,1536]{1,0:T(8,128)(2,1)S(1)} %copy-done.48), channel_id=1, source_target_pairs={{0,1},{1,0},{2,3},{3,2},{4,5},{5,4},{6,7},{7,6},{8,9},{9,8},{10,11... | collective-permute-start | bytes 2654216 | tf_op jit(solution)/shard_map/ppermute | solution.py:614
  701.7 47.9 %collective-permute-start.38 = (f32[34,1536]{1,0:T(8,128)S(1)}, f32[34,1536]{1,0:T(8,128)S(1)}, u32[]{:S(2)}, u32[]{:S(2)}) collective-permute-start(f32[34,1536]{1,0:T(8,128)S(1)} %add.721), channel_id=1, source_target_pairs={{0,4},{4,0},{1,5},{5,1},{2,6},{6,2},{3,7},{7,3},{8,12},{12,8},{9,1... | collective-permute-start | bytes 626696 | tf_op jit(solution)/shard_map/ppermute | solution.py:48
  750.4 12.2 %collective-permute-start.40 = (bf16[1,1,1,192,896]{4,3,2,1,0:T(8,128)(2,1)S(1)}, bf16[1,1,1,192,896]{4,3,2,1,0:T(8,128)(2,1)S(1)}, u32[]{:S(2)}, u32[]{:S(2)}) collective-permute-start(bf16[1,1,1,192,896]{4,3,2,1,0:T(8,128)(2,1)S(1)} %dynamic-slice_convert_fusion.3), channel_id=1, source_target_pairs={{0,4},{4,0},{1,5},{5,1},{2,6},{6,2},{3,7},{7,3},{8,12},{12,8},{9,1... | collective-permute-start | bytes 1032200 | tf_op jit(solution)/shard_map/ppermute | solution.py:48
  (96 other events, 595.7 us)
